TPU v7x, 256 devices: a whole 4x4x8 slice. The times are simulated.
256 devices in a mesh: ka: 16 (over z_hi, x, core), vert: 16 (over y, z_lo).
Axes of the slice: x: 4, y: 4, z: 8 (z_hi: 2, z_lo: 4; z = z_hi * 4 + z_lo), core: 2. Of those that a mesh axis runs over, the one named last changes fastest.
Arguments:
- amplitudes: bfloat16 [1, 16, 16, 16, 96, 1536], P(None, 'ka', None, None, 'vert'), may hold values from -12 to 12
- loop_integral_blocks: bfloat16 [16, 1536, 1536], P('ka', 'vert'), may hold values from -0.15625 to 0.15625
- occupied_energy: float32 [16, 16], replicated, may hold values from -2 to -0.5
- occupied_energy_j: float32 [1, 16], replicated, may hold values from -2 to -0.5
- virtual_energy: float32 [16, 96], replicated, may hold values from 0.5 to 2.5
- kpoint_b_table: int32 [1, 16, 16], replicated, may hold values from 0 to 15, as said below
Outputs:
- update: bfloat16 [1, 16, 16, 16, 96, 1536], P(None, 'ka', None, None, 'vert')
Inputs may be any that keep to these rules, and one draw needn't show every extreme that they name: For every kj and ki, kpoint_b_table[kj, ki, :] is a permutation of the 16 k-points.
All inputs are finite; a program needn't handle non-finite values.
Results may differ from a plain program's by a relative error of at most 0.0051.
Values may be sent and summed in bfloat16 or wider, within the bound.
No kernel may reach another device: no remote copies, remote signals or barrier semaphores. Data moves between devices by JAX's collectives and lax.ppermute only.
A program may use at most 128 MiB of HBM per device.

v0:
```python
import jax
import jax.numpy as jnp
from jax import lax
from jax.sharding import PartitionSpec as P

OCC_ORBITALS = 16
VIRT_ORBITALS = 96


def combine_pairs(blocks):
    shape = blocks.shape
    split = blocks.astype(jnp.float32).reshape(shape[:5] + (OCC_ORBITALS, VIRT_ORBITALS))
    swapped = jnp.swapaxes(split, 3, 5)
    return (2.0 * split - swapped).astype(jnp.bfloat16).reshape(shape)


def energy_gaps_all(
    occupied_energy,
    occupied_energy_j,
    virtual_energy,
    kpoint_b_table,
    kpoint_index,
    virtual_index,
    virtual_slice,
):
    kpoint_b_column = lax.dynamic_index_in_dim(kpoint_b_table, kpoint_index, axis=2, keepdims=False)
    onehot = (
        kpoint_b_column[..., None] == jnp.arange(virtual_energy.shape[0], dtype=jnp.int32)
    ).astype(jnp.float32)
    virtual_b = jnp.einsum("xyn,nv->xyv", onehot, virtual_energy, precision=lax.Precision.HIGHEST)
    virtual_a = lax.dynamic_slice(
        virtual_energy, (kpoint_index, virtual_index * virtual_slice), (1, virtual_slice)
    )[0]
    return (
        occupied_energy[None, :, :, None, None, None]
        + occupied_energy_j[:, None, None, None, :, None]
        - virtual_a[None, None, None, :, None, None]
        - virtual_b[:, :, None, None, None, :]
    )


def per_device(
    amplitudes,
    loop_integral_blocks,
    occupied_energy,
    occupied_energy_j,
    virtual_energy,
    kpoint_b_table,
):
    kpoint_index = lax.axis_index("ka")
    virtual_index = lax.axis_index("vert")
    virtual_slice = amplitudes.shape[4]
    pairs = amplitudes.shape[5]
    joined_terms = combine_pairs(amplitudes)
    regrouped = lax.all_to_all(joined_terms, "ka", split_axis=2, concat_axis=1, tiled=True)
    matrix = regrouped.reshape(-1, pairs)
    cycle = jnp.dot(
        matrix,
        lax.all_gather(loop_integral_blocks, "vert", axis=1, tiled=True)[0],
        preferred_element_type=jnp.float32,
    )
    cycle = cycle.reshape(regrouped.shape)
    energy_gap = energy_gaps_all(
        occupied_energy,
        occupied_energy_j,
        virtual_energy,
        kpoint_b_table,
        kpoint_index,
        virtual_index,
        virtual_slice,
    )
    scaled = cycle.reshape(energy_gap.shape) / energy_gap
    scaled = scaled.astype(jnp.bfloat16).reshape(cycle.shape)
    return lax.all_to_all(scaled, "ka", split_axis=1, concat_axis=2, tiled=True)


def solution(mesh):
    in_specs = (P(None, "ka", None, None, "vert", None), P("ka", "vert", None), P(), P(), P(), P())
    out_specs = P(None, "ka", None, None, "vert", None)
    return jax.shard_map(
        per_device, mesh=mesh, in_specs=in_specs, out_specs=out_specs, check_vma=False
    )
```

profile of v0, /device:TPU:33, one launch (start us, length us, event | category | flops | bytes accessed | tf_op | source)
XLA Modules:
  0.0 388.3 jit_solution(1064120864483103987)
XLA Ops:
  6.5 0.0 copy-start
  6.5 0.0 all-gather.2.cloned.1.call-start
  6.5 0.7 all-gather.2.cloned.1.call-update
  7.3 11.2 %reshape.84 = f32[1,1,16,16,6,16,96]{6,5,3,4,2,1,0:T(8,128)} reshape(bf16[1,1,16,16,6,1536]{5,3,4,2,1,0:T(8,128)(2,1)} %param.6) | data formatting | bytes 14155776 | tf_op jit(solution)/shard_map/reshape | solution.py:12
  18.5 14.6 %fusion = bf16[1,1,16,16,6,16,96]{6,5,3,4,2,1,0:T(8,128)(2,1)} fusion(f32[1,1,16,16,6,16,96]{6,5,3,4,2,1,0:T(8,128)} %reshape.84), kind=kLoop, calls=%fused_computation.1 | loop fusion | flops 7077888 | bytes 14155776 | tf_op jit(solution)/shard_map/convert_element_type | solution.py:14
  33.0 11.2 %reshape.81 = bf16[1,1,16,16,6,1536]{5,3,4,1,0,2:T(8,128)(2,1)} reshape(bf16[1,1,16,16,6,16,96]{6,5,3,4,2,1,0:T(8,128)(2,1)} %fusion) | data formatting | bytes 9437184 | tf_op jit(solution)/shard_map/reshape | solution.py:14
  44.2 0.0 copy-start.3
  44.2 0.0 copy-start.2
  44.2 0.0 copy-start.4
  44.2 10.9 %all-to-all-start = ((bf16[1,1,16,16,6,1536]{5,3,4,1,0,2:T(8,128)(2,1)}), bf16[1,1,16,16,6,1536]{5,3,4,1,0,2:T(8,128)(2,1)}, u32[]{:S(2)}, u32[]{:S(2)}) async-start(bf16[1,1,16,16,6,1536]{5,3,4,1,0,2:T(8,128)(2,1)} %reshape.81), calls=%async_computation | async-start | bytes 9437184 | tf_op jit(solution)/shard_map/all_to_all | solution.py:55
  55.1 0.0 copy-done.3
  55.1 0.2 dynamic-slice_reduce_fusion
  55.3 0.0 copy-done
  55.3 0.1 dynamic-slice_bitcast_fusion
  55.4 0.2 fusion.2
  55.6 0.0 copy-done.2
  55.6 0.0 copy-done.4
  55.6 0.1 broadcast_add_fusion
  55.7 0.1 broadcast_subtract_fusion
  55.8 143.4 %all-gather.2.cloned.1.call-done = bf16[1,1536,1536]{2,1,0:T(8,128)(2,1)} async-done(((bf16[1,96,1536]{2,1,0:T(8,128)(2,1)}), bf16[1,1536,1536]{2,1,0:T(8,128)(2,1)}) %all-gather.2.cloned.1.call-update) | async-done | bytes 4718608 | tf_op jit(solution)/shard_map/all_gather | solution.py:59
  199.3 6.6 %copy.13 = bf16[1536,1536]{1,0:T(8,128)(2,1)} copy(bf16[1536,1536]{0,1:T(8,128)(2,1)} %bitcast.40) | data formatting | bytes 9437184 | tf_op jit(solution)/shard_map/dot_general | solution.py:57
  205.9 20.6 %all-to-all-done = bf16[1,1,16,16,6,1536]{5,3,4,1,0,2:T(8,128)(2,1)} async-done(((bf16[1,1,16,16,6,1536]{5,3,4,1,0,2:T(8,128)(2,1)}), bf16[1,1,16,16,6,1536]{5,3,4,1,0,2:T(8,128)(2,1)}, u32[]{:S(2)}, u32[]{:S(2)}) %all-to-all-start) | async-done | bytes 4718624 | tf_op jit(solution)/shard_map/all_to_all | solution.py:55
  226.5 13.2 %divide_convert_fusion = bf16[16,16,6,16,96]{4,1,3,2,0:T(8,128)(2,1)S(1)} fusion(f32[16,96]{1,0:T(8,128)S(1)} %fusion.2, f32[16,16,6,16]{1,3,2,0:T(8,128)S(1)} %broadcast_subtract_fusion, bf16[16,96,1536,1,1]{2,1,0,4,3:T(8,128)(2,1)} %bitcast.41, bf16[1,1,16,16,6,1536]{5,3,4,1,0,2:T(8,128)(2,1)} %all-to-all-done), kind=kOutput, calls=%fused_computation.2 | convolution fusion | flops 7254835200 | bytes 14260224 | tf_op jit(solution)/shard_map/dot_general | solution.py:57
  239.7 5.3 %copy.14 = bf16[16,16,6,16,96]{4,3,1,2,0:T(8,128)(2,1)} copy(bf16[16,16,6,16,96]{4,1,3,2,0:T(8,128)(2,1)S(1)} %divide_convert_fusion) | data formatting | bytes 9437184 | tf_op jit(solution)/shard_map/convert_element_type | solution.py:73
  244.9 11.2 %reshape.82 = bf16[1,16,1,16,6,1536]{5,3,4,1,2,0:T(8,128)(2,1)} reshape(bf16[16,16,6,16,96]{4,3,1,2,0:T(8,128)(2,1)} %copy.14) | data formatting | bytes 9437184 | tf_op jit(solution)/shard_map/reshape | solution.py:73
  256.1 0.0 copy-start.1
  256.2 123.1 %all_to_all.21 = bf16[1,16,1,16,6,1536]{5,3,4,2,0,1:T(8,128)(2,1)S(1)} all-to-all(bf16[1,16,1,16,6,1536]{5,3,4,2,0,1:T(8,128)(2,1)} %bitcast.39), channel_id=1, replica_groups=mesh['ka'=16,'vert'=16] {'ka'}, dimensions={1} | all-to-all | bytes 9437184 | tf_op jit(solution)/shard_map/all_to_all | solution.py:74
  379.3 2.2 copy.20
  381.5 0.0 copy-done.1
Async XLA Ops:
  6.5 48.8 %copy-start = (f32[16,96]{1,0:T(8,128)S(1)}, f32[16,96]{1,0:T(8,128)}, u32[]{:S(2)}) copy-start(f32[16,96]{1,0:T(8,128)} %param.10) | copy-start | bytes 18436
  6.5 192.7 %all-gather.2.cloned.1.call-start = ((), (), s32[]{:S(2)}) async-start(), calls=%async_computation.2 | async-start | bytes 5013504 | tf_op jit(solution)/shard_map/all_gather | solution.py:59
  44.2 10.9 %copy-start.3 = (s32[1,16,16]{2,1,0:T(8,128)S(1)}, s32[1,16,16]{2,1,0:T(8,128)}, u32[]{:S(2)}) copy-start(s32[1,16,16]{2,1,0:T(8,128)} %param.11) | copy-start | bytes 3076
  44.2 11.4 %copy-start.2 = (f32[16,16]{1,0:T(8,128)S(1)}, f32[16,16]{1,0:T(8,128)}, u32[]{:S(2)}) copy-start(f32[16,16]{1,0:T(8,128)} %param.8) | copy-start | bytes 3076
  44.2 11.4 %copy-start.4 = (f32[1,16]{1,0:T(1,128)S(1)}, f32[1,16]{1,0:T(1,128)}, u32[]{:S(2)}) copy-start(f32[1,16]{1,0:T(1,128)} %param.9) | copy-start | bytes 196
  44.2 182.2 %all-to-all-start = ((bf16[1,1,16,16,6,1536]{5,3,4,1,0,2:T(8,128)(2,1)}), bf16[1,1,16,16,6,1536]{5,3,4,1,0,2:T(8,128)(2,1)}, u32[]{:S(2)}, u32[]{:S(2)}) async-start(bf16[1,1,16,16,6,1536]{5,3,4,1,0,2:T(8,128)(2,1)} %reshape.81), calls=%async_computation | async-start | bytes 9437184 | tf_op jit(solution)/shard_map/all_to_all | solution.py:55
  256.1 125.3 %copy-start.1 = (f32[16,96]{1,0:T(8,128)S(1)}, f32[16,96]{1,0:T(8,128)}, u32[]{:S(2)}) copy-start(f32[16,96]{1,0:T(8,128)} %param.10) | copy-start | bytes 18436
Sparse Core Ops, SparseCore 0:
  9.1 190.0 all-gather.1
where the time goes:
time: 390 us; the launch traced here: 388 us
  waiting for transfers between devices  165 us (42%)
  blocking collectives  123 us (32%)
  local copies, waits for them, and re-layouts  47.9 us (12%)
  other arithmetic  14.8 us (4%)
  matrix products  13.4 us (3%)
  between operations  13.4 us (3%)
  starting transfers between devices  10.9 us (3%)
    all_gather x1, waiting for transfers between devices, per_device(): lax.all_gather(loop_integral_blocks, 'vert', axis=1, tiled=True)[0]  143 us
    all_to_all x1, blocking collectives, per_device(): return lax.all_to_all(scaled, 'ka', split_axis=1, concat_axis=2, tiled=True)  123 us
    all_to_all x1, waiting for transfers between devices, per_device(): lax.all_to_all(joined_terms, 'ka', split_axis=2, concat_axis=1, tiled=True)  20.6 us
    convert_element_type x1, other arithmetic, combine_pairs(): return (2.0 * split - swapped).astype(jnp.bfloat16).reshape(shape)  14.6 us
    dot_general x1, matrix products, per_device(): jnp.dot(matrix, lax.all_gather(loop_integral_blocks, 'vert', axis=1, tile...  13.2 us
    reshape x1, local copies, waits for them, and re-layouts, combine_pairs(): return (2.0 * split - swapped).astype(jnp.bfloat16).reshape(shape)  11.2 us
    reshape x1, local copies, waits for them, and re-layouts, per_device(): scaled = scaled.astype(jnp.bfloat16).reshape(cycle.shape)  11.2 us
    reshape x1, local copies, waits for them, and re-layouts, combine_pairs(): blocks.astype(jnp.float32)  11.2 us
  transfers between devices with their start and end apart: 2, of which 2 were waited for; matrix products, arithmetic and copies ran while one was open for 11% of the time, Pallas kernels for 0%

commit v1 on v0

v1 whole, which is shorter than its diff:
```python
import jax
import jax.numpy as jnp
from jax import lax
from jax.experimental import pallas as pl
from jax.experimental.pallas import tpu as pltpu
from jax.sharding import Mesh, PartitionSpec as P

NO = 16
NV = 96
PAIRS = NO * NV
VS = 6
ROWS = VS * NO
HALF = NV // 2
VMEM = 48 << 20
RING = ("zh", "zl")


def combine_kernel(x_ref, o_ref, scr):
    sq = NO * NO
    for a in range(VS):
        xa = x_ref[0, NO * a : NO * a + NO, :].astype(jnp.float32)
        for p in range(NO):
            scr[a * sq + NO * p : a * sq + NO * p + NO, 0:NV] = xa[:, NV * p : NV * p + NV]
    for a in range(VS):
        xa = x_ref[0, NO * a : NO * a + NO, :].astype(jnp.float32)
        swapped = jnp.concatenate(
            [scr[pl.ds(a * sq + q, NO, stride=NO), :][:, :NV] for q in range(NO)], axis=1
        )
        o_ref[0, NO * a : NO * a + NO, :] = (2.0 * xa - swapped).astype(jnp.bfloat16)


def combine(x):
    nb = x.shape[0]
    spec = pl.BlockSpec((1, ROWS, PAIRS), lambda b: (b, 0, 0))
    return pl.pallas_call(
        combine_kernel,
        grid=(nb,),
        in_specs=[spec],
        out_specs=spec,
        out_shape=jax.ShapeDtypeStruct(x.shape, x.dtype),
        scratch_shapes=[pltpu.VMEM((VS * NO * NO, 128), jnp.float32)],
        compiler_params=pltpu.CompilerParams(vmem_limit_bytes=VMEM),
        cost_estimate=pl.CostEstimate(
            flops=nb * 300000000, bytes_accessed=4 * x.size, transcendentals=0
        ),
        name="combine",
    )(x)


NT = 256


def contract(cs, w, rr, cc):
    nc = len(cs)

    def kernel(*refs):
        x_refs, (w_ref, r_ref, c_ref), o_refs = refs[:nc], refs[nc : nc + 3], refs[nc + 3 :]
        x = jnp.concatenate([ref[0] for ref in x_refs], axis=0) if nc > 1 else x_refs[0][0]
        acc = jnp.dot(x, w_ref[0], preferred_element_type=jnp.float32)
        for m in range(nc):
            gap = r_ref[0, m] + c_ref[0, m]
            o_refs[m][0] = (acc[ROWS * m : ROWS * m + ROWS] / gap).astype(jnp.bfloat16)

    row = pl.BlockSpec((1, ROWS, PAIRS), lambda z, n: (z, 0, 0))
    return pl.pallas_call(
        kernel,
        grid=(2, PAIRS // NT),
        in_specs=[row] * nc
        + [
            pl.BlockSpec((1, PAIRS, NT), lambda z, n: (z, 0, n)),
            pl.BlockSpec((1, nc, ROWS, 1), lambda z, n: (z, 0, 0, 0)),
            pl.BlockSpec((1, nc, 1, NT), lambda z, n: (z, 0, 0, n)),
        ],
        out_specs=[pl.BlockSpec((1, ROWS, NT), lambda z, n: (z, 0, n))] * nc,
        out_shape=[jax.ShapeDtypeStruct((2, ROWS, PAIRS), jnp.bfloat16)] * nc,
        compiler_params=pltpu.CompilerParams(vmem_limit_bytes=VMEM),
        cost_estimate=pl.CostEstimate(
            flops=2 * 2 * nc * ROWS * PAIRS * PAIRS, bytes_accessed=4 * PAIRS * PAIRS, transcendentals=0
        ),
        name="contract",
    )(*cs, w, rr, cc)


def assemble(ring, gathered, pos):
    n = len(ring)

    def kernel(pos_ref, *refs):
        pieces, g_ref, o_ref, sem = refs[:n], refs[n], refs[n + 1], refs[n + 2]
        y, z = pos_ref[0], pos_ref[1]
        copies = []
        for s in range(n):
            src = lax.rem(z + s, n)
            for d in range(4):
                copies.append(
                    pltpu.make_async_copy(
                        pieces[s].at[d],
                        o_ref.at[lax.div(src, 4), lax.rem(y + d, 4), lax.rem(src, 4), 0],
                        sem.at[len(copies)],
                    )
                )
        for zh in range(2):
            for yy in range(4):
                for zl in range(4):
                    copies.append(
                        pltpu.make_async_copy(
                            g_ref.at[zh, zl, yy], o_ref.at[zh, yy, zl, 1], sem.at[len(copies)]
                        )
                    )
        for c in copies:
            c.start()
        for c in copies:
            c.wait()

    anyspec = pl.BlockSpec(memory_space=pl.ANY)
    return pl.pallas_call(
        kernel,
        in_specs=[pl.BlockSpec(memory_space=pltpu.SMEM)] + [anyspec] * (n + 1),
        out_specs=anyspec,
        out_shape=jax.ShapeDtypeStruct((2, 4, 4, 2, HALF, PAIRS), jnp.bfloat16),
        scratch_shapes=[pltpu.SemaphoreType.DMA((64,))],
        compiler_params=pltpu.CompilerParams(vmem_limit_bytes=4 << 20),
        cost_estimate=pl.CostEstimate(flops=0, bytes_accessed=8 * PAIRS * PAIRS, transcendentals=0),
        name="assemble",
    )(pos, *ring, gathered)


def xc_permute(v, dx, dc):
    if dx == 0:
        return lax.ppermute(v, "c", [(0, 1), (1, 0)])
    pairs = [
        (x * 2 + c, ((x + dx) % 4) * 2 + (c ^ dc)) for x in range(4) for c in range(2)
    ]
    return lax.ppermute(v, ("x", "c"), pairs)


def y_permute(v, s):
    return lax.ppermute(v, "y", [(i, (i + s) % 4) for i in range(4)])


def z_permute(v, s):
    return lax.ppermute(v, RING, [(i, (i + s) % 8) for i in range(8)])


CHUNKS = [(2, 0), (2, 1), (1, 0), (1, 1), (3, 0), (3, 1), (0, 1), (0, 0)]
GROUPS = [(0, 2), (2, 6), (6, 8)]


def per_device(amps, wshard, occ, occj, virt, table):
    zh, x, c = lax.axis_index("zh"), lax.axis_index("x"), lax.axis_index("c")
    y, zl = lax.axis_index("y"), lax.axis_index("zl")
    blocks = jnp.transpose(amps[0, 0], (0, 2, 1, 3)).reshape(2, 4, 2, ROWS, PAIRS)

    def block(dx, dc):
        return lax.dynamic_slice(
            blocks, (0, lax.rem(x + dx, 4), c ^ dc, 0, 0), (2, 1, 1, ROWS, PAIRS)
        ).reshape(2, ROWS, PAIRS)

    sent = [block(dx, dc) for dx, dc in CHUNKS]
    got = [
        v if (dx, dc) == (0, 0) else xc_permute(v, dx, dc) for v, (dx, dc) in zip(sent, CHUNKS)
    ]

    w = wshard[0]
    gathered = lax.all_gather(w[HALF:], ("zh", "zl", "y"), axis=0).reshape(2, 4, 4, HALF, PAIRS)
    own = w[:HALF]
    col = jnp.stack([own, y_permute(own, -1), y_permute(own, 2), y_permute(own, 1)])
    up, down = [col], [col]
    for s in range(3):
        up.append(z_permute(up[-1], 1))
        down.append(z_permute(down[-1], -1))
    far = jnp.concatenate([z_permute(up[3][:2], 1), z_permute(down[3][2:], -1)])
    ring = [col, down[1], down[2], down[3], far, up[3], up[2], up[1]]
    pos = jnp.stack([y, zh * 4 + zl]).astype(jnp.int32)
    wall = assemble(ring, gathered, pos).reshape(2, PAIRS, PAIRS)

    ki = jnp.stack([(zh * 4 + lax.rem(x + 4 - dx, 4)) * 2 + (c ^ dc) for dx, dc in CHUNKS])
    ka = jnp.stack([(z * 4 + x) * 2 + c for z in range(2)])
    va = lax.dynamic_slice(virt, (0, (y * 4 + zl) * VS), (NO, VS))[ka]
    rr = occ[ki][None, :, None, :] - va[:, None, :, None]
    rr = rr.reshape(2, len(CHUNKS), ROWS, 1)
    kb = table[0][ki][:, ka].T
    cc = occj[0][None, None, :, None] - virt[kb][:, :, None, :]
    cc = cc.reshape(2, len(CHUNKS), 1, PAIRS)

    out = jnp.zeros((2, 4, 2, ROWS, PAIRS), jnp.bfloat16)
    comb = [combine(v) for v in got]
    for lo, hi in GROUPS:
        res = contract(comb[lo:hi], wall, rr[:, lo:hi], cc[:, lo:hi])
        for v, (dx, dc) in zip(res, CHUNKS[lo:hi]):
            if (dx, dc) != (0, 0):
                v = xc_permute(v, (4 - dx) % 4, dc)
            out = lax.dynamic_update_slice(
                out, v.reshape(2, 1, 1, ROWS, PAIRS), (0, lax.rem(x + dx, 4), c ^ dc, 0, 0)
            )
    out = out.reshape(NO, VS, NO, PAIRS)
    return jnp.transpose(out, (0, 2, 1, 3))[None, None]


def solution(mesh):
    fine = Mesh(mesh.devices.reshape(2, 4, 2, 4, 4), ("zh", "x", "c", "y", "zl"))
    ka, vert = ("zh", "x", "c"), ("y", "zl")
    in_specs = (P(None, ka, None, None, vert, None), P(ka, vert, None), P(), P(), P(), P())
    out_specs = P(None, ka, None, None, vert, None)
    return jax.shard_map(
        per_device, mesh=fine, in_specs=in_specs, out_specs=out_specs, check_vma=False
    )
```

time: 390 us -> 221 us (0.57)
  the two profiles are of different devices: /device:TPU:33 before, /device:TPU:1 now
where the time goes in v1:
time: 221 us; the launch traced here: 220 us
  waiting for transfers between devices  63.9 us (29%)
  starting transfers between devices  56.7 us (26%)
  Pallas kernels  56.4 us (26%)
  local copies, waits for them, and re-layouts  27.7 us (13%)
  between operations  13.9 us (6%)
    ppermute x12, starting transfers between devices, xc_permute(): return lax.ppermute(v, ('x', 'c'), pairs)  32.2 us
    ppermute x8, waiting for transfers between devices, z_permute(): return lax.ppermute(v, RING, [(i, (i + s) % 8) for i in range(8)])  31.3 us
    pallas_call x3, Pallas kernels, contract(): pl.pallas_call(kernel, grid=(2, PAIRS // NT), in_specs=[row] * nc + [pl.B...  30 us
    ppermute x12, waiting for transfers between devices, xc_permute(): return lax.ppermute(v, ('x', 'c'), pairs)  27.2 us
    ppermute x8, starting transfers between devices, z_permute(): return lax.ppermute(v, RING, [(i, (i + s) % 8) for i in range(8)])  16.5 us
    pallas_call x1, Pallas kernels, assemble(): pl.pallas_call(kernel, in_specs=[pl.BlockSpec(memory_space=pltpu.SMEM)] +...  13.9 us
    unnamed x46, local copies, waits for them, and re-layouts  13.6 us
    pallas_call x8, Pallas kernels, combine(): pl.pallas_call(combine_kernel, grid=(nb,), in_specs=[spec], out_specs=spe...  12.5 us
  transfers between devices with their start and end apart: 26, of which 12 were waited for; matrix products, arithmetic and copies ran while one was open for 6% of the time, Pallas kernels for 26%

profile of v1, /device:TPU:1, one launch (start us, length us, event | category | flops | bytes accessed | tf_op | source)
XLA Modules:
  0.0 220.0 jit_solution(10873682643286284638)
XLA Ops:
  6.5 1.7 fusion.3
  8.2 2.2 %collective-permute-start.4 = (bf16[48,1536]{1,0:T(8,128)(2,1)S(1)}, bf16[48,1536]{1,0:T(8,128)(2,1)S(1)}, u32[]{:S(2)}, u32[]{:S(2)}) collective-permute-start(bf16[48,1536]{1,0:T(8,128)(2,1)S(1)} %get-tuple-element.32), channel_id=1, source_target_pairs={{0,4},{4,8},{8,12},{12,0},{1,5},{5,9},{9,13},{13,1},{2,6},{6,10},{... | collective-permute-start | bytes 442376 | tf_op jit(solution)/shard_map/ppermute | solution.py:137
  10.4 2.6 %collective-permute-start.3 = (bf16[48,1536]{1,0:T(8,128)(2,1)S(1)}, bf16[48,1536]{1,0:T(8,128)(2,1)S(1)}, u32[]{:S(2)}, u32[]{:S(2)}) collective-permute-start(bf16[48,1536]{1,0:T(8,128)(2,1)S(1)} %get-tuple-element.32), channel_id=1, source_target_pairs={{0,8},{4,12},{8,0},{12,4},{1,9},{5,13},{9,1},{13,5},{2,10},{6,14},... | collective-permute-start | bytes 442376 | tf_op jit(solution)/shard_map/ppermute | solution.py:137
  13.1 1.1 collective-permute-start.2
  14.4 5.1 %collective-permute-done.3 = bf16[48,1536]{1,0:T(8,128)(2,1)S(1)} collective-permute-done((bf16[48,1536]{1,0:T(8,128)(2,1)S(1)}, bf16[48,1536]{1,0:T(8,128)(2,1)S(1)}, u32[]{:S(2)}, u32[]{:S(2)}) %collective-permute-start.3) | collective-permute-done | bytes 147488 | tf_op jit(solution)/shard_map/ppermute | solution.py:137
  19.6 1.7 collective-permute-start.8
  21.3 4.6 %dynamic-slice_bitcast_fusion = (bf16[2,96,1536]{2,1,0:T(8,128)(2,1)}, bf16[2,96,1536]{2,1,0:T(8,128)(2,1)}, bf16[2,96,1536]{2,1,0:T(8,128)(2,1)}, bf16[2,96,153...) fusion(bf16[2,4,2,96,1536]{4,3,2,1,0:T(8,128)(2,1)} %bitcast.92, ...), kind=kLoop, calls=%fused_computation.15 | loop fusion | bytes 9437208 | tf_op jit(solution)/shard_map/reshape | solution.py:156
  25.9 1.8 collective-permute-start.23
  27.7 2.4 %collective-permute-start.18 = (bf16[2,96,1536]{2,1,0:T(8,128)(2,1)}, bf16[2,96,1536]{2,1,0:T(8,128)(2,1)}, u32[]{:S(2)}, u32[]{:S(2)}) collective-permute-start(bf16[2,96,1536]{2,1,0:T(8,128)(2,1)} %get-tuple-element.23), channel_id=1, source_target_pairs={{0,112},{16,96},{32,16},{48,0},{64,48},{80,32},{96,80},{112,64},{1... | collective-permute-start | bytes 1769480 | tf_op jit(solution)/shard_map/ppermute | solution.py:133
  30.2 0.5 collective-permute-start.17
  30.8 3.7 %collective-permute-start.5 = (bf16[4,48,1536]{2,1,0:T(8,128)(2,1)S(1)}, bf16[4,48,1536]{2,1,0:T(8,128)(2,1)S(1)}, u32[]{:S(2)}, u32[]{:S(2)}) collective-permute-start(bf16[4,48,1536]{2,1,0:T(8,128)(2,1)S(1)} %pad_maximum_fusion.refs_0_), channel_id=1, source_target_pairs={{0,131},{1,0},{2,1},{3,2},{128,3},{129,128},{130,129},{131,130},{4... | collective-permute-start | bytes 1769480 | tf_op jit(solution)/shard_map/ppermute | solution.py:141
  34.6 4.7 %collective-permute-done.8.refs_7_ = bf16[4,48,1536]{2,1,0:T(8,128)(2,1)S(1)} collective-permute-done((bf16[4,48,1536]{2,1,0:T(8,128)(2,1)S(1)}, bf16[4,48,1536]{2,1,0:T(8,128)(2,1)S(1)}, u32[]{:S(2)}, u32[]{:S(2)}) %collective-permute-start.8) | collective-permute-done | bytes 589856 | tf_op jit(solution)/shard_map/ppermute | solution.py:141
  39.3 0.6 gather_fusion.2
  40.0 0.6 gather_fusion.3
  40.7 9.4 %collective-permute-done.5.refs_1_ = bf16[4,48,1536]{2,1,0:T(8,128)(2,1)S(1)} collective-permute-done((bf16[4,48,1536]{2,1,0:T(8,128)(2,1)S(1)}, bf16[4,48,1536]{2,1,0:T(8,128)(2,1)S(1)}, u32[]{:S(2)}, u32[]{:S(2)}) %collective-permute-start.5) | collective-permute-done | bytes 589856 | tf_op jit(solution)/shard_map/ppermute | solution.py:141
  50.1 3.6 %collective-permute-start.6 = (bf16[4,48,1536]{2,1,0:T(8,128)(2,1)S(1)}, bf16[4,48,1536]{2,1,0:T(8,128)(2,1)}, u32[]{:S(2)}, u32[]{:S(2)}) collective-permute-start(bf16[4,48,1536]{2,1,0:T(8,128)(2,1)S(1)} %collective-permute-done.5.refs_1_), channel_id=1, source_target_pairs={{0,131},{1,0},{2,1},{3,2},{128,3},{129,128},{130,129},{131,130},{4... | collective-permute-start | bytes 1769480 | tf_op jit(solution)/shard_map/ppermute | solution.py:141
  53.8 0.6 gather_fusion.4
  54.6 1.6 collective-permute-done.9.refs_6_
  56.3 0.6 gather_fusion
  56.9 0.6 gather_fusion.1
  57.7 7.1 %collective-permute-done.6.refs_2_ = bf16[4,48,1536]{2,1,0:T(8,128)(2,1)} collective-permute-done((bf16[4,48,1536]{2,1,0:T(8,128)(2,1)S(1)}, bf16[4,48,1536]{2,1,0:T(8,128)(2,1)}, u32[]{:S(2)}, u32[]{:S(2)}) %collective-permute-start.6) | collective-permute-done | bytes 589856 | tf_op jit(solution)/shard_map/ppermute | solution.py:141
  64.9 3.5 %collective-permute-start.7 = (bf16[4,48,1536]{2,1,0:T(8,128)(2,1)}, bf16[4,48,1536]{2,1,0:T(8,128)(2,1)S(1)}, u32[]{:S(2)}, u32[]{:S(2)}) collective-permute-start(bf16[4,48,1536]{2,1,0:T(8,128)(2,1)} %collective-permute-done.6.refs_2_), channel_id=1, source_target_pairs={{0,131},{1,0},{2,1},{3,2},{128,3},{129,128},{130,129},{131,130},{4... | collective-permute-start | bytes 1769480 | tf_op jit(solution)/shard_map/ppermute | solution.py:141
  68.4 2.0 collective-permute-done.10.refs_5_
  70.4 12.2 %collective-permute-start.1 = (bf16[2,96,1536]{2,1,0:T(8,128)(2,1)}, bf16[2,96,1536]{2,1,0:T(8,128)(2,1)}, u32[]{:S(2)}, u32[]{:S(2)}) collective-permute-start(bf16[2,96,1536]{2,1,0:T(8,128)(2,1)} %get-tuple-element.27), channel_id=1, source_target_pairs={{0,80},{16,64},{32,112},{48,96},{64,16},{80,0},{96,48},{112,32},{1... | collective-permute-start | bytes 1769480 | tf_op jit(solution)/shard_map/ppermute | solution.py:133
  82.6 1.1 broadcast_subtract_fusion
  83.7 6.4 %collective-permute-done.7.refs_3_ = bf16[4,48,1536]{2,1,0:T(8,128)(2,1)S(1)} collective-permute-done((bf16[4,48,1536]{2,1,0:T(8,128)(2,1)}, bf16[4,48,1536]{2,1,0:T(8,128)(2,1)S(1)}, u32[]{:S(2)}, u32[]{:S(2)}) %collective-permute-start.7) | collective-permute-done | bytes 589856 | tf_op jit(solution)/shard_map/ppermute | solution.py:141
  90.1 1.9 collective-permute-start
  92.1 1.0 fusion.2
  93.2 4.0 %collective-permute-start.11 = (bf16[2,48,1536]{2,1,0:T(8,128)(2,1)S(1)}, bf16[2,48,1536]{2,1,0:T(8,128)(2,1)S(1)}, u32[]{:S(2)}, u32[]{:S(2)}) collective-permute-start(bf16[2,48,1536]{2,1,0:T(8,128)(2,1)S(1)} %slice.55), channel_id=1, source_target_pairs={{0,1},{1,2},{2,3},{3,128},{128,129},{129,130},{130,131},{131,0},{4... | collective-permute-start | bytes 884744 | tf_op jit(solution)/shard_map/ppermute | solution.py:141
  97.2 1.1 copy-done.13
  98.3 0.8 combine.15.refs_1_
  99.1 0.8 copy-done.5
  99.9 1.8 slice.59.refs_5_
  101.7 1.8 combine.14.refs_0_
  103.5 0.8 copy-done.7
  104.3 5.8 %collective-permute-start.16 = (bf16[2,96,1536]{2,1,0:T(8,128)(2,1)}, bf16[2,96,1536]{2,1,0:T(8,128)(2,1)}, u32[]{:S(2)}, u32[]{:S(2)}) collective-permute-start(bf16[2,96,1536]{2,1,0:T(8,128)(2,1)} %get-tuple-element.25), channel_id=1, source_target_pairs={{0,48},{16,32},{32,80},{48,64},{64,112},{80,96},{96,16},{112,0},{1... | collective-permute-start | bytes 1769480 | tf_op jit(solution)/shard_map/ppermute | solution.py:133
  110.0 1.8 combine.13.refs_3_
  111.9 0.8 copy-done.15
  112.7 3.5 %collective-permute-start.15 = (bf16[2,96,1536]{2,1,0:T(8,128)(2,1)}, bf16[2,96,1536]{2,1,0:T(8,128)(2,1)}, u32[]{:S(2)}, u32[]{:S(2)}) collective-permute-start(bf16[2,96,1536]{2,1,0:T(8,128)(2,1)} %get-tuple-element.26), channel_id=1, source_target_pairs={{0,32},{16,48},{32,64},{48,80},{64,96},{80,112},{96,0},{112,16},{1... | collective-permute-start | bytes 1769480 | tf_op jit(solution)/shard_map/ppermute | solution.py:133
  116.1 1.8 combine.12.refs_2_
  117.9 2.0 combine.9.refs_1_
  120.0 0.8 combine.8.refs_0_
  120.8 0.8 copy-done.11
  121.8 2.3 %copy-done.2 = bf16[32,48,1536]{2,1,0:T(8,128)(2,1)S(1)} copy-done((bf16[32,48,1536]{2,1,0:T(8,128)(2,1)S(1)}, bf16[32,48,1536]{2,1,0:T(8,128)(2,1)}, u32[]{:S(2)}) %copy-start.2) | copy-done | bytes 4718616
  124.1 1.1 copy-done.4
  125.1 13.9 %assemble.1 = bf16[2,4,4,2,48,1536]{5,4,3,2,1,0:T(8,128)(2,1)S(1)} custom-call(s32[2]{0:T(128)S(1)} %pad_add_fusion.pos_ref, bf16[4,48,1536]{2,1,0:T(8,128)(2,1)S(1)} %pad_maximum_fusion.refs_0_, bf16[4,48,1536]{2,1,0:T(8,128)(2,1)S(1)} %copy-done.4, bf16[4,48,1536]{2,1,0:T(8,128)(2,1)} %collective-permute-done.6.refs_2_, ...), custom_call_target="tpu_custom_call" | custom-call | bytes 18874368 | tf_op jit(solution)/shard_map/assemble/pallas_call | solution.py:115
  139.0 3.6 %copy-done.1 = bf16[2,4,4,2,48,1536]{5,4,3,2,1,0:T(8,128)(2,1)} copy-done((bf16[2,4,4,2,48,1536]{5,4,3,2,1,0:T(8,128)(2,1)}, bf16[2,4,4,2,48,1536]{5,4,3,2,1,0:T(8,128)(2,1)S(1)}, u32[]{:S(2)}) %copy-start.1) | copy-done | bytes 9437208
  142.7 9.6 %contract.3 = (bf16[2,96,1536]{2,1,0:T(8,128)(2,1)S(1)}, bf16[2,96,1536]{2,1,0:T(8,128)(2,1)S(1)}) custom-call(bf16[2,96,1536]{2,1,0:T(8,128)(2,1)S(1)} %copy-done.12, bf16[2,96,1536]{2,1,0:T(8,128)(2,1)S(1)} %copy-done.10, bf16[2,1536,1536]{2,1,0:T(8,128)(2,1)} %bitcast.88, f32[2,2,96,1]{3,2,1,0:T(8,128)S(1)} %get-tuple-element.30.refs_3_, ...), custom_call_target="tpu_custom_call" | custom-call | flops 1811939328 | bytes 9437184 | tf_op jit(solution)/shard_map/contract/pallas_call | solution.py:65
  152.3 1.0 collective-permute-start.13
  153.3 1.8 combine.11.refs_1_
  155.1 1.8 combine.10.refs_0_
  156.9 9.7 %contract.5 = (bf16[2,96,1536]{2,1,0:T(8,128)(2,1)S(1)}, bf16[2,96,1536]{2,1,0:T(8,128)(2,1)S(1)}) custom-call(bf16[2,96,1536]{2,1,0:T(8,128)(2,1)S(1)} %copy-done.8, bf16[2,96,1536]{2,1,0:T(8,128)(2,1)S(1)} %copy-done.6, bf16[2,1536,1536]{2,1,0:T(8,128)(2,1)} %bitcast.89, f32[2,2,96,1]{3,2,1,0:T(8,128)S(1)} %get-tuple-element.29.refs_3_, ...), custom_call_target="tpu_custom_call" | custom-call | flops 1811939328 | bytes 9437184 | tf_op jit(solution)/shard_map/contract/pallas_call | solution.py:65
  166.8 2.3 %collective-permute-start.14 = (bf16[2,96,1536]{2,1,0:T(8,128)(2,1)S(1)}, bf16[2,96,1536]{2,1,0:T(8,128)(2,1)S(1)}, u32[]{:S(2)}, u32[]{:S(2)}) collective-permute-start(bf16[2,96,1536]{2,1,0:T(8,128)(2,1)S(1)} %get-tuple-element.14), channel_id=1, source_target_pairs={{0,80},{16,64},{32,112},{48,96},{64,16},{80,0},{96,48},{112,32},{1... | collective-permute-start | bytes 1769480 | tf_op jit(solution)/shard_map/ppermute | solution.py:133
  169.2 10.7 %contract.4 = (bf16[2,96,1536]{2,1,0:T(8,128)(2,1)S(1)}, bf16[2,96,1536]{2,1,0:T(8,128)(2,1)S(1)}, bf16[2,96,1536]{2,1,0:T(8,128)(2,1)S(1)}, bf16[2,96,1536]{2,1,0:T(8,128)(2,1)S(1)}) custom-call(bf16[2,96,1536]{2,1,0:T(8,128)(2,1)S(1)} %combine.10.refs_0_, bf16[2,96,1536]{2,1,0:T(8,128)(2,1)S(1)} %combine.11.refs_1_, bf16[2,96,1536]{2,1,0:T(8,128)(2,1)S(1)} %copy-done.18, ...), custom_call_target="tpu_custom_call" | custom-call | flops 3623878656 | bytes 9437184 | tf_op jit(solution)/shard_map/contract/pallas_call | solution.py:65
  180.0 1.5 collective-permute-start.20
  181.5 0.5 collective-permute-start.21
  182.0 0.4 broadcast_in_dim.6
  182.5 1.1 collective-permute-done.14
  183.7 0.4 collective-permute-start.22
  184.1 11.2 %collective-permute-done.19 = bf16[2,96,1536]{2,1,0:T(8,128)(2,1)S(1)} collective-permute-done((bf16[2,96,1536]{2,1,0:T(8,128)(2,1)S(1)}, bf16[2,96,1536]{2,1,0:T(8,128)(2,1)S(1)}, u32[]{:S(2)}, u32[]{:S(2)}) %collective-permute-start.19) | collective-permute-done | bytes 589856 | tf_op jit(solution)/shard_map/ppermute | solution.py:133
  195.4 13.1 %collective-permute-done.20 = bf16[2,96,1536]{2,1,0:T(8,128)(2,1)S(1)} collective-permute-done((bf16[2,96,1536]{2,1,0:T(8,128)(2,1)S(1)}, bf16[2,96,1536]{2,1,0:T(8,128)(2,1)S(1)}, u32[]{:S(2)}, u32[]{:S(2)}) %collective-permute-start.20) | collective-permute-done | bytes 589856 | tf_op jit(solution)/shard_map/ppermute | solution.py:133
  208.7 1.7 collective-permute-done.22
  210.5 0.4 copy.38
  211.0 2.2 copy-done.19
  (93 shorter events, 2.5 us)
Async XLA Ops:
  6.5 47.3 %copy-start = (f32[16,96]{1,0:T(8,128)S(1)}, f32[16,96]{1,0:T(8,128)}, u32[]{:S(2)}) copy-start(f32[16,96]{1,0:T(8,128)} %param.10) | copy-start | bytes 18436
  6.5 115.2 %all-gather.2.cloned.1.call-start = ((), (), s32[]{:S(2)}) async-start(), calls=%async_computation | async-start | bytes 4866048 | tf_op jit(solution)/shard_map/all_gather | solution.py:164
  8.2 6.2 %collective-permute-start.4 = (bf16[48,1536]{1,0:T(8,128)(2,1)S(1)}, bf16[48,1536]{1,0:T(8,128)(2,1)S(1)}, u32[]{:S(2)}, u32[]{:S(2)}) collective-permute-start(bf16[48,1536]{1,0:T(8,128)(2,1)S(1)} %get-tuple-element.32), channel_id=1, source_target_pairs={{0,4},{4,8},{8,12},{12,0},{1,5},{5,9},{9,13},{13,1},{2,6},{6,10},{... | collective-permute-start | bytes 442376 | tf_op jit(solution)/shard_map/ppermute | solution.py:137
  10.4 9.0 %collective-permute-start.3 = (bf16[48,1536]{1,0:T(8,128)(2,1)S(1)}, bf16[48,1536]{1,0:T(8,128)(2,1)S(1)}, u32[]{:S(2)}, u32[]{:S(2)}) collective-permute-start(bf16[48,1536]{1,0:T(8,128)(2,1)S(1)} %get-tuple-element.32), channel_id=1, source_target_pairs={{0,8},{4,12},{8,0},{12,4},{1,9},{5,13},{9,1},{13,5},{2,10},{6,14},... | collective-permute-start | bytes 442376 | tf_op jit(solution)/shard_map/ppermute | solution.py:137
  13.1 6.4 %collective-permute-start.2 = (bf16[48,1536]{1,0:T(8,128)(2,1)S(1)}, bf16[48,1536]{1,0:T(8,128)(2,1)S(1)}, u32[]{:S(2)}, u32[]{:S(2)}) collective-permute-start(bf16[48,1536]{1,0:T(8,128)(2,1)S(1)} %get-tuple-element.32), channel_id=1, source_target_pairs={{0,12},{4,0},{8,4},{12,8},{1,13},{5,1},{9,5},{13,9},{2,14},{6,2},{... | collective-permute-start | bytes 442376 | tf_op jit(solution)/shard_map/ppermute | solution.py:137
  19.6 19.7 %collective-permute-start.8 = (bf16[4,48,1536]{2,1,0:T(8,128)(2,1)S(1)}, bf16[4,48,1536]{2,1,0:T(8,128)(2,1)S(1)}, u32[]{:S(2)}, u32[]{:S(2)}) collective-permute-start(bf16[4,48,1536]{2,1,0:T(8,128)(2,1)S(1)} %pad_maximum_fusion.refs_0_), channel_id=1, source_target_pairs={{0,1},{1,2},{2,3},{3,128},{128,129},{129,130},{130,131},{131,0},{4... | collective-permute-start | bytes 1769480 | tf_op jit(solution)/shard_map/ppermute | solution.py:141
  21.3 18.0 %copy-start.20 = (s32[1,16,16]{2,1,0:T(8,128)S(1)}, s32[1,16,16]{2,1,0:T(8,128)}, u32[]{:S(2)}) copy-start(s32[1,16,16]{2,1,0:T(8,128)} %param.11) | copy-start | bytes 3076
  21.3 32.4 %copy-start.22 = (f32[1,16]{1,0:T(1,128)S(1)}, f32[1,16]{1,0:T(1,128)}, u32[]{:S(2)}) copy-start(f32[1,16]{1,0:T(1,128)} %param.9) | copy-start | bytes 196
  21.3 35.0 %copy-start.21 = (f32[16,16]{1,0:T(8,128)S(1)}, f32[16,16]{1,0:T(8,128)}, u32[]{:S(2)}) copy-start(f32[16,16]{1,0:T(8,128)} %param.8) | copy-start | bytes 3076
  25.9 67.3 %collective-permute-start.23 = (bf16[2,96,1536]{2,1,0:T(8,128)(2,1)}, bf16[2,96,1536]{2,1,0:T(8,128)(2,1)}, u32[]{:S(2)}, u32[]{:S(2)}) collective-permute-start(bf16[2,96,1536]{2,1,0:T(8,128)(2,1)} %get-tuple-element.22), channel_id=1, source_target_pairs={{0,16},{16,0},{1,17},{17,1},{2,18},{18,2},{3,19},{19,3},{4,20},{20... | collective-permute-start | bytes 1769480 | tf_op jit(solution)/shard_map/ppermute | solution.py:129
  27.7 69.5 %collective-permute-start.18 = (bf16[2,96,1536]{2,1,0:T(8,128)(2,1)}, bf16[2,96,1536]{2,1,0:T(8,128)(2,1)}, u32[]{:S(2)}, u32[]{:S(2)}) collective-permute-start(bf16[2,96,1536]{2,1,0:T(8,128)(2,1)} %get-tuple-element.23), channel_id=1, source_target_pairs={{0,112},{16,96},{32,16},{48,0},{64,48},{80,32},{96,80},{112,64},{1... | collective-permute-start | bytes 1769480 | tf_op jit(solution)/shard_map/ppermute | solution.py:133
  30.2 74.1 %collective-permute-start.17 = (bf16[2,96,1536]{2,1,0:T(8,128)(2,1)}, bf16[2,96,1536]{2,1,0:T(8,128)(2,1)}, u32[]{:S(2)}, u32[]{:S(2)}) collective-permute-start(bf16[2,96,1536]{2,1,0:T(8,128)(2,1)} %get-tuple-element.24), channel_id=1, source_target_pairs={{0,96},{16,112},{32,0},{48,16},{64,32},{80,48},{96,64},{112,80},{1... | collective-permute-start | bytes 1769480 | tf_op jit(solution)/shard_map/ppermute | solution.py:133
  30.8 19.2 %collective-permute-start.5 = (bf16[4,48,1536]{2,1,0:T(8,128)(2,1)S(1)}, bf16[4,48,1536]{2,1,0:T(8,128)(2,1)S(1)}, u32[]{:S(2)}, u32[]{:S(2)}) collective-permute-start(bf16[4,48,1536]{2,1,0:T(8,128)(2,1)S(1)} %pad_maximum_fusion.refs_0_), channel_id=1, source_target_pairs={{0,131},{1,0},{2,1},{3,2},{128,3},{129,128},{130,129},{131,130},{4... | collective-permute-start | bytes 1769480 | tf_op jit(solution)/shard_map/ppermute | solution.py:141
  39.3 16.9 %collective-permute-start.9 = (bf16[4,48,1536]{2,1,0:T(8,128)(2,1)S(1)}, bf16[4,48,1536]{2,1,0:T(8,128)(2,1)}, u32[]{:S(2)}, u32[]{:S(2)}) collective-permute-start(bf16[4,48,1536]{2,1,0:T(8,128)(2,1)S(1)} %collective-permute-done.8.refs_7_), channel_id=1, source_target_pairs={{0,1},{1,2},{2,3},{3,128},{128,129},{129,130},{130,131},{131,0},{4... | collective-permute-start | bytes 1769480 | tf_op jit(solution)/shard_map/ppermute | solution.py:141
  50.1 61.8 %copy-start.3 = (bf16[4,48,1536]{2,1,0:T(8,128)(2,1)}, bf16[4,48,1536]{2,1,0:T(8,128)(2,1)S(1)}, u32[]{:S(2)}) copy-start(bf16[4,48,1536]{2,1,0:T(8,128)(2,1)S(1)} %collective-permute-done.5.refs_1_) | copy-start | bytes 1769476
  50.1 14.8 %collective-permute-start.6 = (bf16[4,48,1536]{2,1,0:T(8,128)(2,1)S(1)}, bf16[4,48,1536]{2,1,0:T(8,128)(2,1)}, u32[]{:S(2)}, u32[]{:S(2)}) collective-permute-start(bf16[4,48,1536]{2,1,0:T(8,128)(2,1)S(1)} %collective-permute-done.5.refs_1_), channel_id=1, source_target_pairs={{0,131},{1,0},{2,1},{3,2},{128,3},{129,128},{130,129},{131,130},{4... | collective-permute-start | bytes 1769480 | tf_op jit(solution)/shard_map/ppermute | solution.py:141
  56.2 14.2 %collective-permute-start.10 = (bf16[4,48,1536]{2,1,0:T(8,128)(2,1)}, bf16[4,48,1536]{2,1,0:T(8,128)(2,1)S(1)}, u32[]{:S(2)}, u32[]{:S(2)}) collective-permute-start(bf16[4,48,1536]{2,1,0:T(8,128)(2,1)} %collective-permute-done.9.refs_6_), channel_id=1, source_target_pairs={{0,1},{1,2},{2,3},{3,128},{128,129},{129,130},{130,131},{131,0},{4... | collective-permute-start | bytes 1769480 | tf_op jit(solution)/shard_map/ppermute | solution.py:141
  64.9 25.3 %collective-permute-start.7 = (bf16[4,48,1536]{2,1,0:T(8,128)(2,1)}, bf16[4,48,1536]{2,1,0:T(8,128)(2,1)S(1)}, u32[]{:S(2)}, u32[]{:S(2)}) collective-permute-start(bf16[4,48,1536]{2,1,0:T(8,128)(2,1)} %collective-permute-done.6.refs_2_), channel_id=1, source_target_pairs={{0,131},{1,0},{2,1},{3,2},{128,3},{129,128},{130,129},{131,130},{4... | collective-permute-start | bytes 1769480 | tf_op jit(solution)/shard_map/ppermute | solution.py:141
  70.4 42.3 %collective-permute-start.1 = (bf16[2,96,1536]{2,1,0:T(8,128)(2,1)}, bf16[2,96,1536]{2,1,0:T(8,128)(2,1)}, u32[]{:S(2)}, u32[]{:S(2)}) collective-permute-start(bf16[2,96,1536]{2,1,0:T(8,128)(2,1)} %get-tuple-element.27), channel_id=1, source_target_pairs={{0,80},{16,64},{32,112},{48,96},{64,16},{80,0},{96,48},{112,32},{1... | collective-permute-start | bytes 1769480 | tf_op jit(solution)/shard_map/ppermute | solution.py:133
  90.1 29.8 %collective-permute-start = (bf16[2,96,1536]{2,1,0:T(8,128)(2,1)}, bf16[2,96,1536]{2,1,0:T(8,128)(2,1)S(1)}, u32[]{:S(2)}, u32[]{:S(2)}) collective-permute-start(bf16[2,96,1536]{2,1,0:T(8,128)(2,1)} %get-tuple-element.28), channel_id=1, source_target_pairs={{0,64},{16,80},{32,96},{48,112},{64,0},{80,16},{96,32},{112,48},{1... | collective-permute-start | bytes 1769480 | tf_op jit(solution)/shard_map/ppermute | solution.py:133
  93.2 28.4 %collective-permute-start.11 = (bf16[2,48,1536]{2,1,0:T(8,128)(2,1)S(1)}, bf16[2,48,1536]{2,1,0:T(8,128)(2,1)S(1)}, u32[]{:S(2)}, u32[]{:S(2)}) collective-permute-start(bf16[2,48,1536]{2,1,0:T(8,128)(2,1)S(1)} %slice.55), channel_id=1, source_target_pairs={{0,1},{1,2},{2,3},{3,128},{128,129},{129,130},{130,131},{131,0},{4... | collective-permute-start | bytes 884744 | tf_op jit(solution)/shard_map/ppermute | solution.py:141
  97.2 24.5 %collective-permute-start.12 = (bf16[2,48,1536]{2,1,0:T(8,128)(2,1)S(1)}, bf16[2,48,1536]{2,1,0:T(8,128)(2,1)S(1)}, u32[]{:S(2)}, u32[]{:S(2)}) collective-permute-start(bf16[2,48,1536]{2,1,0:T(8,128)(2,1)S(1)} %slice.56), channel_id=1, source_target_pairs={{0,131},{1,0},{2,1},{3,2},{128,3},{129,128},{130,129},{131,130},{4... | collective-permute-start | bytes 884744 | tf_op jit(solution)/shard_map/ppermute | solution.py:141
  97.2 1.1 copy-start.13
  99.1 0.8 copy-start.5
  103.5 0.8 copy-start.7
  104.3 49.0 %collective-permute-start.16 = (bf16[2,96,1536]{2,1,0:T(8,128)(2,1)}, bf16[2,96,1536]{2,1,0:T(8,128)(2,1)}, u32[]{:S(2)}, u32[]{:S(2)}) collective-permute-start(bf16[2,96,1536]{2,1,0:T(8,128)(2,1)} %get-tuple-element.25), channel_id=1, source_target_pairs={{0,48},{16,32},{32,80},{48,64},{64,112},{80,96},{96,16},{112,0},{1... | collective-permute-start | bytes 1769480 | tf_op jit(solution)/shard_map/ppermute | solution.py:133
  111.8 0.8 copy-start.15
  112.7 42.4 %collective-permute-start.15 = (bf16[2,96,1536]{2,1,0:T(8,128)(2,1)}, bf16[2,96,1536]{2,1,0:T(8,128)(2,1)}, u32[]{:S(2)}, u32[]{:S(2)}) collective-permute-start(bf16[2,96,1536]{2,1,0:T(8,128)(2,1)} %get-tuple-element.26), channel_id=1, source_target_pairs={{0,32},{16,48},{32,64},{48,80},{64,96},{80,112},{96,0},{112,16},{1... | collective-permute-start | bytes 1769480 | tf_op jit(solution)/shard_map/ppermute | solution.py:133
  117.9 2.0 copy-start.17
  120.0 1.7 copy-start.9
  120.8 0.8 copy-start.11
  121.7 2.3 %copy-start.2 = (bf16[32,48,1536]{2,1,0:T(8,128)(2,1)S(1)}, bf16[32,48,1536]{2,1,0:T(8,128)(2,1)}, u32[]{:S(2)}) copy-start(bf16[32,48,1536]{2,1,0:T(8,128)(2,1)} %all-gather.2.cloned.1.call-done) | copy-start | bytes 14155780
  124.1 1.1 copy-start.4
  125.1 17.5 %copy-start.10 = (bf16[2,96,1536]{2,1,0:T(8,128)(2,1)S(1)}, bf16[2,96,1536]{2,1,0:T(8,128)(2,1)}, u32[]{:S(2)}) copy-start(bf16[2,96,1536]{2,1,0:T(8,128)(2,1)} %copy-done.9) | copy-start | bytes 1769476
  125.1 17.5 %copy-start.12 = (bf16[2,96,1536]{2,1,0:T(8,128)(2,1)S(1)}, bf16[2,96,1536]{2,1,0:T(8,128)(2,1)}, u32[]{:S(2)}) copy-start(bf16[2,96,1536]{2,1,0:T(8,128)(2,1)} %copy-done.11) | copy-start | bytes 1769476
  139.0 3.6 %copy-start.1 = (bf16[2,4,4,2,48,1536]{5,4,3,2,1,0:T(8,128)(2,1)}, bf16[2,4,4,2,48,1536]{5,4,3,2,1,0:T(8,128)(2,1)S(1)}, u32[]{:S(2)}) copy-start(bf16[2,4,4,2,48,1536]{5,4,3,2,1,0:T(8,128)(2,1)S(1)} %assemble.1) | copy-start | bytes 28311556
  152.2 4.6 %copy-start.6 = (bf16[2,96,1536]{2,1,0:T(8,128)(2,1)S(1)}, bf16[2,96,1536]{2,1,0:T(8,128)(2,1)}, u32[]{:S(2)}) copy-start(bf16[2,96,1536]{2,1,0:T(8,128)(2,1)} %copy-done.5) | copy-start | bytes 1769476
  152.2 4.6 %copy-start.8 = (bf16[2,96,1536]{2,1,0:T(8,128)(2,1)S(1)}, bf16[2,96,1536]{2,1,0:T(8,128)(2,1)}, u32[]{:S(2)}) copy-start(bf16[2,96,1536]{2,1,0:T(8,128)(2,1)} %copy-done.7) | copy-start | bytes 1769476
  152.3 29.2 %collective-permute-start.13 = (bf16[2,96,1536]{2,1,0:T(8,128)(2,1)S(1)}, bf16[2,96,1536]{2,1,0:T(8,128)(2,1)S(1)}, u32[]{:S(2)}, u32[]{:S(2)}) collective-permute-start(bf16[2,96,1536]{2,1,0:T(8,128)(2,1)S(1)} %get-tuple-element.13), channel_id=1, source_target_pairs={{0,64},{16,80},{32,96},{48,112},{64,0},{80,16},{96,32},{112,48},{1... | collective-permute-start | bytes 1769480 | tf_op jit(solution)/shard_map/ppermute | solution.py:133
  156.9 12.3 %copy-start.14 = (f32[2,4,96,1]{3,2,1,0:T(8,128)S(1)}, f32[2,4,96,1]{3,2,1,0:T(8,128)}, u32[]{:S(2)}) copy-start(f32[2,4,96,1]{3,2,1,0:T(8,128)} %slice.59.refs_5_) | copy-start | bytes 9220
  156.9 12.2 %copy-start.16 = (bf16[2,96,1536]{2,1,0:T(8,128)(2,1)S(1)}, bf16[2,96,1536]{2,1,0:T(8,128)(2,1)}, u32[]{:S(2)}) copy-start(bf16[2,96,1536]{2,1,0:T(8,128)(2,1)} %copy-done.15) | copy-start | bytes 1769476
  156.9 12.2 %copy-start.18 = (bf16[2,96,1536]{2,1,0:T(8,128)(2,1)S(1)}, bf16[2,96,1536]{2,1,0:T(8,128)(2,1)}, u32[]{:S(2)}) copy-start(bf16[2,96,1536]{2,1,0:T(8,128)(2,1)} %copy-done.17) | copy-start | bytes 1769476
  166.6 43.8 %collective-permute-start.24 = (bf16[2,96,1536]{2,1,0:T(8,128)(2,1)S(1)}, bf16[2,96,1536]{2,1,0:T(8,128)(2,1)S(1)}, u32[]{:S(2)}, u32[]{:S(2)}) collective-permute-start(bf16[2,96,1536]{2,1,0:T(8,128)(2,1)S(1)} %get-tuple-element.19), channel_id=1, source_target_pairs={{0,16},{16,0},{1,17},{17,1},{2,18},{18,2},{3,19},{19,3},{4,20},{20... | collective-permute-start | bytes 1769480 | tf_op jit(solution)/shard_map/ppermute | solution.py:129
  166.8 16.8 %collective-permute-start.14 = (bf16[2,96,1536]{2,1,0:T(8,128)(2,1)S(1)}, bf16[2,96,1536]{2,1,0:T(8,128)(2,1)S(1)}, u32[]{:S(2)}, u32[]{:S(2)}) collective-permute-start(bf16[2,96,1536]{2,1,0:T(8,128)(2,1)S(1)} %get-tuple-element.14), channel_id=1, source_target_pairs={{0,80},{16,64},{32,112},{48,96},{64,16},{80,0},{96,48},{112,32},{1... | collective-permute-start | bytes 1769480 | tf_op jit(solution)/shard_map/ppermute | solution.py:133
  179.9 15.5 %collective-permute-start.19 = (bf16[2,96,1536]{2,1,0:T(8,128)(2,1)S(1)}, bf16[2,96,1536]{2,1,0:T(8,128)(2,1)S(1)}, u32[]{:S(2)}, u32[]{:S(2)}) collective-permute-start(bf16[2,96,1536]{2,1,0:T(8,128)(2,1)S(1)} %get-tuple-element.15), channel_id=1, source_target_pairs={{0,96},{16,112},{32,0},{48,16},{64,32},{80,48},{96,64},{112,80},{1... | collective-permute-start | bytes 1769480 | tf_op jit(solution)/shard_map/ppermute | solution.py:133
  180.0 28.6 %collective-permute-start.20 = (bf16[2,96,1536]{2,1,0:T(8,128)(2,1)S(1)}, bf16[2,96,1536]{2,1,0:T(8,128)(2,1)S(1)}, u32[]{:S(2)}, u32[]{:S(2)}) collective-permute-start(bf16[2,96,1536]{2,1,0:T(8,128)(2,1)S(1)} %get-tuple-element.16), channel_id=1, source_target_pairs={{0,112},{16,96},{32,16},{48,0},{64,48},{80,32},{96,80},{112,64},{1... | collective-permute-start | bytes 1769480 | tf_op jit(solution)/shard_map/ppermute | solution.py:133
  181.5 27.1 %collective-permute-start.21 = (bf16[2,96,1536]{2,1,0:T(8,128)(2,1)S(1)}, bf16[2,96,1536]{2,1,0:T(8,128)(2,1)S(1)}, u32[]{:S(2)}, u32[]{:S(2)}) collective-permute-start(bf16[2,96,1536]{2,1,0:T(8,128)(2,1)S(1)} %get-tuple-element.17), channel_id=1, source_target_pairs={{0,32},{16,48},{32,64},{48,80},{64,96},{80,112},{96,0},{112,16},{1... | collective-permute-start | bytes 1769480 | tf_op jit(solution)/shard_map/ppermute | solution.py:133
  183.7 26.7 %collective-permute-start.22 = (bf16[2,96,1536]{2,1,0:T(8,128)(2,1)S(1)}, bf16[2,96,1536]{2,1,0:T(8,128)(2,1)S(1)}, u32[]{:S(2)}, u32[]{:S(2)}) collective-permute-start(bf16[2,96,1536]{2,1,0:T(8,128)(2,1)S(1)} %get-tuple-element.18), channel_id=1, source_target_pairs={{0,48},{16,32},{32,80},{48,64},{64,112},{80,96},{96,16},{112,0},{1... | collective-permute-start | bytes 1769480 | tf_op jit(solution)/shard_map/ppermute | solution.py:133
  211.0 2.2 copy-start.19
Sparse Core Ops, SparseCore 0:
  9.9 94.0 all-gather.1

commit v2 on v0

v2 whole, which is shorter than its diff:
```python
import jax
import jax.numpy as jnp
from jax import lax
from jax.experimental import pallas as pl
from jax.experimental.pallas import tpu as pltpu
from jax.sharding import Mesh, PartitionSpec as P

NO = 16
NV = 96
PAIRS = NO * NV
VS = 6
ROWS = VS * NO
VMEM = 48 << 20
RING = ("zh", "zl")
NA = 768
NT = 384


def combine(x):
    nb, sq, step = x.shape[0], NO * NO, 4

    def kernel(x_ref, o_ref, scr):
        @pl.loop(0, step)
        def _(e):
            for a in range(VS):
                xa = x_ref[e, NO * a : NO * a + NO, :].astype(jnp.float32)
                for p in range(NO):
                    lo = a * sq + NO * p
                    scr[lo : lo + NO, 0:NV] = xa[:, NV * p : NV * p + NV]
            for a in range(VS):
                xa = x_ref[e, NO * a : NO * a + NO, :].astype(jnp.float32)
                swapped = jnp.concatenate(
                    [scr[pl.ds(a * sq + q, NO, stride=NO), :][:, :NV] for q in range(NO)], axis=1
                )
                o_ref[e, NO * a : NO * a + NO, :] = (2.0 * xa - swapped).astype(jnp.bfloat16)

    return pl.pallas_call(
        kernel,
        grid=(2, nb // step),
        in_specs=[pl.BlockSpec((step, None, ROWS, PAIRS), lambda q, b: (b, q, 0, 0))],
        out_specs=pl.BlockSpec((None, step, ROWS, PAIRS), lambda q, b: (q, b, 0, 0)),
        out_shape=jax.ShapeDtypeStruct((2, nb, ROWS, PAIRS), x.dtype),
        scratch_shapes=[pltpu.VMEM((VS * sq, 128), jnp.float32)],
        compiler_params=pltpu.CompilerParams(vmem_limit_bytes=VMEM),
        cost_estimate=pl.CostEstimate(
            flops=2 * nb * 300000000, bytes_accessed=4 * x.size, transcendentals=0
        ),
        name="combine",
    )(x)


def contract(comb, pos, pieces, place, rr, cc, lo, name):
    nb = comb.shape[1]
    width = NA if lo == 0 else PAIRS - NA
    npc = len(pieces)

    def kernel(pos_ref, x_ref, *refs):
        p_refs, (r_ref, c_ref, o_ref, w_ref) = refs[:npc], refs[npc:]
        q, n = pl.program_id(0), pl.program_id(1)

        @pl.when(n == 0)
        def _():
            place(p_refs, w_ref, q, pos_ref[0], pos_ref[1])

        cols = pl.ds(pl.multiple_of(n * NT, NT), NT)
        x = x_ref[...].reshape(nb * ROWS, PAIRS)
        acc = jnp.dot(x, w_ref[:, cols], preferred_element_type=jnp.float32)
        for m in range(nb):
            gap = r_ref[m] + c_ref[m]
            o_ref[m] = (acc[ROWS * m : ROWS * m + ROWS] / gap).astype(jnp.bfloat16)

    vmem = pl.BlockSpec(memory_space=pltpu.VMEM)
    return pl.pallas_call(
        kernel,
        grid=(2, width // NT),
        in_specs=[
            pl.BlockSpec(memory_space=pltpu.SMEM),
            pl.BlockSpec((None, nb, ROWS, PAIRS), lambda q, n: (q, 0, 0, 0)),
        ]
        + [vmem] * npc
        + [
            pl.BlockSpec((None, nb, ROWS, 1), lambda q, n: (q, 0, 0, 0)),
            pl.BlockSpec((None, nb, 1, NT), lambda q, n: (q, 0, 0, lo // NT + n)),
        ],
        out_specs=pl.BlockSpec((nb, None, ROWS, NT), lambda q, n: (0, q, 0, n)),
        out_shape=jax.ShapeDtypeStruct((nb, 2, ROWS, width), jnp.bfloat16),
        scratch_shapes=[pltpu.VMEM((PAIRS, width), jnp.bfloat16)],
        compiler_params=pltpu.CompilerParams(vmem_limit_bytes=VMEM),
        cost_estimate=pl.CostEstimate(
            flops=4 * nb * ROWS * PAIRS * width, bytes_accessed=8 * PAIRS * width, transcendentals=0
        ),
        name=name,
    )(pos, comb, *pieces, rr, cc)


def place_a(p_refs, w_ref, q, y, z):
    for zl in range(4):
        for e in range(4):
            k = lax.rem(y + e, 4) * 4 + zl
            w_ref[pl.ds(pl.multiple_of(k * NV, NV), NV), :] = p_refs[0][q * 4 + zl, e]


def place_b(p_refs, w_ref, q, y, z):
    for e in range(4):
        for zl in range(4):
            k = lax.rem(y + e, 4) * 4 + zl
            s = lax.rem(q * 4 + zl + 8 - z, 8)
            w_ref[pl.ds(pl.multiple_of(k * NV, NV), NV), :] = p_refs[e][s]


def merge(part, lo, out, name):
    nb, width = part.shape[0], part.shape[-1]

    def kernel(v_ref, *refs):
        refs[-1][...] = v_ref[...]

    return pl.pallas_call(
        kernel,
        grid=(2, nb // 4),
        in_specs=[pl.BlockSpec((4, None, ROWS, width), lambda q, b: (b, q, 0, 0))]
        + [pl.BlockSpec(memory_space=pl.ANY)] * (out is not None),
        out_specs=pl.BlockSpec((None, 4, ROWS, width), lambda q, b: (q, b, 0, lo // width)),
        out_shape=jax.ShapeDtypeStruct((2, nb, ROWS, PAIRS), jnp.bfloat16),
        input_output_aliases={} if out is None else {1: 0},
        compiler_params=pltpu.CompilerParams(vmem_limit_bytes=VMEM),
        name=name,
    )(part, *([] if out is None else [out]))


def y_permute(v, s):
    return lax.ppermute(v, "y", [(i, (i + s) % 4) for i in range(4)])


def z_permute(v, s):
    return lax.ppermute(v, RING, [(i, (i + s) % 8) for i in range(8)])


def tie(*vs):
    return lax.optimization_barrier(vs)


def gather_w(own, got):
    a, b = own[:, :NA], own[:, NA:]
    half = NV // 2
    a1, a2, a3 = y_permute(a, -1), y_permute(a, 2), y_permute(a, 1)
    up, down = [b], [b]
    for s in range(3):
        up.append(z_permute(up[-1], 1))
        down.append(z_permute(down[-1], -1))
        if s == 0:
            col = jnp.stack([a, a1, a2, a3])
            col, up[1], down[1] = tie(col, up[1], down[1])
    col = lax.all_gather(col, RING, axis=0)
    far = jnp.concatenate([z_permute(up[3][:half], 1), z_permute(down[3][half:], -1)])
    row = jnp.stack([b, down[1], down[2], down[3], far, up[3], up[2], up[1]])
    below, above = y_permute(row, 1), y_permute(row, -1)
    comb = combine(got)
    below, above, comb = tie(below, above, comb)
    far = jnp.concatenate([y_permute(below[:4], 1), y_permute(above[4:], -1)])
    return [col], [row, above, far, below], comb


def per_device(amps, wshard, occ, occj, virt, table):
    zh, x, c = lax.axis_index("zh"), lax.axis_index("x"), lax.axis_index("c")
    y, zl = lax.axis_index("y"), lax.axis_index("zl")
    pos = jnp.stack([y, zh * 4 + zl]).astype(jnp.int32)

    blocks = jnp.transpose(amps[0, 0], (0, 2, 1, 3)).reshape(2, 8, ROWS, PAIRS)
    blocks = jnp.swapaxes(blocks, 0, 1)
    own, blocks = tie(wshard[0], blocks)
    got = lax.all_to_all(blocks, ("x", "c"), split_axis=0, concat_axis=0, tiled=True)
    part_a, part_b, comb = gather_w(own, got)

    va = lax.dynamic_slice(virt, (0, (y * 4 + zl) * VS), (NO, VS)).reshape(2, 8, VS)
    va = lax.dynamic_index_in_dim(va, x * 2 + c, 1, False)
    occ_i = lax.dynamic_slice(occ, (zh * 8, 0), (8, NO))
    rr = (occ_i[None, :, None, :] - va[:, None, :, None]).reshape(2, 8, ROWS, 1)
    kb = lax.dynamic_slice(table[0], (zh * 8, 0), (8, NO)).reshape(8, 2, 8)
    kb = lax.dynamic_index_in_dim(kb, x * 2 + c, 2, False).T
    cc = (occj[0][None, None, :, None] - virt[kb][:, :, None, :]).reshape(2, 8, 1, PAIRS)

    out = None
    for lo, part, place, name in ((0, part_a, place_a, "_a"), (NA, part_b, place_b, "_b")):
        res = contract(comb, pos, part, place, rr, cc, lo, "contract" + name)
        res = lax.all_to_all(res, ("x", "c"), split_axis=0, concat_axis=0, tiled=True)
        out = merge(res, lo, out, "merge" + name)
    out = out.reshape(NO, VS, NO, PAIRS)
    return jnp.transpose(out, (0, 2, 1, 3))[None, None]


def solution(mesh):
    fine = Mesh(mesh.devices.reshape(2, 4, 2, 4, 4), ("zh", "x", "c", "y", "zl"))
    ka, vert = ("zh", "x", "c"), ("y", "zl")
    in_specs = (P(None, ka, None, None, vert, None), P(ka, vert, None), P(), P(), P(), P())
    out_specs = P(None, ka, None, None, vert, None)
    return jax.shard_map(
        per_device, mesh=fine, in_specs=in_specs, out_specs=out_specs, check_vma=False
    )
```

time: 390 us -> 188 us (0.48)
  the two profiles are of different devices: /device:TPU:33 before, /device:TPU:1 now
where the time goes in v2:
time: 188 us; the launch traced here: 187 us
  waiting for transfers between devices  80 us (43%)
  starting transfers between devices  42.1 us (22%)
  Pallas kernels  33.3 us (18%)
  local copies, waits for them, and re-layouts  16.3 us (9%)
  between operations  13.6 us (7%)
  other arithmetic  2.04 us (1%)
    all_to_all x2, waiting for transfers between devices, per_device(): lax.all_to_all(res, ('x', 'c'), split_axis=0, concat_axis=0, tiled=True)  29.3 us
    all_to_all x1, waiting for transfers between devices, per_device(): lax.all_to_all(blocks, ('x', 'c'), split_axis=0, concat_axis=0, tiled=True)  19.7 us
    pallas_call x2, Pallas kernels, contract(): pl.pallas_call(kernel, grid=(2, width // NT), in_specs=[pl.BlockSpec(memo...  19.7 us
    ppermute x8, waiting for transfers between devices, z_permute(): return lax.ppermute(v, RING, [(i, (i + s) % 8) for i in range(8)])  16.3 us
    ppermute x8, starting transfers between devices, z_permute(): return lax.ppermute(v, RING, [(i, (i + s) % 8) for i in range(8)])  15.7 us
    ppermute x7, waiting for transfers between devices, y_permute(): return lax.ppermute(v, 'y', [(i, (i + s) % 4) for i in range(4)])  14.7 us
    ppermute x7, starting transfers between devices, y_permute(): return lax.ppermute(v, 'y', [(i, (i + s) % 4) for i in range(4)])  10.1 us
    all_to_all x2, starting transfers between devices, per_device(): lax.all_to_all(res, ('x', 'c'), split_axis=0, concat_axis=0, tiled=True)  9.49 us
  transfers between devices with their start and end apart: 19, of which 10 were waited for; matrix products, arithmetic and copies ran while one was open for 5% of the time, Pallas kernels for 10%

profile of v2, /device:TPU:1, one launch (start us, length us, event | category | flops | bytes accessed | tf_op | source)
XLA Modules:
  0.0 187.4 jit_solution(13348206053314725506)
XLA Ops:
  6.5 5.0 %copy.23 = bf16[2,8,96,1536]{3,2,0,1:T(8,128)(2,1)} copy(bf16[2,8,96,1536]{3,2,1,0:T(8,128)(2,1)} %bitcast.54) | data formatting | bytes 9437184 | tf_op jit(solution)/shard_map/reshape | solution.py:168
  11.6 2.2 %collective-permute-start.2 = (bf16[96,768]{1,0:T(8,128)(2,1)S(1)}, bf16[96,768]{1,0:T(8,128)(2,1)S(1)}, u32[]{:S(2)}, u32[]{:S(2)}) collective-permute-start(bf16[96,768]{1,0:T(8,128)(2,1)S(1)} %get-tuple-element.23), channel_id=1, source_target_pairs={{0,4},{4,8},{8,12},{12,0},{1,5},{5,9},{9,13},{13,1},{2,6},{6,10},{... | collective-permute-start | bytes 442376 | tf_op jit(solution)/shard_map/ppermute | solution.py:131
  13.8 2.6 %collective-permute-start.1 = (bf16[96,768]{1,0:T(8,128)(2,1)S(1)}, bf16[96,768]{1,0:T(8,128)(2,1)S(1)}, u32[]{:S(2)}, u32[]{:S(2)}) collective-permute-start(bf16[96,768]{1,0:T(8,128)(2,1)S(1)} %get-tuple-element.23), channel_id=1, source_target_pairs={{0,8},{4,12},{8,0},{12,4},{1,9},{5,13},{9,1},{13,5},{2,10},{6,14},... | collective-permute-start | bytes 442376 | tf_op jit(solution)/shard_map/ppermute | solution.py:131
  16.4 1.1 collective-permute-start
  17.5 1.6 collective-permute-start.3
  19.1 3.9 %collective-permute-start.4 = (bf16[96,768]{1,0:T(8,128)(2,1)S(1)}, bf16[96,768]{1,0:T(8,128)(2,1)S(1)}, u32[]{:S(2)}, u32[]{:S(2)}) collective-permute-start(bf16[96,768]{1,0:T(8,128)(2,1)S(1)} %get-tuple-element.21), channel_id=1, source_target_pairs={{0,131},{1,0},{2,1},{3,2},{128,3},{129,128},{130,129},{131,130},{4... | collective-permute-start | bytes 442376 | tf_op jit(solution)/shard_map/ppermute | solution.py:135
  23.0 0.9 pad_maximum_fusion.1
  23.9 1.6 collective-permute-done.3
  25.6 0.0 all-gather.3.cloned.1.call-update
  25.6 6.9 %all-to-all-start = ((bf16[8,2,96,1536]{3,2,1,0:T(8,128)(2,1)}), bf16[8,2,96,1536]{3,2,1,0:T(8,128)(2,1)}, u32[]{:S(2)}, u32[]{:S(2)}) async-start(bf16[8,2,96,1536]{3,2,1,0:T(8,128)(2,1)} %bitcast.53), calls=%async_computation | async-start | bytes 9437184 | tf_op jit(solution)/shard_map/all_to_all | solution.py:171
  32.5 0.1 reshape.41
  32.6 0.1 constant_dynamic-slice_fusion
  32.7 0.1 copy.18
  32.8 0.1 reshape.45
  32.9 0.1 dynamic-slice_bitcast_fusion
  33.0 0.7 bitcast_dynamic-update-slice_fusion.6
  33.7 3.0 %collective-permute-start.5 = (bf16[96,768]{1,0:T(8,128)(2,1)S(1)}, bf16[96,768]{1,0:T(8,128)(2,1)S(1)}, u32[]{:S(2)}, u32[]{:S(2)}) collective-permute-start(bf16[96,768]{1,0:T(8,128)(2,1)S(1)} %collective-permute-done.4), channel_id=1, source_target_pairs={{0,131},{1,0},{2,1},{3,2},{128,3},{129,128},{130,129},{131,130},{4... | collective-permute-start | bytes 442376 | tf_op jit(solution)/shard_map/ppermute | solution.py:135
  36.6 0.7 bitcast_dynamic-update-slice_fusion.5
  37.3 3.7 %collective-permute-done.5 = bf16[96,768]{1,0:T(8,128)(2,1)S(1)} collective-permute-done((bf16[96,768]{1,0:T(8,128)(2,1)S(1)}, bf16[96,768]{1,0:T(8,128)(2,1)S(1)}, u32[]{:S(2)}, u32[]{:S(2)}) %collective-permute-start.5) | collective-permute-done | bytes 147488 | tf_op jit(solution)/shard_map/ppermute | solution.py:135
  41.0 3.5 %collective-permute-start.6 = (bf16[96,768]{1,0:T(8,128)(2,1)S(1)}, bf16[96,768]{1,0:T(8,128)(2,1)S(1)}, u32[]{:S(2)}, u32[]{:S(2)}) collective-permute-start(bf16[96,768]{1,0:T(8,128)(2,1)S(1)} %collective-permute-done.5), channel_id=1, source_target_pairs={{0,131},{1,0},{2,1},{3,2},{128,3},{129,128},{130,129},{131,130},{4... | collective-permute-start | bytes 442376 | tf_op jit(solution)/shard_map/ppermute | solution.py:135
  44.5 0.7 bitcast_dynamic-update-slice_fusion.4
  45.2 5.3 %collective-permute-done.6 = bf16[96,768]{1,0:T(8,128)(2,1)S(1)} collective-permute-done((bf16[96,768]{1,0:T(8,128)(2,1)S(1)}, bf16[96,768]{1,0:T(8,128)(2,1)S(1)}, u32[]{:S(2)}, u32[]{:S(2)}) %collective-permute-start.6) | collective-permute-done | bytes 147488 | tf_op jit(solution)/shard_map/ppermute | solution.py:135
  50.4 3.5 %collective-permute-start.10 = (bf16[48,768]{1,0:T(8,128)(2,1)S(1)}, bf16[48,768]{1,0:T(8,128)(2,1)S(1)}, u32[]{:S(2)}, u32[]{:S(2)}) collective-permute-start(bf16[48,768]{1,0:T(8,128)(2,1)S(1)} %slice.27), channel_id=1, source_target_pairs={{0,131},{1,0},{2,1},{3,2},{128,3},{129,128},{130,129},{131,130},{4... | collective-permute-start | bytes 221192 | tf_op jit(solution)/shard_map/ppermute | solution.py:135
  54.0 0.1 collective-permute-start.9
  54.1 0.7 bitcast_dynamic-update-slice_fusion.3
  54.7 2.1 %collective-permute-done.10 = bf16[48,768]{1,0:T(8,128)(2,1)S(1)} collective-permute-done((bf16[48,768]{1,0:T(8,128)(2,1)S(1)}, bf16[48,768]{1,0:T(8,128)(2,1)S(1)}, u32[]{:S(2)}, u32[]{:S(2)}) %collective-permute-start.10) | collective-permute-done | bytes 73760 | tf_op jit(solution)/shard_map/ppermute | solution.py:135
  56.8 3.6 %collective-permute-done.9 = bf16[48,768]{1,0:T(8,128)(2,1)S(1)} collective-permute-done((bf16[48,768]{1,0:T(8,128)(2,1)S(1)}, bf16[48,768]{1,0:T(8,128)(2,1)S(1)}, u32[]{:S(2)}, u32[]{:S(2)}) %collective-permute-start.9) | collective-permute-done | bytes 73760 | tf_op jit(solution)/shard_map/ppermute | solution.py:135
  60.4 0.7 fusion
  61.1 0.7 bitcast_dynamic-update-slice_fusion.2
  61.8 0.7 bitcast_dynamic-update-slice_fusion.1
  62.4 0.7 bitcast_dynamic-update-slice_fusion.refs_0_
  63.1 0.5 collective-permute-start.11
  63.6 2.2 %collective-permute-start.12 = (bf16[8,96,768]{2,1,0:T(8,128)(2,1)}, bf16[8,96,768]{2,1,0:T(8,128)(2,1)S(1)}, u32[]{:S(2)}, u32[]{:S(2)}) collective-permute-start(bf16[8,96,768]{2,1,0:T(8,128)(2,1)} %bitcast_dynamic-update-slice_fusion.refs_0_), channel_id=1, source_target_pairs={{0,12},{4,0},{8,4},{12,8},{1,13},{5,1},{9,5},{13,9},{2,14},{6,2},{... | collective-permute-start | bytes 3538952 | tf_op jit(solution)/shard_map/ppermute | solution.py:131
  65.8 0.1 pad_add_fusion.pos_ref
  65.9 0.1 sub.62
  66.0 0.1 sub.63
  66.0 0.1 sub.59
  66.1 0.6 gather_fusion
  66.7 0.2 sub.71
  66.9 0.1 sub.67
  67.0 0.1 sub.68
  67.0 0.2 broadcast_subtract_fusion.refs_4_.refs_1_
  67.3 0.1 broadcast_subtract_fusion.1.refs_5_.refs_2_
  67.3 19.7 %all-to-all-done.x_ref = bf16[8,2,96,1536]{3,2,1,0:T(8,128)(2,1)} async-done(((bf16[8,2,96,1536]{3,2,1,0:T(8,128)(2,1)}), bf16[8,2,96,1536]{3,2,1,0:T(8,128)(2,1)}, u32[]{:S(2)}, u32[]{:S(2)}) %all-to-all-start) | async-done | bytes 4718624 | tf_op jit(solution)/shard_map/all_to_all | solution.py:171
  87.1 7.7 %combine.1.x_ref = bf16[2,8,96,1536]{3,2,1,0:T(8,128)(2,1)S(1)} custom-call(bf16[8,2,96,1536]{3,2,1,0:T(8,128)(2,1)} %all-to-all-done.x_ref), custom_call_target="tpu_custom_call" | custom-call | flops 4800000000 | bytes 9437184 | tf_op jit(solution)/shard_map/combine/pallas_call | solution.py:37
  94.8 0.0 copy-start.6
  94.8 2.2 %copy-done.6 = bf16[2,8,96,1536]{3,2,1,0:T(8,128)(2,1)} copy-done((bf16[2,8,96,1536]{3,2,1,0:T(8,128)(2,1)}, bf16[2,8,96,1536]{3,2,1,0:T(8,128)(2,1)S(1)}, u32[]{:S(2)}) %copy-start.6) | copy-done | bytes 4718616
  97.0 0.0 all-gather.3.cloned.1.call-done
  97.0 10.3 %contract_a.1 = bf16[8,2,96,768]{3,2,1,0:T(8,128)(2,1)S(1)} custom-call(s32[2]{0:T(128)S(1)} %pad_add_fusion.pos_ref, bf16[2,8,96,1536]{3,2,1,0:T(8,128)(2,1)} %copy-done.6, bf16[8,4,96,768]{3,2,1,0:T(8,128)(2,1)} %bitcast.63, f32[2,8,96,1]{3,2,1,0:T(8,128)S(1)} %broadcast_subtract_fusion.refs_4_.refs_1_, ...), custom_call_target="tpu_custom_call" | custom-call | flops 3623878656 | bytes 9437184 | tf_op jit(solution)/shard_map/contract_a/pallas_call | solution.py:73
  107.4 1.4 copy-done.1
  108.8 4.4 %all-to-all-start.2 = ((bf16[8,2,96,768]{3,2,1,0:T(8,128)(2,1)}), bf16[8,2,96,768]{3,2,1,0:T(8,128)(2,1)S(1)}, u32[]{:S(2)}, u32[]{:S(2)}) async-start(bf16[8,2,96,768]{3,2,1,0:T(8,128)(2,1)} %copy-done.1), calls=%async_computation.2 | async-start | bytes 4718592 | tf_op jit(solution)/shard_map/all_to_all | solution.py:185
  113.2 1.2 slice.23
  114.4 0.1 collective-permute-start.14
  114.4 0.2 copy-done.3
  114.7 1.4 collective-permute-start.13
  116.1 13.3 %collective-permute-done.14 = bf16[4,96,768]{2,1,0:T(8,128)(2,1)S(1)} collective-permute-done((bf16[4,96,768]{2,1,0:T(8,128)(2,1)S(1)}, bf16[4,96,768]{2,1,0:T(8,128)(2,1)S(1)}, u32[]{:S(2)}, u32[]{:S(2)}) %collective-permute-start.14) | collective-permute-done | bytes 589856 | tf_op jit(solution)/shard_map/ppermute | solution.py:131
  129.3 1.4 collective-permute-done.13
  130.7 0.1 pad_maximum_fusion.refs_2_
  130.8 9.4 %contract_b.1 = bf16[8,2,96,768]{3,2,1,0:T(8,128)(2,1)} custom-call(s32[2]{0:T(128)S(1)} %pad_add_fusion.pos_ref, bf16[2,8,96,1536]{3,2,1,0:T(8,128)(2,1)} %copy-done.6, bf16[8,96,768]{2,1,0:T(8,128)(2,1)} %bitcast_dynamic-update-slice_fusion.refs_0_, bf16[8,96,768]{2,1,0:T(8,128)(2,1)S(1)} %copy-done.5, bf16[8,96,768]{2,1,0:T(8,128)(2,1)S(1)} %pad_maximum_fusion.refs_2_, ...), custom_call_target="tpu_custom_call" | custom-call | flops 3623878656 | bytes 9437184 | tf_op jit(solution)/shard_map/contract_b/pallas_call | solution.py:73
  140.2 2.1 %all-to-all-done.2.v_ref = bf16[8,2,96,768]{3,2,1,0:T(8,128)(2,1)S(1)} async-done(((bf16[8,2,96,768]{3,2,1,0:T(8,128)(2,1)}), bf16[8,2,96,768]{3,2,1,0:T(8,128)(2,1)S(1)}, u32[]{:S(2)}, u32[]{:S(2)}) %all-to-all-start.2) | async-done | bytes 2359328 | tf_op jit(solution)/shard_map/all_to_all | solution.py:185
  142.3 5.1 %all-to-all-start.1 = ((bf16[8,2,96,768]{3,2,1,0:T(8,128)(2,1)}), bf16[8,2,96,768]{3,2,1,0:T(8,128)(2,1)}, u32[]{:S(2)}, u32[]{:S(2)}) async-start(bf16[8,2,96,768]{3,2,1,0:T(8,128)(2,1)} %contract_b.1), calls=%async_computation.1 | async-start | bytes 4718592 | tf_op jit(solution)/shard_map/all_to_all | solution.py:185
  147.4 2.0 %merge_a.1.refs_0_ = bf16[2,8,96,1536]{3,2,1,0:T(8,128)(2,1)} custom-call(bf16[8,2,96,768]{3,2,1,0:T(8,128)(2,1)S(1)} %all-to-all-done.2.v_ref), custom_call_target="tpu_custom_call" | custom-call | tf_op jit(solution)/shard_map/merge_a/pallas_call | solution.py:117
  149.5 27.2 %all-to-all-done.1.v_ref = bf16[8,2,96,768]{3,2,1,0:T(8,128)(2,1)} async-done(((bf16[8,2,96,768]{3,2,1,0:T(8,128)(2,1)}), bf16[8,2,96,768]{3,2,1,0:T(8,128)(2,1)}, u32[]{:S(2)}, u32[]{:S(2)}) %all-to-all-start.1) | async-done | bytes 2359328 | tf_op jit(solution)/shard_map/all_to_all | solution.py:185
  176.7 3.9 %merge_b.1 = bf16[2,8,96,1536]{3,2,1,0:T(8,128)(2,1)} custom-call(bf16[8,2,96,768]{3,2,1,0:T(8,128)(2,1)} %all-to-all-done.1.v_ref, bf16[2,8,96,1536]{3,2,1,0:T(8,128)(2,1)} %merge_a.1.refs_0_), custom_call_target="tpu_custom_call", output_to_operand_aliasing={{}: (1, {})} | custom-call | tf_op jit(solution)/shard_map/merge_b/pallas_call | solution.py:117
  (40 shorter events, 0.2 us)
Async XLA Ops:
  6.5 26.3 %copy-start = (f32[16,96]{1,0:T(8,128)S(1)}, f32[16,96]{1,0:T(8,128)}, u32[]{:S(2)}) copy-start(f32[16,96]{1,0:T(8,128)} %param.10) | copy-start | bytes 18436
  6.5 90.5 %all-gather.3.cloned.1.call-start = ((), (), s32[]{:S(2)}) async-start(), calls=%async_computation.3 | async-start | bytes 5308416 | tf_op jit(solution)/shard_map/all_gather | solution.py:153
  6.5 5.0 %copy-start.7 = (bf16[1,96,1536]{2,1,0:T(8,128)(2,1)S(1)}, bf16[1,96,1536]{2,1,0:T(8,128)(2,1)}, u32[]{:S(2)}) copy-start(bf16[1,96,1536]{2,1,0:T(8,128)(2,1)} %param.7) | copy-start | bytes 884740
  11.6 11.5 %collective-permute-start.2 = (bf16[96,768]{1,0:T(8,128)(2,1)S(1)}, bf16[96,768]{1,0:T(8,128)(2,1)S(1)}, u32[]{:S(2)}, u32[]{:S(2)}) collective-permute-start(bf16[96,768]{1,0:T(8,128)(2,1)S(1)} %get-tuple-element.23), channel_id=1, source_target_pairs={{0,4},{4,8},{8,12},{12,0},{1,5},{5,9},{9,13},{13,1},{2,6},{6,10},{... | collective-permute-start | bytes 442376 | tf_op jit(solution)/shard_map/ppermute | solution.py:131
  13.8 9.3 %collective-permute-start.1 = (bf16[96,768]{1,0:T(8,128)(2,1)S(1)}, bf16[96,768]{1,0:T(8,128)(2,1)S(1)}, u32[]{:S(2)}, u32[]{:S(2)}) collective-permute-start(bf16[96,768]{1,0:T(8,128)(2,1)S(1)} %get-tuple-element.23), channel_id=1, source_target_pairs={{0,8},{4,12},{8,0},{12,4},{1,9},{5,13},{9,1},{13,5},{2,10},{6,14},... | collective-permute-start | bytes 442376 | tf_op jit(solution)/shard_map/ppermute | solution.py:131
  16.4 6.7 %collective-permute-start = (bf16[96,768]{1,0:T(8,128)(2,1)S(1)}, bf16[96,768]{1,0:T(8,128)(2,1)S(1)}, u32[]{:S(2)}, u32[]{:S(2)}) collective-permute-start(bf16[96,768]{1,0:T(8,128)(2,1)S(1)} %get-tuple-element.23), channel_id=1, source_target_pairs={{0,12},{4,0},{8,4},{12,8},{1,13},{5,1},{9,5},{13,9},{2,14},{6,2},{... | collective-permute-start | bytes 442376 | tf_op jit(solution)/shard_map/ppermute | solution.py:131
  17.5 8.1 %collective-permute-start.3 = (bf16[96,768]{1,0:T(8,128)(2,1)S(1)}, bf16[96,768]{1,0:T(8,128)(2,1)S(1)}, u32[]{:S(2)}, u32[]{:S(2)}) collective-permute-start(bf16[96,768]{1,0:T(8,128)(2,1)S(1)} %get-tuple-element.21), channel_id=1, source_target_pairs={{0,1},{1,2},{2,3},{3,128},{128,129},{129,130},{130,131},{131,0},{4... | collective-permute-start | bytes 442376 | tf_op jit(solution)/shard_map/ppermute | solution.py:135
  19.1 6.5 %collective-permute-start.4 = (bf16[96,768]{1,0:T(8,128)(2,1)S(1)}, bf16[96,768]{1,0:T(8,128)(2,1)S(1)}, u32[]{:S(2)}, u32[]{:S(2)}) collective-permute-start(bf16[96,768]{1,0:T(8,128)(2,1)S(1)} %get-tuple-element.21), channel_id=1, source_target_pairs={{0,131},{1,0},{2,1},{3,2},{128,3},{129,128},{130,129},{131,130},{4... | collective-permute-start | bytes 442376 | tf_op jit(solution)/shard_map/ppermute | solution.py:135
  25.6 6.9 %copy-start.8 = (s32[1,16,16]{2,1,0:T(8,128)S(1)}, s32[1,16,16]{2,1,0:T(8,128)}, u32[]{:S(2)}) copy-start(s32[1,16,16]{2,1,0:T(8,128)} %param.11) | copy-start | bytes 3076
  25.6 7.3 %copy-start.9 = (f32[16,16]{1,0:T(8,128)S(1)}, f32[16,16]{1,0:T(8,128)}, u32[]{:S(2)}) copy-start(f32[16,16]{1,0:T(8,128)} %param.8) | copy-start | bytes 3076
  25.6 61.4 %all-to-all-start = ((bf16[8,2,96,1536]{3,2,1,0:T(8,128)(2,1)}), bf16[8,2,96,1536]{3,2,1,0:T(8,128)(2,1)}, u32[]{:S(2)}, u32[]{:S(2)}) async-start(bf16[8,2,96,1536]{3,2,1,0:T(8,128)(2,1)} %bitcast.53), calls=%async_computation | async-start | bytes 9437184 | tf_op jit(solution)/shard_map/all_to_all | solution.py:171
  33.7 7.3 %collective-permute-start.5 = (bf16[96,768]{1,0:T(8,128)(2,1)S(1)}, bf16[96,768]{1,0:T(8,128)(2,1)S(1)}, u32[]{:S(2)}, u32[]{:S(2)}) collective-permute-start(bf16[96,768]{1,0:T(8,128)(2,1)S(1)} %collective-permute-done.4), channel_id=1, source_target_pairs={{0,131},{1,0},{2,1},{3,2},{128,3},{129,128},{130,129},{131,130},{4... | collective-permute-start | bytes 442376 | tf_op jit(solution)/shard_map/ppermute | solution.py:135
  36.6 7.9 %collective-permute-start.7 = (bf16[96,768]{1,0:T(8,128)(2,1)S(1)}, bf16[96,768]{1,0:T(8,128)(2,1)S(1)}, u32[]{:S(2)}, u32[]{:S(2)}) collective-permute-start(bf16[96,768]{1,0:T(8,128)(2,1)S(1)} %collective-permute-done.3), channel_id=1, source_target_pairs={{0,1},{1,2},{2,3},{3,128},{128,129},{129,130},{130,131},{131,0},{4... | collective-permute-start | bytes 442376 | tf_op jit(solution)/shard_map/ppermute | solution.py:135
  41.0 9.5 %collective-permute-start.6 = (bf16[96,768]{1,0:T(8,128)(2,1)S(1)}, bf16[96,768]{1,0:T(8,128)(2,1)S(1)}, u32[]{:S(2)}, u32[]{:S(2)}) collective-permute-start(bf16[96,768]{1,0:T(8,128)(2,1)S(1)} %collective-permute-done.5), channel_id=1, source_target_pairs={{0,131},{1,0},{2,1},{3,2},{128,3},{129,128},{130,129},{131,130},{4... | collective-permute-start | bytes 442376 | tf_op jit(solution)/shard_map/ppermute | solution.py:135
  44.5 9.5 %collective-permute-start.8 = (bf16[96,768]{1,0:T(8,128)(2,1)S(1)}, bf16[96,768]{1,0:T(8,128)(2,1)S(1)}, u32[]{:S(2)}, u32[]{:S(2)}) collective-permute-start(bf16[96,768]{1,0:T(8,128)(2,1)S(1)} %collective-permute-done.7), channel_id=1, source_target_pairs={{0,1},{1,2},{2,3},{3,128},{128,129},{129,130},{130,131},{131,0},{4... | collective-permute-start | bytes 442376 | tf_op jit(solution)/shard_map/ppermute | solution.py:135
  45.2 21.7 %copy-start.10 = (f32[1,16]{1,0:T(1,128)S(1)}, f32[1,16]{1,0:T(1,128)}, u32[]{:S(2)}) copy-start(f32[1,16]{1,0:T(1,128)} %param.9) | copy-start | bytes 196
  50.4 6.4 %collective-permute-start.10 = (bf16[48,768]{1,0:T(8,128)(2,1)S(1)}, bf16[48,768]{1,0:T(8,128)(2,1)S(1)}, u32[]{:S(2)}, u32[]{:S(2)}) collective-permute-start(bf16[48,768]{1,0:T(8,128)(2,1)S(1)} %slice.27), channel_id=1, source_target_pairs={{0,131},{1,0},{2,1},{3,2},{128,3},{129,128},{130,129},{131,130},{4... | collective-permute-start | bytes 221192 | tf_op jit(solution)/shard_map/ppermute | solution.py:135
  54.0 6.4 %collective-permute-start.9 = (bf16[48,768]{1,0:T(8,128)(2,1)S(1)}, bf16[48,768]{1,0:T(8,128)(2,1)S(1)}, u32[]{:S(2)}, u32[]{:S(2)}) collective-permute-start(bf16[48,768]{1,0:T(8,128)(2,1)S(1)} %slice.26), channel_id=1, source_target_pairs={{0,1},{1,2},{2,3},{3,128},{128,129},{129,130},{130,131},{131,0},{4... | collective-permute-start | bytes 221192 | tf_op jit(solution)/shard_map/ppermute | solution.py:135
  63.1 33.9 %collective-permute-start.11 = (bf16[8,96,768]{2,1,0:T(8,128)(2,1)}, bf16[8,96,768]{2,1,0:T(8,128)(2,1)S(1)}, u32[]{:S(2)}, u32[]{:S(2)}) collective-permute-start(bf16[8,96,768]{2,1,0:T(8,128)(2,1)} %bitcast_dynamic-update-slice_fusion.refs_0_), channel_id=1, source_target_pairs={{0,4},{4,8},{8,12},{12,0},{1,5},{5,9},{9,13},{13,1},{2,6},{6,10},{... | collective-permute-start | bytes 3538952 | tf_op jit(solution)/shard_map/ppermute | solution.py:131
  63.6 33.4 %collective-permute-start.12 = (bf16[8,96,768]{2,1,0:T(8,128)(2,1)}, bf16[8,96,768]{2,1,0:T(8,128)(2,1)S(1)}, u32[]{:S(2)}, u32[]{:S(2)}) collective-permute-start(bf16[8,96,768]{2,1,0:T(8,128)(2,1)} %bitcast_dynamic-update-slice_fusion.refs_0_), channel_id=1, source_target_pairs={{0,12},{4,0},{8,4},{12,8},{1,13},{5,1},{9,5},{13,9},{2,14},{6,2},{... | collective-permute-start | bytes 3538952 | tf_op jit(solution)/shard_map/ppermute | solution.py:131
  94.8 2.2 %copy-start.6 = (bf16[2,8,96,1536]{3,2,1,0:T(8,128)(2,1)}, bf16[2,8,96,1536]{3,2,1,0:T(8,128)(2,1)S(1)}, u32[]{:S(2)}) copy-start(bf16[2,8,96,1536]{3,2,1,0:T(8,128)(2,1)S(1)} %combine.1.x_ref) | copy-start | bytes 14155780
  97.0 10.3 %copy-start.2 = (bf16[8,96,768]{2,1,0:T(8,128)(2,1)}, bf16[8,96,768]{2,1,0:T(8,128)(2,1)S(1)}, u32[]{:S(2)}) copy-start(bf16[8,96,768]{2,1,0:T(8,128)(2,1)S(1)} %collective-permute-done.11.refs_3_) | copy-start | bytes 3538948
  97.0 10.3 %copy-start.4 = (bf16[8,96,768]{2,1,0:T(8,128)(2,1)}, bf16[8,96,768]{2,1,0:T(8,128)(2,1)S(1)}, u32[]{:S(2)}) copy-start(bf16[8,96,768]{2,1,0:T(8,128)(2,1)S(1)} %collective-permute-done.12.refs_1_) | copy-start | bytes 3538948
  107.4 1.4 copy-start.1
  108.8 33.5 %all-to-all-start.2 = ((bf16[8,2,96,768]{3,2,1,0:T(8,128)(2,1)}), bf16[8,2,96,768]{3,2,1,0:T(8,128)(2,1)S(1)}, u32[]{:S(2)}, u32[]{:S(2)}) async-start(bf16[8,2,96,768]{3,2,1,0:T(8,128)(2,1)} %copy-done.1), calls=%async_computation.2 | async-start | bytes 4718592 | tf_op jit(solution)/shard_map/all_to_all | solution.py:185
  113.1 1.4 copy-start.3
  114.4 15.0 %collective-permute-start.14 = (bf16[4,96,768]{2,1,0:T(8,128)(2,1)S(1)}, bf16[4,96,768]{2,1,0:T(8,128)(2,1)S(1)}, u32[]{:S(2)}, u32[]{:S(2)}) collective-permute-start(bf16[4,96,768]{2,1,0:T(8,128)(2,1)S(1)} %slice.23), channel_id=1, source_target_pairs={{0,12},{4,0},{8,4},{12,8},{1,13},{5,1},{9,5},{13,9},{2,14},{6,2},{... | collective-permute-start | bytes 1769480 | tf_op jit(solution)/shard_map/ppermute | solution.py:131
  114.6 16.2 %copy-start.5 = (bf16[8,96,768]{2,1,0:T(8,128)(2,1)S(1)}, bf16[8,96,768]{2,1,0:T(8,128)(2,1)}, u32[]{:S(2)}) copy-start(bf16[8,96,768]{2,1,0:T(8,128)(2,1)} %copy-done.4) | copy-start | bytes 3538948
  114.7 16.1 %collective-permute-start.13 = (bf16[4,96,768]{2,1,0:T(8,128)(2,1)S(1)}, bf16[4,96,768]{2,1,0:T(8,128)(2,1)S(1)}, u32[]{:S(2)}, u32[]{:S(2)}) collective-permute-start(bf16[4,96,768]{2,1,0:T(8,128)(2,1)S(1)} %slice.22), channel_id=1, source_target_pairs={{0,4},{4,8},{8,12},{12,0},{1,5},{5,9},{9,13},{13,1},{2,6},{6,10},{... | collective-permute-start | bytes 1769480 | tf_op jit(solution)/shard_map/ppermute | solution.py:131
  142.3 34.4 %all-to-all-start.1 = ((bf16[8,2,96,768]{3,2,1,0:T(8,128)(2,1)}), bf16[8,2,96,768]{3,2,1,0:T(8,128)(2,1)}, u32[]{:S(2)}, u32[]{:S(2)}) async-start(bf16[8,2,96,768]{3,2,1,0:T(8,128)(2,1)} %contract_b.1), calls=%async_computation.1 | async-start | bytes 4718592 | tf_op jit(solution)/shard_map/all_to_all | solution.py:185
Sparse Core Ops, SparseCore 0:
  25.7 67.4 all-gather.2

commit v3 on v2

v3 whole, which is shorter than its diff:
```python
import jax
import jax.numpy as jnp
from jax import lax
from jax.experimental import pallas as pl
from jax.experimental.pallas import tpu as pltpu
from jax.sharding import Mesh, PartitionSpec as P

NO = 16
NV = 96
PAIRS = NO * NV
VS = 6
ROWS = VS * NO
VMEM = 48 << 20
RING = ("zh", "zl")
NA = 384


def combine(x, q, out):
    nb, sq, step = x.shape[1], NO * NO, 2

    def kernel(x_ref, *refs):
        o_ref, scr = refs[-2:]

        @pl.loop(0, step)
        def _(e):
            for a in range(VS):
                xa = x_ref[e, NO * a : NO * a + NO, :].astype(jnp.float32)
                for p in range(NO):
                    lo = a * sq + NO * p
                    scr[lo : lo + NO, 0:NV] = xa[:, NV * p : NV * p + NV]
            for a in range(VS):
                xa = x_ref[e, NO * a : NO * a + NO, :].astype(jnp.float32)
                swapped = jnp.concatenate(
                    [scr[pl.ds(a * sq + q, NO, stride=NO), :][:, :NV] for q in range(NO)], axis=1
                )
                o_ref[e, NO * a : NO * a + NO, :] = (2.0 * xa - swapped).astype(jnp.bfloat16)

    return pl.pallas_call(
        kernel,
        grid=(nb // step,),
        in_specs=[pl.BlockSpec((None, step, ROWS, PAIRS), lambda b: (q, b, 0, 0))]
        + [pl.BlockSpec(memory_space=pl.ANY)] * (out is not None),
        out_specs=pl.BlockSpec((step, None, ROWS, PAIRS), lambda b: (b, q, 0, 0)),
        out_shape=jax.ShapeDtypeStruct((nb, 2, ROWS, PAIRS), x.dtype),
        input_output_aliases={} if out is None else {1: 0},
        scratch_shapes=[pltpu.VMEM((VS * sq, 128), jnp.float32)],
        compiler_params=pltpu.CompilerParams(vmem_limit_bytes=62 << 20),
        cost_estimate=pl.CostEstimate(
            flops=nb * 300000000, bytes_accessed=2 * x.size, transcendentals=0
        ),
        name="combine",
    )(x, *([] if out is None else [out]))


def contract(comb, pos, pieces, place, rr, cc, lo, name):
    nb = comb.shape[0]
    width = NA if lo == 0 else PAIRS - NA
    nt = width if width % 256 else width // 2
    npc = len(pieces)

    def kernel(pos_ref, x_ref, *refs):
        p_refs, (r_ref, c_ref, o_ref, w_ref) = refs[:npc], refs[npc:]
        q, n = pl.program_id(0), pl.program_id(1)

        @pl.when(n == 0)
        def _():
            place(p_refs, w_ref, q, pos_ref[0], pos_ref[1])

        cols = pl.ds(pl.multiple_of(n * nt, nt), nt)
        x = x_ref[...].reshape(nb * ROWS, PAIRS)
        acc = jnp.dot(x, w_ref[:, cols], preferred_element_type=jnp.float32)
        for m in range(nb):
            gap = r_ref[m] + c_ref[m]
            o_ref[m] = (acc[ROWS * m : ROWS * m + ROWS] / gap).astype(jnp.bfloat16)

    vmem = pl.BlockSpec(memory_space=pltpu.VMEM)
    return pl.pallas_call(
        kernel,
        grid=(2, width // nt),
        in_specs=[
            pl.BlockSpec(memory_space=pltpu.SMEM),
            pl.BlockSpec((nb, None, ROWS, PAIRS), lambda q, n: (0, q, 0, 0)),
        ]
        + [vmem] * npc
        + [
            pl.BlockSpec((None, nb, ROWS, 1), lambda q, n: (q, 0, 0, 0)),
            pl.BlockSpec((None, nb, 1, nt), lambda q, n: (q, 0, 0, n)),
        ],
        out_specs=pl.BlockSpec((nb, None, ROWS, nt), lambda q, n: (0, q, 0, n)),
        out_shape=jax.ShapeDtypeStruct((nb, 2, ROWS, width), jnp.bfloat16),
        scratch_shapes=[pltpu.VMEM((PAIRS, width), jnp.bfloat16)],
        compiler_params=pltpu.CompilerParams(vmem_limit_bytes=VMEM),
        cost_estimate=pl.CostEstimate(
            flops=PAIRS * width, bytes_accessed=PAIRS, transcendentals=0
        ),
        name=name,
    )(pos, comb, *pieces, rr, cc[..., lo : lo + width])


def place_a(p_refs, w_ref, q, y, z):
    for s in range(8):
        src = lax.rem(z + s, 8)

        @pl.when(lax.div(src, 4) == q)
        def _():
            for e in range(4):
                k = lax.rem(y + e, 4) * 4 + lax.rem(src, 4)
                w_ref[pl.ds(pl.multiple_of(k * NV, NV), NV), :] = p_refs[s][e]


def place_b(p_refs, w_ref, q, y, z):
    for k in range(16):
        w_ref[k * NV : k * NV + NV, :] = p_refs[0][q * 4 + k % 4, k // 4]


def merge(part, lo, out, name):
    nb, width = part.shape[0], part.shape[-1]

    def kernel(v_ref, *refs):
        o_ref, sem = refs[-2:]
        copies = [
            pltpu.make_async_copy(
                v_ref.at[e, q], o_ref.at[q, e, :, lo : lo + width], sem.at[q * nb + e]
            )
            for q in range(2)
            for e in range(nb)
        ]
        for copy in copies:
            copy.start()
        for copy in copies:
            copy.wait()

    anywhere = pl.BlockSpec(memory_space=pl.ANY)
    return pl.pallas_call(
        kernel,
        in_specs=[anywhere] * (1 if out is None else 2),
        out_specs=anywhere,
        out_shape=jax.ShapeDtypeStruct((2, nb, ROWS, PAIRS), jnp.bfloat16),
        input_output_aliases={} if out is None else {1: 0},
        scratch_shapes=[pltpu.SemaphoreType.DMA((2 * nb,))],
        compiler_params=pltpu.CompilerParams(vmem_limit_bytes=VMEM),
        name=name,
    )(part, *([] if out is None else [out]))


def y_permute(v, s):
    return lax.ppermute(v, "y", [(i, (i + s) % 4) for i in range(4)])


def z_permute(v, s):
    return lax.ppermute(v, RING, [(i, (i + s) % 8) for i in range(8)])


def tie(*vs):
    return lax.optimization_barrier(vs)


def gather_w(own, blocks):
    a, b = own[:, :NA], own[:, NA:]
    rest = lax.all_gather(b, RING + ("y",), axis=0).reshape(8, 4, NV, PAIRS - NA)
    col = jnp.stack([a, y_permute(a, -1), y_permute(a, 2), y_permute(a, 1)])
    col, blocks = tie(col, blocks)
    up, down = [col], [col]
    for s in range(3):
        up.append(z_permute(up[-1], 1))
        down.append(z_permute(down[-1], -1))
    far = jnp.concatenate([z_permute(up[3][:2], 1), z_permute(down[3][2:], -1)])
    return [col, down[1], down[2], down[3], far, up[3], up[2], up[1]], [rest], blocks


def per_device(amps, wshard, occ, occj, virt, table):
    zh, x, c = lax.axis_index("zh"), lax.axis_index("x"), lax.axis_index("c")
    y, zl = lax.axis_index("y"), lax.axis_index("zl")
    pos = jnp.stack([y, zh * 4 + zl]).astype(jnp.int32)

    blocks = jnp.transpose(amps[0, 0], (0, 2, 1, 3)).reshape(2, 8, ROWS, PAIRS)
    comb = combine(blocks, 0, None)
    part_a, part_b, blocks = gather_w(wshard[0], blocks)
    comb = combine(blocks, 1, comb)
    comb = lax.all_to_all(comb, ("x", "c"), split_axis=0, concat_axis=0, tiled=True)

    va = lax.dynamic_slice(virt, (0, (y * 4 + zl) * VS), (NO, VS)).reshape(2, 8, VS)
    va = lax.dynamic_index_in_dim(va, x * 2 + c, 1, False)
    occ_i = lax.dynamic_slice(occ, (zh * 8, 0), (8, NO))
    rr = (occ_i[None, :, None, :] - va[:, None, :, None]).reshape(2, 8, ROWS, 1)
    kb = lax.dynamic_slice(table[0], (zh * 8, 0), (8, NO)).reshape(8, 2, 8)
    kb = lax.dynamic_index_in_dim(kb, x * 2 + c, 2, False).T
    cc = (occj[0][None, None, :, None] - virt[kb][:, :, None, :]).reshape(2, 8, 1, PAIRS)

    out = None
    for lo, part, place, name in ((0, part_a, place_a, "_a"), (NA, part_b, place_b, "_b")):
        res = contract(comb, pos, part, place, rr, cc, lo, "contract" + name)
        res, comb = tie(res, comb)
        res = lax.all_to_all(res, ("x", "c"), split_axis=0, concat_axis=0, tiled=True)
        out = merge(res, lo, out, "merge" + name)
    out = out.reshape(NO, VS, NO, PAIRS)
    return jnp.transpose(out, (0, 2, 1, 3))[None, None]


def solution(mesh):
    fine = Mesh(mesh.devices.reshape(2, 4, 2, 4, 4), ("zh", "x", "c", "y", "zl"))
    ka, vert = ("zh", "x", "c"), ("y", "zl")
    in_specs = (P(None, ka, None, None, vert, None), P(ka, vert, None), P(), P(), P(), P())
    out_specs = P(None, ka, None, None, vert, None)
    return jax.shard_map(
        per_device, mesh=fine, in_specs=in_specs, out_specs=out_specs, check_vma=False
    )
```

time: 188 us -> 176 us (0.936)
  local copies, waits for them, and re-layouts: 16.3 us -> 6.44 us
  waiting for transfers between devices: 80 us -> 85.3 us
  starting transfers between devices: 42.1 us -> 37.1 us
    ppermute x7 -> x3, waiting for transfers between devices: 14.7 us -> 0.01 us  [y_permute(): return lax.ppermute(v, 'y', [(i, (i + s) % 4) for i in range(4)])]
    all_to_all x1, waiting for transfers between devices: 19.7 us -> 8.04 us  [per_device(): lax.all_to_all(comb, ('x', 'c'), split_axis=0, concat_axis=0, tiled=True)]
    ppermute x8, waiting for transfers between devices: 16.3 us -> 27.3 us  [z_permute(): return lax.ppermute(v, RING, [(i, (i + s) % 8) for i in range(8)])]
    all_gather x1, waiting for transfers between devices: 0.02 us -> 10.5 us  [gather_w(): lax.all_gather(b, RING + ('y',), axis=0).reshape(8, 4, NV, PAIRS - NA)]
    all_to_all x2, waiting for transfers between devices: 29.3 us -> 39.4 us  [per_device(): lax.all_to_all(res, ('x', 'c'), split_axis=0, concat_axis=0, tiled=True)]
    unnamed x28 -> x12, local copies, waits for them, and re-layouts: 7.82 us -> 2.3 us
    reshape x1 -> x0, local copies, waits for them, and re-layouts: 4.98 us -> none  [per_device(): blocks = jnp.transpose(amps[0, 0], (0, 2, 1, 3)).reshape(2, 8, ROWS, PAIRS)]
    ppermute x7 -> x3, starting transfers between devices: 10.1 us -> 5.89 us  [y_permute(): return lax.ppermute(v, 'y', [(i, (i + s) % 4) for i in range(4)])]
  transfers between devices with their start and end apart: 19 -> 15, of which waited for: 10 -> 8; matrix products, arithmetic and copies ran while one was open for 5% -> 2% of each run, Pallas kernels for 10% -> 17%
where the time goes in v3:
time: 176 us; the launch traced here: 175 us
  waiting for transfers between devices  85.3 us (48%)
  starting transfers between devices  37.1 us (21%)
  Pallas kernels  31.7 us (18%)
  between operations  13.5 us (8%)
  local copies, waits for them, and re-layouts  6.44 us (4%)
    all_to_all x2, waiting for transfers between devices, per_device(): lax.all_to_all(res, ('x', 'c'), split_axis=0, concat_axis=0, tiled=True)  39.4 us
    ppermute x8, waiting for transfers between devices, z_permute(): return lax.ppermute(v, RING, [(i, (i + s) % 8) for i in range(8)])  27.3 us
    pallas_call x2, Pallas kernels, contract(): pl.pallas_call(kernel, grid=(2, width // nt), in_specs=[pl.BlockSpec(memo...  17.4 us
    ppermute x8, starting transfers between devices, z_permute(): return lax.ppermute(v, RING, [(i, (i + s) % 8) for i in range(8)])  16.2 us
    pallas_call x2, Pallas kernels, combine(): pl.pallas_call(kernel, grid=(nb // step,), in_specs=[pl.BlockSpec((None,...  11.2 us
    all_gather x1, waiting for transfers between devices, gather_w(): lax.all_gather(b, RING + ('y',), axis=0).reshape(8, 4, NV, PAIRS - NA)  10.5 us
    all_to_all x2, starting transfers between devices, per_device(): lax.all_to_all(res, ('x', 'c'), split_axis=0, concat_axis=0, tiled=True)  8.89 us
    all_to_all x1, waiting for transfers between devices, per_device(): lax.all_to_all(comb, ('x', 'c'), split_axis=0, concat_axis=0, tiled=True)  8.04 us
  transfers between devices with their start and end apart: 15, of which 8 were waited for; matrix products, arithmetic and copies ran while one was open for 2% of the time, Pallas kernels for 17%

profile of v3, /device:TPU:1, one launch (start us, length us, event | category | flops | bytes accessed | tf_op | source)
XLA Modules:
  0.0 175.4 jit_solution(4998185748918355970)
XLA Ops:
  6.5 0.0 copy-start
  6.5 0.0 all-gather.3.cloned.1.call-start
  6.5 1.6 slice.30
  8.2 0.0 all-gather.3.cloned.1.call-update
  8.2 0.9 slice_bitcast_fusion
  9.1 2.2 %collective-permute-start.2 = (bf16[96,384]{1,0:T(8,128)(2,1)S(1)}, bf16[96,384]{1,0:T(8,128)(2,1)S(1)}, u32[]{:S(2)}, u32[]{:S(2)}) collective-permute-start(bf16[96,384]{1,0:T(8,128)(2,1)S(1)} %get-tuple-element.16), channel_id=1, source_target_pairs={{0,4},{4,8},{8,12},{12,0},{1,5},{5,9},{9,13},{13,1},{2,6},{6,10},{... | collective-permute-start | bytes 221192 | tf_op jit(solution)/shard_map/ppermute | solution.py:147
  11.3 2.6 %collective-permute-start.1 = (bf16[96,384]{1,0:T(8,128)(2,1)S(1)}, bf16[96,384]{1,0:T(8,128)(2,1)S(1)}, u32[]{:S(2)}, u32[]{:S(2)}) collective-permute-start(bf16[96,384]{1,0:T(8,128)(2,1)S(1)} %get-tuple-element.16), channel_id=1, source_target_pairs={{0,8},{4,12},{8,0},{12,4},{1,9},{5,13},{9,1},{13,5},{2,10},{6,14},... | collective-permute-start | bytes 221192 | tf_op jit(solution)/shard_map/ppermute | solution.py:147
  13.9 1.1 collective-permute-start
  15.0 5.6 %combine.2.refs_0_ = bf16[8,2,96,1536]{3,2,1,0:T(8,128)(2,1)} custom-call(bf16[2,8,96,1536]{3,2,1,0:T(8,128)(2,1)} %bitcast.32), custom_call_target="tpu_custom_call" | custom-call | flops 2400000000 | bytes 4718592 | tf_op jit(solution)/shard_map/combine/pallas_call | solution.py:38
  20.6 0.0 collective-permute-done.2
  20.6 0.0 collective-permute-done.1
  20.6 0.0 collective-permute-done
  20.6 0.1 pad_maximum_fusion.refs_0_
  20.7 5.6 %combine.3 = bf16[8,2,96,1536]{3,2,1,0:T(8,128)(2,1)} custom-call(bf16[2,8,96,1536]{3,2,1,0:T(8,128)(2,1)} %bitcast.33, bf16[8,2,96,1536]{3,2,1,0:T(8,128)(2,1)} %combine.2.refs_0_), custom_call_target="tpu_custom_call", output_to_operand_aliasing={{}: (1, {})} | custom-call | flops 2400000000 | bytes 4718592 | tf_op jit(solution)/shard_map/combine/pallas_call | solution.py:38
  26.3 0.0 copy-start.3
  26.3 6.1 %all-to-all-start = ((bf16[8,2,96,1536]{3,2,1,0:T(8,128)(2,1)}), bf16[8,2,96,1536]{3,2,1,0:T(8,128)(2,1)}, u32[]{:S(2)}, u32[]{:S(2)}) async-start(bf16[8,2,96,1536]{3,2,1,0:T(8,128)(2,1)} %combine.3), calls=%async_computation | async-start | bytes 9437184 | tf_op jit(solution)/shard_map/all_to_all | solution.py:180
  32.4 0.0 copy-done
  32.4 0.1 dynamic-slice_bitcast_fusion
  32.5 0.1 sub.62
  32.6 0.1 sub.63
  32.7 5.6 %collective-permute-start.3 = (bf16[4,96,384]{2,1,0:T(8,128)(2,1)S(1)}, bf16[4,96,384]{2,1,0:T(8,128)(2,1)S(1)}, u32[]{:S(2)}, u32[]{:S(2)}) collective-permute-start(bf16[4,96,384]{2,1,0:T(8,128)(2,1)S(1)} %pad_maximum_fusion.refs_0_), channel_id=1, source_target_pairs={{0,131},{1,0},{2,1},{3,2},{128,3},{129,128},{130,129},{131,130},{4... | collective-permute-start | bytes 884744 | tf_op jit(solution)/shard_map/ppermute | solution.py:151
  38.3 0.0 collective-permute-start.6
  38.3 0.0 copy-done.3
  38.3 0.1 sub.59
  38.4 0.0 copy-done.4
  38.4 0.1 reshape.44
  38.5 0.1 constant_dynamic-slice_fusion
  38.6 0.1 copy.14
  38.6 9.1 %collective-permute-done.3.refs_1_ = bf16[4,96,384]{2,1,0:T(8,128)(2,1)S(1)} collective-permute-done((bf16[4,96,384]{2,1,0:T(8,128)(2,1)S(1)}, bf16[4,96,384]{2,1,0:T(8,128)(2,1)S(1)}, u32[]{:S(2)}, u32[]{:S(2)}) %collective-permute-start.3) | collective-permute-done | bytes 294944 | tf_op jit(solution)/shard_map/ppermute | solution.py:151
  47.8 3.5 %collective-permute-start.4 = (bf16[4,96,384]{2,1,0:T(8,128)(2,1)S(1)}, bf16[4,96,384]{2,1,0:T(8,128)(2,1)S(1)}, u32[]{:S(2)}, u32[]{:S(2)}) collective-permute-start(bf16[4,96,384]{2,1,0:T(8,128)(2,1)S(1)} %collective-permute-done.3.refs_1_), channel_id=1, source_target_pairs={{0,131},{1,0},{2,1},{3,2},{128,3},{129,128},{130,129},{131,130},{4... | collective-permute-start | bytes 884744 | tf_op jit(solution)/shard_map/ppermute | solution.py:151
  51.3 0.0 collective-permute-done.6.refs_7_
  51.3 0.0 collective-permute-start.7
  51.3 0.1 reshape.49
  51.4 0.6 gather_fusion
  52.0 0.2 sub.71
  52.1 0.0 copy-done.5
  52.2 0.1 sub.67
  52.2 0.1 sub.68
  52.3 5.1 %collective-permute-done.4.refs_2_ = bf16[4,96,384]{2,1,0:T(8,128)(2,1)S(1)} collective-permute-done((bf16[4,96,384]{2,1,0:T(8,128)(2,1)S(1)}, bf16[4,96,384]{2,1,0:T(8,128)(2,1)S(1)}, u32[]{:S(2)}, u32[]{:S(2)}) %collective-permute-start.4) | collective-permute-done | bytes 294944 | tf_op jit(solution)/shard_map/ppermute | solution.py:151
  57.4 3.4 %collective-permute-start.5 = (bf16[4,96,384]{2,1,0:T(8,128)(2,1)S(1)}, bf16[4,96,384]{2,1,0:T(8,128)(2,1)S(1)}, u32[]{:S(2)}, u32[]{:S(2)}) collective-permute-start(bf16[4,96,384]{2,1,0:T(8,128)(2,1)S(1)} %collective-permute-done.4.refs_2_), channel_id=1, source_target_pairs={{0,131},{1,0},{2,1},{3,2},{128,3},{129,128},{130,129},{131,130},{4... | collective-permute-start | bytes 884744 | tf_op jit(solution)/shard_map/ppermute | solution.py:151
  60.7 0.0 collective-permute-done.7.refs_6_
  60.7 0.0 collective-permute-start.8
  60.7 0.1 broadcast_subtract_fusion.1
  60.8 4.6 %collective-permute-done.5.refs_3_ = bf16[4,96,384]{2,1,0:T(8,128)(2,1)S(1)} collective-permute-done((bf16[4,96,384]{2,1,0:T(8,128)(2,1)S(1)}, bf16[4,96,384]{2,1,0:T(8,128)(2,1)S(1)}, u32[]{:S(2)}, u32[]{:S(2)}) %collective-permute-start.5) | collective-permute-done | bytes 294944 | tf_op jit(solution)/shard_map/ppermute | solution.py:151
  65.4 3.6 %collective-permute-start.10 = (bf16[2,96,384]{2,1,0:T(8,128)(2,1)S(1)}, bf16[2,96,384]{2,1,0:T(8,128)(2,1)S(1)}, u32[]{:S(2)}, u32[]{:S(2)}) collective-permute-start(bf16[2,96,384]{2,1,0:T(8,128)(2,1)S(1)} %slice.28), channel_id=1, source_target_pairs={{0,131},{1,0},{2,1},{3,2},{128,3},{129,128},{130,129},{131,130},{4... | collective-permute-start | bytes 442376 | tf_op jit(solution)/shard_map/ppermute | solution.py:151
  69.0 0.0 collective-permute-done.8.refs_5_
  69.0 0.1 collective-permute-start.9
  69.1 0.2 broadcast_subtract_fusion.refs_8_.refs_1_
  69.4 0.1 pad_add_fusion.pos_ref
  69.5 5.3 %collective-permute-done.10 = bf16[2,96,384]{2,1,0:T(8,128)(2,1)S(1)} collective-permute-done((bf16[2,96,384]{2,1,0:T(8,128)(2,1)S(1)}, bf16[2,96,384]{2,1,0:T(8,128)(2,1)S(1)}, u32[]{:S(2)}, u32[]{:S(2)}) %collective-permute-start.10) | collective-permute-done | bytes 147488 | tf_op jit(solution)/shard_map/ppermute | solution.py:151
  74.7 3.3 %collective-permute-done.9 = bf16[2,96,384]{2,1,0:T(8,128)(2,1)} collective-permute-done((bf16[2,96,384]{2,1,0:T(8,128)(2,1)S(1)}, bf16[2,96,384]{2,1,0:T(8,128)(2,1)}, u32[]{:S(2)}, u32[]{:S(2)}) %collective-permute-start.9) | collective-permute-done | bytes 147488 | tf_op jit(solution)/shard_map/ppermute | solution.py:151
  78.0 0.9 pad_maximum_fusion.1.refs_4_
  79.0 8.0 %all-to-all-done.x_ref = bf16[8,2,96,1536]{3,2,1,0:T(8,128)(2,1)} async-done(((bf16[8,2,96,1536]{3,2,1,0:T(8,128)(2,1)}), bf16[8,2,96,1536]{3,2,1,0:T(8,128)(2,1)}, u32[]{:S(2)}, u32[]{:S(2)}) %all-to-all-start) | async-done | bytes 4718624 | tf_op jit(solution)/shard_map/all_to_all | solution.py:180
  87.0 5.8 %contract_a.1 = bf16[8,2,96,384]{3,2,1,0:T(8,128)(2,1)} custom-call(s32[2]{0:T(128)S(1)} %pad_add_fusion.pos_ref, bf16[8,2,96,1536]{3,2,1,0:T(8,128)(2,1)} %all-to-all-done.x_ref, bf16[4,96,384]{2,1,0:T(8,128)(2,1)S(1)} %pad_maximum_fusion.refs_0_, bf16[4,96,384]{2,1,0:T(8,128)(2,1)S(1)} %collective-permute-done.3.refs_1_, ...), custom_call_target="tpu_custom_call" | custom-call | flops 589824 | bytes 1536 | tf_op jit(solution)/shard_map/contract_a/pallas_call | solution.py:77
  92.8 4.3 %all-to-all-start.2 = ((bf16[8,2,96,384]{3,2,1,0:T(8,128)(2,1)}), bf16[8,2,96,384]{3,2,1,0:T(8,128)(2,1)S(1)}, u32[]{:S(2)}, u32[]{:S(2)}) async-start(bf16[8,2,96,384]{3,2,1,0:T(8,128)(2,1)} %contract_a.1), calls=%async_computation.2 | async-start | bytes 2359296 | tf_op jit(solution)/shard_map/all_to_all | solution.py:194
  97.1 10.5 %all-gather.3.cloned.1.call-done = bf16[3072,1152]{1,0:T(8,128)(2,1)} async-done(((bf16[96,1152]{1,0:T(8,128)(2,1)}), bf16[3072,1152]{1,0:T(8,128)(2,1)}) %all-gather.3.cloned.1.call-update) | async-done | bytes 7077904 | tf_op jit(solution)/shard_map/all_gather | solution.py:160
  107.7 11.6 %contract_b.1 = bf16[8,2,96,1152]{3,2,1,0:T(8,128)(2,1)} custom-call(s32[2]{0:T(128)S(1)} %pad_add_fusion.pos_ref, bf16[8,2,96,1536]{3,2,1,0:T(8,128)(2,1)} %all-to-all-done.x_ref, bf16[8,4,96,1152]{3,2,1,0:T(8,128)(2,1)} %bitcast.34, f32[2,8,96,1]{3,2,1,0:T(8,128)S(1)} %broadcast_subtract_fusion.refs_8_.refs_1_, f32[2,8,1,1152]{3,2,1,0:T(1,128)S(1)} %slice.31.refs_2_), custom_call_target="tpu_custom_call" | custom-call | flops 1769472 | bytes 1536 | tf_op jit(solution)/shard_map/contract_b/pallas_call | solution.py:77
  119.3 0.0 all-to-all-done.2.v_ref
  119.3 1.0 copy-done.1
  120.3 4.6 %all-to-all-start.1 = ((bf16[8,2,96,1152]{3,2,1,0:T(8,128)(2,1)}), bf16[8,2,96,1152]{3,2,1,0:T(8,128)(2,1)S(1)}, u32[]{:S(2)}, u32[]{:S(2)}) async-start(bf16[8,2,96,1152]{3,2,1,0:T(8,128)(2,1)} %contract_b.1), calls=%async_computation.1 | async-start | bytes 7077888 | tf_op jit(solution)/shard_map/all_to_all | solution.py:194
  124.9 1.3 copy-done.2
  126.1 1.1 merge_a.1.refs_0_
  127.3 39.4 %all-to-all-done.1.v_ref = bf16[8,2,96,1152]{3,2,1,0:T(8,128)(2,1)S(1)} async-done(((bf16[8,2,96,1152]{3,2,1,0:T(8,128)(2,1)}), bf16[8,2,96,1152]{3,2,1,0:T(8,128)(2,1)S(1)}, u32[]{:S(2)}, u32[]{:S(2)}) %all-to-all-start.1) | async-done | bytes 3538976 | tf_op jit(solution)/shard_map/all_to_all | solution.py:194
  166.7 1.9 %merge_b.1 = bf16[2,8,96,1536]{3,2,1,0:T(8,128)(2,1)} custom-call(bf16[8,2,96,1152]{3,2,1,0:T(8,128)(2,1)S(1)} %all-to-all-done.1.v_ref, bf16[2,8,96,1536]{3,2,1,0:T(8,128)(2,1)} %merge_a.1.refs_0_), custom_call_target="tpu_custom_call", output_to_operand_aliasing={{}: (1, {})} | custom-call | tf_op jit(solution)/shard_map/merge_b/pallas_call | solution.py:134
  (15 shorter events, 0.1 us)
Async XLA Ops:
  6.5 25.9 %copy-start = (f32[16,96]{1,0:T(8,128)S(1)}, f32[16,96]{1,0:T(8,128)}, u32[]{:S(2)}) copy-start(f32[16,96]{1,0:T(8,128)} %param.10) | copy-start | bytes 18436
  6.5 101.1 %all-gather.3.cloned.1.call-start = ((), (), s32[]{:S(2)}) async-start(), calls=%async_computation.3 | async-start | bytes 7299072 | tf_op jit(solution)/shard_map/all_gather | solution.py:160
  9.1 11.5 %collective-permute-start.2 = (bf16[96,384]{1,0:T(8,128)(2,1)S(1)}, bf16[96,384]{1,0:T(8,128)(2,1)S(1)}, u32[]{:S(2)}, u32[]{:S(2)}) collective-permute-start(bf16[96,384]{1,0:T(8,128)(2,1)S(1)} %get-tuple-element.16), channel_id=1, source_target_pairs={{0,4},{4,8},{8,12},{12,0},{1,5},{5,9},{9,13},{13,1},{2,6},{6,10},{... | collective-permute-start | bytes 221192 | tf_op jit(solution)/shard_map/ppermute | solution.py:147
  11.3 9.3 %collective-permute-start.1 = (bf16[96,384]{1,0:T(8,128)(2,1)S(1)}, bf16[96,384]{1,0:T(8,128)(2,1)S(1)}, u32[]{:S(2)}, u32[]{:S(2)}) collective-permute-start(bf16[96,384]{1,0:T(8,128)(2,1)S(1)} %get-tuple-element.16), channel_id=1, source_target_pairs={{0,8},{4,12},{8,0},{12,4},{1,9},{5,13},{9,1},{13,5},{2,10},{6,14},... | collective-permute-start | bytes 221192 | tf_op jit(solution)/shard_map/ppermute | solution.py:147
  13.9 6.7 %collective-permute-start = (bf16[96,384]{1,0:T(8,128)(2,1)S(1)}, bf16[96,384]{1,0:T(8,128)(2,1)S(1)}, u32[]{:S(2)}, u32[]{:S(2)}) collective-permute-start(bf16[96,384]{1,0:T(8,128)(2,1)S(1)} %get-tuple-element.16), channel_id=1, source_target_pairs={{0,12},{4,0},{8,4},{12,8},{1,13},{5,1},{9,5},{13,9},{2,14},{6,2},{... | collective-permute-start | bytes 221192 | tf_op jit(solution)/shard_map/ppermute | solution.py:147
  26.3 12.0 %copy-start.3 = (f32[16,16]{1,0:T(8,128)S(1)}, f32[16,16]{1,0:T(8,128)}, u32[]{:S(2)}) copy-start(f32[16,16]{1,0:T(8,128)} %param.8) | copy-start | bytes 3076
  26.3 12.1 %copy-start.4 = (s32[1,16,16]{2,1,0:T(8,128)S(1)}, s32[1,16,16]{2,1,0:T(8,128)}, u32[]{:S(2)}) copy-start(s32[1,16,16]{2,1,0:T(8,128)} %param.11) | copy-start | bytes 3076
  26.3 25.8 %copy-start.5 = (f32[1,16]{1,0:T(1,128)S(1)}, f32[1,16]{1,0:T(1,128)}, u32[]{:S(2)}) copy-start(f32[1,16]{1,0:T(1,128)} %param.9) | copy-start | bytes 196
  26.3 60.7 %all-to-all-start = ((bf16[8,2,96,1536]{3,2,1,0:T(8,128)(2,1)}), bf16[8,2,96,1536]{3,2,1,0:T(8,128)(2,1)}, u32[]{:S(2)}, u32[]{:S(2)}) async-start(bf16[8,2,96,1536]{3,2,1,0:T(8,128)(2,1)} %combine.3), calls=%async_computation | async-start | bytes 9437184 | tf_op jit(solution)/shard_map/all_to_all | solution.py:180
  32.7 15.1 %collective-permute-start.3 = (bf16[4,96,384]{2,1,0:T(8,128)(2,1)S(1)}, bf16[4,96,384]{2,1,0:T(8,128)(2,1)S(1)}, u32[]{:S(2)}, u32[]{:S(2)}) collective-permute-start(bf16[4,96,384]{2,1,0:T(8,128)(2,1)S(1)} %pad_maximum_fusion.refs_0_), channel_id=1, source_target_pairs={{0,131},{1,0},{2,1},{3,2},{128,3},{129,128},{130,129},{131,130},{4... | collective-permute-start | bytes 884744 | tf_op jit(solution)/shard_map/ppermute | solution.py:151
  38.3 13.0 %collective-permute-start.6 = (bf16[4,96,384]{2,1,0:T(8,128)(2,1)S(1)}, bf16[4,96,384]{2,1,0:T(8,128)(2,1)S(1)}, u32[]{:S(2)}, u32[]{:S(2)}) collective-permute-start(bf16[4,96,384]{2,1,0:T(8,128)(2,1)S(1)} %pad_maximum_fusion.refs_0_), channel_id=1, source_target_pairs={{0,1},{1,2},{2,3},{3,128},{128,129},{129,130},{130,131},{131,0},{4... | collective-permute-start | bytes 884744 | tf_op jit(solution)/shard_map/ppermute | solution.py:151
  47.8 9.6 %collective-permute-start.4 = (bf16[4,96,384]{2,1,0:T(8,128)(2,1)S(1)}, bf16[4,96,384]{2,1,0:T(8,128)(2,1)S(1)}, u32[]{:S(2)}, u32[]{:S(2)}) collective-permute-start(bf16[4,96,384]{2,1,0:T(8,128)(2,1)S(1)} %collective-permute-done.3.refs_1_), channel_id=1, source_target_pairs={{0,131},{1,0},{2,1},{3,2},{128,3},{129,128},{130,129},{131,130},{4... | collective-permute-start | bytes 884744 | tf_op jit(solution)/shard_map/ppermute | solution.py:151
  51.3 9.5 %collective-permute-start.7 = (bf16[4,96,384]{2,1,0:T(8,128)(2,1)S(1)}, bf16[4,96,384]{2,1,0:T(8,128)(2,1)S(1)}, u32[]{:S(2)}, u32[]{:S(2)}) collective-permute-start(bf16[4,96,384]{2,1,0:T(8,128)(2,1)S(1)} %collective-permute-done.6.refs_7_), channel_id=1, source_target_pairs={{0,1},{1,2},{2,3},{3,128},{128,129},{129,130},{130,131},{131,0},{4... | collective-permute-start | bytes 884744 | tf_op jit(solution)/shard_map/ppermute | solution.py:151
  57.4 8.0 %collective-permute-start.5 = (bf16[4,96,384]{2,1,0:T(8,128)(2,1)S(1)}, bf16[4,96,384]{2,1,0:T(8,128)(2,1)S(1)}, u32[]{:S(2)}, u32[]{:S(2)}) collective-permute-start(bf16[4,96,384]{2,1,0:T(8,128)(2,1)S(1)} %collective-permute-done.4.refs_2_), channel_id=1, source_target_pairs={{0,131},{1,0},{2,1},{3,2},{128,3},{129,128},{130,129},{131,130},{4... | collective-permute-start | bytes 884744 | tf_op jit(solution)/shard_map/ppermute | solution.py:151
  60.7 8.3 %collective-permute-start.8 = (bf16[4,96,384]{2,1,0:T(8,128)(2,1)S(1)}, bf16[4,96,384]{2,1,0:T(8,128)(2,1)S(1)}, u32[]{:S(2)}, u32[]{:S(2)}) collective-permute-start(bf16[4,96,384]{2,1,0:T(8,128)(2,1)S(1)} %collective-permute-done.7.refs_6_), channel_id=1, source_target_pairs={{0,1},{1,2},{2,3},{3,128},{128,129},{129,130},{130,131},{131,0},{4... | collective-permute-start | bytes 884744 | tf_op jit(solution)/shard_map/ppermute | solution.py:151
  65.4 9.3 %collective-permute-start.10 = (bf16[2,96,384]{2,1,0:T(8,128)(2,1)S(1)}, bf16[2,96,384]{2,1,0:T(8,128)(2,1)S(1)}, u32[]{:S(2)}, u32[]{:S(2)}) collective-permute-start(bf16[2,96,384]{2,1,0:T(8,128)(2,1)S(1)} %slice.28), channel_id=1, source_target_pairs={{0,131},{1,0},{2,1},{3,2},{128,3},{129,128},{130,129},{131,130},{4... | collective-permute-start | bytes 442376 | tf_op jit(solution)/shard_map/ppermute | solution.py:151
  69.0 9.0 %collective-permute-start.9 = (bf16[2,96,384]{2,1,0:T(8,128)(2,1)S(1)}, bf16[2,96,384]{2,1,0:T(8,128)(2,1)}, u32[]{:S(2)}, u32[]{:S(2)}) collective-permute-start(bf16[2,96,384]{2,1,0:T(8,128)(2,1)S(1)} %slice.27), channel_id=1, source_target_pairs={{0,1},{1,2},{2,3},{3,128},{128,129},{129,130},{130,131},{131,0},{4... | collective-permute-start | bytes 442376 | tf_op jit(solution)/shard_map/ppermute | solution.py:151
  92.8 26.5 %all-to-all-start.2 = ((bf16[8,2,96,384]{3,2,1,0:T(8,128)(2,1)}), bf16[8,2,96,384]{3,2,1,0:T(8,128)(2,1)S(1)}, u32[]{:S(2)}, u32[]{:S(2)}) async-start(bf16[8,2,96,384]{3,2,1,0:T(8,128)(2,1)} %contract_a.1), calls=%async_computation.2 | async-start | bytes 2359296 | tf_op jit(solution)/shard_map/all_to_all | solution.py:194
  119.3 1.0 copy-start.1
  120.3 46.4 %all-to-all-start.1 = ((bf16[8,2,96,1152]{3,2,1,0:T(8,128)(2,1)}), bf16[8,2,96,1152]{3,2,1,0:T(8,128)(2,1)S(1)}, u32[]{:S(2)}, u32[]{:S(2)}) async-start(bf16[8,2,96,1152]{3,2,1,0:T(8,128)(2,1)} %contract_b.1), calls=%async_computation.1 | async-start | bytes 7077888 | tf_op jit(solution)/shard_map/all_to_all | solution.py:194
  124.9 1.3 copy-start.2
Sparse Core Ops, SparseCore 0:
  9.9 97.7 all-gather.2

commit v4 on v3

--- a/solution.py
+++ b/solution.py
@@ -10,7 +10,7 @@
 PAIRS = NO * NV
 VS = 6
 ROWS = VS * NO
-VMEM = 48 << 20
+VMEM = 62 << 20
 RING = ("zh", "zl")
 NA = 384
 
@@ -55,25 +55,34 @@
 def contract(comb, pos, pieces, place, rr, cc, lo, name):
     nb = comb.shape[0]
     width = NA if lo == 0 else PAIRS - NA
-    nt = width if width % 256 else width // 2
+    nt = width
     npc = len(pieces)
 
     def kernel(pos_ref, x_ref, *refs):
         p_refs, (r_ref, c_ref, o_ref, w_ref) = refs[:npc], refs[npc:]
         q, n = pl.program_id(0), pl.program_id(1)
 
-        @pl.when(n == 0)
-        def _():
-            place(p_refs, w_ref, q, pos_ref[0], pos_ref[1])
-
-        cols = pl.ds(pl.multiple_of(n * nt, nt), nt)
+        if place is None:
+            w = p_refs[0][...].reshape(PAIRS, width)
+        else:
+
+            @pl.when(n == 0)
+            def _():
+                place(p_refs, w_ref, q, pos_ref[0], pos_ref[1])
+
+            w = w_ref[:, pl.ds(pl.multiple_of(n * nt, nt), nt)]
+
+
         x = x_ref[...].reshape(nb * ROWS, PAIRS)
-        acc = jnp.dot(x, w_ref[:, cols], preferred_element_type=jnp.float32)
+        acc = jnp.dot(x, w, preferred_element_type=jnp.float32)
         for m in range(nb):
             gap = r_ref[m] + c_ref[m]
             o_ref[m] = (acc[ROWS * m : ROWS * m + ROWS] / gap).astype(jnp.bfloat16)
 
-    vmem = pl.BlockSpec(memory_space=pltpu.VMEM)
+    if place is None:
+        piece = pl.BlockSpec((4, 4, NV, width), lambda q, n: (0, q, 0, 0))
+    else:
+        piece = pl.BlockSpec(memory_space=pltpu.VMEM)
     return pl.pallas_call(
         kernel,
         grid=(2, width // nt),
@@ -81,15 +90,15 @@
             pl.BlockSpec(memory_space=pltpu.SMEM),
             pl.BlockSpec((nb, None, ROWS, PAIRS), lambda q, n: (0, q, 0, 0)),
         ]
-        + [vmem] * npc
+        + [piece] * npc
         + [
             pl.BlockSpec((None, nb, ROWS, 1), lambda q, n: (q, 0, 0, 0)),
             pl.BlockSpec((None, nb, 1, nt), lambda q, n: (q, 0, 0, n)),
         ],
         out_specs=pl.BlockSpec((nb, None, ROWS, nt), lambda q, n: (0, q, 0, n)),
         out_shape=jax.ShapeDtypeStruct((nb, 2, ROWS, width), jnp.bfloat16),
-        scratch_shapes=[pltpu.VMEM((PAIRS, width), jnp.bfloat16)],
-        compiler_params=pltpu.CompilerParams(vmem_limit_bytes=VMEM),
+        scratch_shapes=[pltpu.VMEM((PAIRS, width) if place else (16, 128), jnp.bfloat16)],
+        compiler_params=pltpu.CompilerParams(vmem_limit_bytes=48 << 20),
         cost_estimate=pl.CostEstimate(
             flops=PAIRS * width, bytes_accessed=PAIRS, transcendentals=0
         ),
@@ -106,11 +115,6 @@
             for e in range(4):
                 k = lax.rem(y + e, 4) * 4 + lax.rem(src, 4)
                 w_ref[pl.ds(pl.multiple_of(k * NV, NV), NV), :] = p_refs[s][e]
-
-
-def place_b(p_refs, w_ref, q, y, z):
-    for k in range(16):
-        w_ref[k * NV : k * NV + NV, :] = p_refs[0][q * 4 + k % 4, k // 4]
 
 
 def merge(part, lo, out, name):
@@ -133,12 +137,12 @@
     anywhere = pl.BlockSpec(memory_space=pl.ANY)
     return pl.pallas_call(
         kernel,
-        in_specs=[anywhere] * (1 if out is None else 2),
+        in_specs=[pl.BlockSpec(memory_space=pltpu.VMEM)] + [anywhere] * (out is not None),
         out_specs=anywhere,
         out_shape=jax.ShapeDtypeStruct((2, nb, ROWS, PAIRS), jnp.bfloat16),
         input_output_aliases={} if out is None else {1: 0},
         scratch_shapes=[pltpu.SemaphoreType.DMA((2 * nb,))],
-        compiler_params=pltpu.CompilerParams(vmem_limit_bytes=VMEM),
+        compiler_params=pltpu.CompilerParams(vmem_limit_bytes=48 << 20),
         name=name,
     )(part, *([] if out is None else [out]))
 
@@ -157,7 +161,7 @@
 
 def gather_w(own, blocks):
     a, b = own[:, :NA], own[:, NA:]
-    rest = lax.all_gather(b, RING + ("y",), axis=0).reshape(8, 4, NV, PAIRS - NA)
+    rest = lax.all_gather(b, ("y",) + RING, axis=0).reshape(4, 8, NV, PAIRS - NA)
     col = jnp.stack([a, y_permute(a, -1), y_permute(a, 2), y_permute(a, 1)])
     col, blocks = tie(col, blocks)
     up, down = [col], [col]
@@ -188,7 +192,7 @@
     cc = (occj[0][None, None, :, None] - virt[kb][:, :, None, :]).reshape(2, 8, 1, PAIRS)
 
     out = None
-    for lo, part, place, name in ((0, part_a, place_a, "_a"), (NA, part_b, place_b, "_b")):
+    for lo, part, place, name in ((0, part_a, place_a, "_a"), (NA, part_b, None, "_b")):
         res = contract(comb, pos, part, place, rr, cc, lo, "contract" + name)
         res, comb = tie(res, comb)
         res = lax.all_to_all(res, ("x", "c"), split_axis=0, concat_axis=0, tiled=True)

time: 176 us -> 175 us (level)
  transfers between devices with their start and end apart: 15 -> 15, of which waited for: 8 -> 8; matrix products, arithmetic and copies ran while one was open for 2% -> 2% of each run, Pallas kernels for 17% -> 16%
where the time goes in v4:
time: 175 us; the launch traced here: 174 us
  waiting for transfers between devices  85.3 us (49%)
  starting transfers between devices  37.2 us (21%)
  Pallas kernels  30.5 us (17%)
  between operations  13.5 us (8%)
  local copies, waits for them, and re-layouts  6.44 us (4%)
    all_to_all x2, waiting for transfers between devices, per_device(): lax.all_to_all(res, ('x', 'c'), split_axis=0, concat_axis=0, tiled=True)  39.4 us
    ppermute x8, waiting for transfers between devices, z_permute(): return lax.ppermute(v, RING, [(i, (i + s) % 8) for i in range(8)])  27.2 us
    pallas_call x2, Pallas kernels, contract(): pl.pallas_call(kernel, grid=(2, width // nt), in_specs=[pl.BlockSpec(memo...  16.2 us
    ppermute x8, starting transfers between devices, z_permute(): return lax.ppermute(v, RING, [(i, (i + s) % 8) for i in range(8)])  16.2 us
    pallas_call x2, Pallas kernels, combine(): pl.pallas_call(kernel, grid=(nb // step,), in_specs=[pl.BlockSpec((None,...  11.2 us
    all_gather x1, waiting for transfers between devices, gather_w(): lax.all_gather(b, ('y',) + RING, axis=0).reshape(4, 8, NV, PAIRS - NA)  10.5 us
    all_to_all x2, starting transfers between devices, per_device(): lax.all_to_all(res, ('x', 'c'), split_axis=0, concat_axis=0, tiled=True)  9.03 us
    all_to_all x1, waiting for transfers between devices, per_device(): lax.all_to_all(comb, ('x', 'c'), split_axis=0, concat_axis=0, tiled=True)  8.13 us
  transfers between devices with their start and end apart: 15, of which 8 were waited for; matrix products, arithmetic and copies ran while one was open for 2% of the time, Pallas kernels for 16%

profile of v4, /device:TPU:1, one launch (start us, length us, event | category | flops | bytes accessed | tf_op | source)
XLA Modules:
  0.0 174.4 jit_solution(17507778489929866695)
XLA Ops:
  6.5 0.0 copy-start
  6.5 0.0 all-gather.3.cloned.1.call-start
  6.5 1.6 slice.30
  8.2 0.0 all-gather.3.cloned.1.call-update
  8.2 0.9 slice_bitcast_fusion
  9.1 2.2 %collective-permute-start.2 = (bf16[96,384]{1,0:T(8,128)(2,1)S(1)}, bf16[96,384]{1,0:T(8,128)(2,1)S(1)}, u32[]{:S(2)}, u32[]{:S(2)}) collective-permute-start(bf16[96,384]{1,0:T(8,128)(2,1)S(1)} %get-tuple-element.16), channel_id=1, source_target_pairs={{0,4},{4,8},{8,12},{12,0},{1,5},{5,9},{9,13},{13,1},{2,6},{6,10},{... | collective-permute-start | bytes 221192 | tf_op jit(solution)/shard_map/ppermute | solution.py:151
  11.3 2.6 %collective-permute-start.1 = (bf16[96,384]{1,0:T(8,128)(2,1)S(1)}, bf16[96,384]{1,0:T(8,128)(2,1)S(1)}, u32[]{:S(2)}, u32[]{:S(2)}) collective-permute-start(bf16[96,384]{1,0:T(8,128)(2,1)S(1)} %get-tuple-element.16), channel_id=1, source_target_pairs={{0,8},{4,12},{8,0},{12,4},{1,9},{5,13},{9,1},{13,5},{2,10},{6,14},... | collective-permute-start | bytes 221192 | tf_op jit(solution)/shard_map/ppermute | solution.py:151
  13.9 1.1 collective-permute-start
  15.0 5.6 %combine.2.refs_0_ = bf16[8,2,96,1536]{3,2,1,0:T(8,128)(2,1)} custom-call(bf16[2,8,96,1536]{3,2,1,0:T(8,128)(2,1)} %bitcast.32), custom_call_target="tpu_custom_call" | custom-call | flops 2400000000 | bytes 4718592 | tf_op jit(solution)/shard_map/combine/pallas_call | solution.py:38
  20.6 0.0 collective-permute-done.2
  20.6 0.0 collective-permute-done.1
  20.6 0.0 collective-permute-done
  20.6 0.1 pad_maximum_fusion.refs_0_
  20.7 5.6 %combine.3 = bf16[8,2,96,1536]{3,2,1,0:T(8,128)(2,1)} custom-call(bf16[2,8,96,1536]{3,2,1,0:T(8,128)(2,1)} %bitcast.33, bf16[8,2,96,1536]{3,2,1,0:T(8,128)(2,1)} %combine.2.refs_0_), custom_call_target="tpu_custom_call", output_to_operand_aliasing={{}: (1, {})} | custom-call | flops 2400000000 | bytes 4718592 | tf_op jit(solution)/shard_map/combine/pallas_call | solution.py:38
  26.3 0.0 copy-start.3
  26.3 6.1 %all-to-all-start = ((bf16[8,2,96,1536]{3,2,1,0:T(8,128)(2,1)}), bf16[8,2,96,1536]{3,2,1,0:T(8,128)(2,1)}, u32[]{:S(2)}, u32[]{:S(2)}) async-start(bf16[8,2,96,1536]{3,2,1,0:T(8,128)(2,1)} %combine.3), calls=%async_computation | async-start | bytes 9437184 | tf_op jit(solution)/shard_map/all_to_all | solution.py:184
  32.4 0.0 copy-done
  32.4 0.1 dynamic-slice_bitcast_fusion
  32.5 0.1 sub.62
  32.6 0.1 sub.63
  32.7 5.6 %collective-permute-start.3 = (bf16[4,96,384]{2,1,0:T(8,128)(2,1)S(1)}, bf16[4,96,384]{2,1,0:T(8,128)(2,1)S(1)}, u32[]{:S(2)}, u32[]{:S(2)}) collective-permute-start(bf16[4,96,384]{2,1,0:T(8,128)(2,1)S(1)} %pad_maximum_fusion.refs_0_), channel_id=1, source_target_pairs={{0,131},{1,0},{2,1},{3,2},{128,3},{129,128},{130,129},{131,130},{4... | collective-permute-start | bytes 884744 | tf_op jit(solution)/shard_map/ppermute | solution.py:155
  38.3 0.0 collective-permute-start.6
  38.3 0.0 copy-done.3
  38.3 0.1 sub.59
  38.4 0.0 copy-done.4
  38.4 0.1 reshape.44
  38.5 0.1 constant_dynamic-slice_fusion
  38.6 0.1 copy.14
  38.6 9.1 %collective-permute-done.3.refs_1_ = bf16[4,96,384]{2,1,0:T(8,128)(2,1)S(1)} collective-permute-done((bf16[4,96,384]{2,1,0:T(8,128)(2,1)S(1)}, bf16[4,96,384]{2,1,0:T(8,128)(2,1)S(1)}, u32[]{:S(2)}, u32[]{:S(2)}) %collective-permute-start.3) | collective-permute-done | bytes 294944 | tf_op jit(solution)/shard_map/ppermute | solution.py:155
  47.8 3.5 %collective-permute-start.4 = (bf16[4,96,384]{2,1,0:T(8,128)(2,1)S(1)}, bf16[4,96,384]{2,1,0:T(8,128)(2,1)S(1)}, u32[]{:S(2)}, u32[]{:S(2)}) collective-permute-start(bf16[4,96,384]{2,1,0:T(8,128)(2,1)S(1)} %collective-permute-done.3.refs_1_), channel_id=1, source_target_pairs={{0,131},{1,0},{2,1},{3,2},{128,3},{129,128},{130,129},{131,130},{4... | collective-permute-start | bytes 884744 | tf_op jit(solution)/shard_map/ppermute | solution.py:155
  51.3 0.0 collective-permute-done.6.refs_7_
  51.3 0.0 collective-permute-start.7
  51.3 0.1 reshape.49
  51.4 0.6 gather_fusion
  52.0 0.2 sub.71
  52.1 0.0 copy-done.5
  52.2 0.1 sub.67
  52.2 0.1 sub.68
  52.3 5.1 %collective-permute-done.4.refs_2_ = bf16[4,96,384]{2,1,0:T(8,128)(2,1)S(1)} collective-permute-done((bf16[4,96,384]{2,1,0:T(8,128)(2,1)S(1)}, bf16[4,96,384]{2,1,0:T(8,128)(2,1)S(1)}, u32[]{:S(2)}, u32[]{:S(2)}) %collective-permute-start.4) | collective-permute-done | bytes 294944 | tf_op jit(solution)/shard_map/ppermute | solution.py:155
  57.4 3.3 %collective-permute-start.5 = (bf16[4,96,384]{2,1,0:T(8,128)(2,1)S(1)}, bf16[4,96,384]{2,1,0:T(8,128)(2,1)S(1)}, u32[]{:S(2)}, u32[]{:S(2)}) collective-permute-start(bf16[4,96,384]{2,1,0:T(8,128)(2,1)S(1)} %collective-permute-done.4.refs_2_), channel_id=1, source_target_pairs={{0,131},{1,0},{2,1},{3,2},{128,3},{129,128},{130,129},{131,130},{4... | collective-permute-start | bytes 884744 | tf_op jit(solution)/shard_map/ppermute | solution.py:155
  60.7 0.0 collective-permute-done.7.refs_6_
  60.7 0.0 collective-permute-start.8
  60.8 0.1 broadcast_subtract_fusion.1
  60.8 4.6 %collective-permute-done.5.refs_3_ = bf16[4,96,384]{2,1,0:T(8,128)(2,1)S(1)} collective-permute-done((bf16[4,96,384]{2,1,0:T(8,128)(2,1)S(1)}, bf16[4,96,384]{2,1,0:T(8,128)(2,1)S(1)}, u32[]{:S(2)}, u32[]{:S(2)}) %collective-permute-start.5) | collective-permute-done | bytes 294944 | tf_op jit(solution)/shard_map/ppermute | solution.py:155
  65.4 3.6 %collective-permute-start.10 = (bf16[2,96,384]{2,1,0:T(8,128)(2,1)S(1)}, bf16[2,96,384]{2,1,0:T(8,128)(2,1)S(1)}, u32[]{:S(2)}, u32[]{:S(2)}) collective-permute-start(bf16[2,96,384]{2,1,0:T(8,128)(2,1)S(1)} %slice.28), channel_id=1, source_target_pairs={{0,131},{1,0},{2,1},{3,2},{128,3},{129,128},{130,129},{131,130},{4... | collective-permute-start | bytes 442376 | tf_op jit(solution)/shard_map/ppermute | solution.py:155
  69.0 0.0 collective-permute-done.8.refs_5_
  69.0 0.1 collective-permute-start.9
  69.1 0.2 broadcast_subtract_fusion.refs_8_.refs_1_
  69.4 0.1 pad_add_fusion.pos_ref
  69.5 5.2 %collective-permute-done.10 = bf16[2,96,384]{2,1,0:T(8,128)(2,1)S(1)} collective-permute-done((bf16[2,96,384]{2,1,0:T(8,128)(2,1)S(1)}, bf16[2,96,384]{2,1,0:T(8,128)(2,1)S(1)}, u32[]{:S(2)}, u32[]{:S(2)}) %collective-permute-start.10) | collective-permute-done | bytes 147488 | tf_op jit(solution)/shard_map/ppermute | solution.py:155
  74.6 3.3 %collective-permute-done.9 = bf16[2,96,384]{2,1,0:T(8,128)(2,1)} collective-permute-done((bf16[2,96,384]{2,1,0:T(8,128)(2,1)S(1)}, bf16[2,96,384]{2,1,0:T(8,128)(2,1)}, u32[]{:S(2)}, u32[]{:S(2)}) %collective-permute-start.9) | collective-permute-done | bytes 147488 | tf_op jit(solution)/shard_map/ppermute | solution.py:155
  77.9 0.9 pad_maximum_fusion.1.refs_4_
  78.9 8.1 %all-to-all-done.x_ref = bf16[8,2,96,1536]{3,2,1,0:T(8,128)(2,1)} async-done(((bf16[8,2,96,1536]{3,2,1,0:T(8,128)(2,1)}), bf16[8,2,96,1536]{3,2,1,0:T(8,128)(2,1)}, u32[]{:S(2)}, u32[]{:S(2)}) %all-to-all-start) | async-done | bytes 4718624 | tf_op jit(solution)/shard_map/all_to_all | solution.py:184
  87.0 5.8 %contract_a.1 = bf16[8,2,96,384]{3,2,1,0:T(8,128)(2,1)} custom-call(s32[2]{0:T(128)S(1)} %pad_add_fusion.pos_ref, bf16[8,2,96,1536]{3,2,1,0:T(8,128)(2,1)} %all-to-all-done.x_ref, bf16[4,96,384]{2,1,0:T(8,128)(2,1)S(1)} %pad_maximum_fusion.refs_0_, bf16[4,96,384]{2,1,0:T(8,128)(2,1)S(1)} %collective-permute-done.3.refs_1_, ...), custom_call_target="tpu_custom_call" | custom-call | flops 589824 | bytes 1536 | tf_op jit(solution)/shard_map/contract_a/pallas_call | solution.py:86
  92.8 4.3 %all-to-all-start.2 = ((bf16[8,2,96,384]{3,2,1,0:T(8,128)(2,1)}), bf16[8,2,96,384]{3,2,1,0:T(8,128)(2,1)S(1)}, u32[]{:S(2)}, u32[]{:S(2)}) async-start(bf16[8,2,96,384]{3,2,1,0:T(8,128)(2,1)} %contract_a.1), calls=%async_computation.2 | async-start | bytes 2359296 | tf_op jit(solution)/shard_map/all_to_all | solution.py:198
  97.1 10.5 %all-gather.3.cloned.1.call-done = bf16[3072,1152]{1,0:T(8,128)(2,1)} async-done(((bf16[96,1152]{1,0:T(8,128)(2,1)}), bf16[3072,1152]{1,0:T(8,128)(2,1)}) %all-gather.3.cloned.1.call-update) | async-done | bytes 7077904 | tf_op jit(solution)/shard_map/all_gather | solution.py:164
  107.7 10.4 %contract_b.1 = bf16[8,2,96,1152]{3,2,1,0:T(8,128)(2,1)} custom-call(s32[2]{0:T(128)S(1)} %pad_add_fusion.pos_ref, bf16[8,2,96,1536]{3,2,1,0:T(8,128)(2,1)} %all-to-all-done.x_ref, bf16[4,8,96,1152]{3,2,1,0:T(8,128)(2,1)} %bitcast.34, f32[2,8,96,1]{3,2,1,0:T(8,128)S(1)} %broadcast_subtract_fusion.refs_8_.refs_1_, f32[2,8,1,1152]{3,2,1,0:T(1,128)S(1)} %slice.31.refs_2_), custom_call_target="tpu_custom_call" | custom-call | flops 1769472 | bytes 1536 | tf_op jit(solution)/shard_map/contract_b/pallas_call | solution.py:86
  118.1 0.0 all-to-all-done.2.v_ref
  118.1 1.0 copy-done.1
  119.1 4.7 %all-to-all-start.1 = ((bf16[8,2,96,1152]{3,2,1,0:T(8,128)(2,1)}), bf16[8,2,96,1152]{3,2,1,0:T(8,128)(2,1)S(1)}, u32[]{:S(2)}, u32[]{:S(2)}) async-start(bf16[8,2,96,1152]{3,2,1,0:T(8,128)(2,1)} %contract_b.1), calls=%async_computation.1 | async-start | bytes 7077888 | tf_op jit(solution)/shard_map/all_to_all | solution.py:198
  123.8 1.3 copy-done.2
  125.1 1.1 merge_a.1.refs_0_
  126.2 39.4 %all-to-all-done.1.v_ref = bf16[8,2,96,1152]{3,2,1,0:T(8,128)(2,1)S(1)} async-done(((bf16[8,2,96,1152]{3,2,1,0:T(8,128)(2,1)}), bf16[8,2,96,1152]{3,2,1,0:T(8,128)(2,1)S(1)}, u32[]{:S(2)}, u32[]{:S(2)}) %all-to-all-start.1) | async-done | bytes 3538976 | tf_op jit(solution)/shard_map/all_to_all | solution.py:198
  165.6 1.9 %merge_b.1 = bf16[2,8,96,1536]{3,2,1,0:T(8,128)(2,1)} custom-call(bf16[8,2,96,1152]{3,2,1,0:T(8,128)(2,1)S(1)} %all-to-all-done.1.v_ref, bf16[2,8,96,1536]{3,2,1,0:T(8,128)(2,1)} %merge_a.1.refs_0_), custom_call_target="tpu_custom_call", output_to_operand_aliasing={{}: (1, {})} | custom-call | tf_op jit(solution)/shard_map/merge_b/pallas_call | solution.py:138
  (15 shorter events, 0.1 us)
Async XLA Ops:
  6.5 25.9 %copy-start = (f32[16,96]{1,0:T(8,128)S(1)}, f32[16,96]{1,0:T(8,128)}, u32[]{:S(2)}) copy-start(f32[16,96]{1,0:T(8,128)} %param.10) | copy-start | bytes 18436
  6.5 101.1 %all-gather.3.cloned.1.call-start = ((), (), s32[]{:S(2)}) async-start(), calls=%async_computation.3 | async-start | bytes 7299072 | tf_op jit(solution)/shard_map/all_gather | solution.py:164
  9.1 11.5 %collective-permute-start.2 = (bf16[96,384]{1,0:T(8,128)(2,1)S(1)}, bf16[96,384]{1,0:T(8,128)(2,1)S(1)}, u32[]{:S(2)}, u32[]{:S(2)}) collective-permute-start(bf16[96,384]{1,0:T(8,128)(2,1)S(1)} %get-tuple-element.16), channel_id=1, source_target_pairs={{0,4},{4,8},{8,12},{12,0},{1,5},{5,9},{9,13},{13,1},{2,6},{6,10},{... | collective-permute-start | bytes 221192 | tf_op jit(solution)/shard_map/ppermute | solution.py:151
  11.3 9.3 %collective-permute-start.1 = (bf16[96,384]{1,0:T(8,128)(2,1)S(1)}, bf16[96,384]{1,0:T(8,128)(2,1)S(1)}, u32[]{:S(2)}, u32[]{:S(2)}) collective-permute-start(bf16[96,384]{1,0:T(8,128)(2,1)S(1)} %get-tuple-element.16), channel_id=1, source_target_pairs={{0,8},{4,12},{8,0},{12,4},{1,9},{5,13},{9,1},{13,5},{2,10},{6,14},... | collective-permute-start | bytes 221192 | tf_op jit(solution)/shard_map/ppermute | solution.py:151
  13.9 6.7 %collective-permute-start = (bf16[96,384]{1,0:T(8,128)(2,1)S(1)}, bf16[96,384]{1,0:T(8,128)(2,1)S(1)}, u32[]{:S(2)}, u32[]{:S(2)}) collective-permute-start(bf16[96,384]{1,0:T(8,128)(2,1)S(1)} %get-tuple-element.16), channel_id=1, source_target_pairs={{0,12},{4,0},{8,4},{12,8},{1,13},{5,1},{9,5},{13,9},{2,14},{6,2},{... | collective-permute-start | bytes 221192 | tf_op jit(solution)/shard_map/ppermute | solution.py:151
  26.3 12.0 %copy-start.3 = (f32[16,16]{1,0:T(8,128)S(1)}, f32[16,16]{1,0:T(8,128)}, u32[]{:S(2)}) copy-start(f32[16,16]{1,0:T(8,128)} %param.8) | copy-start | bytes 3076
  26.3 12.1 %copy-start.4 = (s32[1,16,16]{2,1,0:T(8,128)S(1)}, s32[1,16,16]{2,1,0:T(8,128)}, u32[]{:S(2)}) copy-start(s32[1,16,16]{2,1,0:T(8,128)} %param.11) | copy-start | bytes 3076
  26.3 25.8 %copy-start.5 = (f32[1,16]{1,0:T(1,128)S(1)}, f32[1,16]{1,0:T(1,128)}, u32[]{:S(2)}) copy-start(f32[1,16]{1,0:T(1,128)} %param.9) | copy-start | bytes 196
  26.3 60.7 %all-to-all-start = ((bf16[8,2,96,1536]{3,2,1,0:T(8,128)(2,1)}), bf16[8,2,96,1536]{3,2,1,0:T(8,128)(2,1)}, u32[]{:S(2)}, u32[]{:S(2)}) async-start(bf16[8,2,96,1536]{3,2,1,0:T(8,128)(2,1)} %combine.3), calls=%async_computation | async-start | bytes 9437184 | tf_op jit(solution)/shard_map/all_to_all | solution.py:184
  32.7 15.1 %collective-permute-start.3 = (bf16[4,96,384]{2,1,0:T(8,128)(2,1)S(1)}, bf16[4,96,384]{2,1,0:T(8,128)(2,1)S(1)}, u32[]{:S(2)}, u32[]{:S(2)}) collective-permute-start(bf16[4,96,384]{2,1,0:T(8,128)(2,1)S(1)} %pad_maximum_fusion.refs_0_), channel_id=1, source_target_pairs={{0,131},{1,0},{2,1},{3,2},{128,3},{129,128},{130,129},{131,130},{4... | collective-permute-start | bytes 884744 | tf_op jit(solution)/shard_map/ppermute | solution.py:155
  38.3 13.0 %collective-permute-start.6 = (bf16[4,96,384]{2,1,0:T(8,128)(2,1)S(1)}, bf16[4,96,384]{2,1,0:T(8,128)(2,1)S(1)}, u32[]{:S(2)}, u32[]{:S(2)}) collective-permute-start(bf16[4,96,384]{2,1,0:T(8,128)(2,1)S(1)} %pad_maximum_fusion.refs_0_), channel_id=1, source_target_pairs={{0,1},{1,2},{2,3},{3,128},{128,129},{129,130},{130,131},{131,0},{4... | collective-permute-start | bytes 884744 | tf_op jit(solution)/shard_map/ppermute | solution.py:155
  47.8 9.6 %collective-permute-start.4 = (bf16[4,96,384]{2,1,0:T(8,128)(2,1)S(1)}, bf16[4,96,384]{2,1,0:T(8,128)(2,1)S(1)}, u32[]{:S(2)}, u32[]{:S(2)}) collective-permute-start(bf16[4,96,384]{2,1,0:T(8,128)(2,1)S(1)} %collective-permute-done.3.refs_1_), channel_id=1, source_target_pairs={{0,131},{1,0},{2,1},{3,2},{128,3},{129,128},{130,129},{131,130},{4... | collective-permute-start | bytes 884744 | tf_op jit(solution)/shard_map/ppermute | solution.py:155
  51.3 9.5 %collective-permute-start.7 = (bf16[4,96,384]{2,1,0:T(8,128)(2,1)S(1)}, bf16[4,96,384]{2,1,0:T(8,128)(2,1)S(1)}, u32[]{:S(2)}, u32[]{:S(2)}) collective-permute-start(bf16[4,96,384]{2,1,0:T(8,128)(2,1)S(1)} %collective-permute-done.6.refs_7_), channel_id=1, source_target_pairs={{0,1},{1,2},{2,3},{3,128},{128,129},{129,130},{130,131},{131,0},{4... | collective-permute-start | bytes 884744 | tf_op jit(solution)/shard_map/ppermute | solution.py:155
  57.4 8.0 %collective-permute-start.5 = (bf16[4,96,384]{2,1,0:T(8,128)(2,1)S(1)}, bf16[4,96,384]{2,1,0:T(8,128)(2,1)S(1)}, u32[]{:S(2)}, u32[]{:S(2)}) collective-permute-start(bf16[4,96,384]{2,1,0:T(8,128)(2,1)S(1)} %collective-permute-done.4.refs_2_), channel_id=1, source_target_pairs={{0,131},{1,0},{2,1},{3,2},{128,3},{129,128},{130,129},{131,130},{4... | collective-permute-start | bytes 884744 | tf_op jit(solution)/shard_map/ppermute | solution.py:155
  60.7 8.3 %collective-permute-start.8 = (bf16[4,96,384]{2,1,0:T(8,128)(2,1)S(1)}, bf16[4,96,384]{2,1,0:T(8,128)(2,1)S(1)}, u32[]{:S(2)}, u32[]{:S(2)}) collective-permute-start(bf16[4,96,384]{2,1,0:T(8,128)(2,1)S(1)} %collective-permute-done.7.refs_6_), channel_id=1, source_target_pairs={{0,1},{1,2},{2,3},{3,128},{128,129},{129,130},{130,131},{131,0},{4... | collective-permute-start | bytes 884744 | tf_op jit(solution)/shard_map/ppermute | solution.py:155
  65.4 9.2 %collective-permute-start.10 = (bf16[2,96,384]{2,1,0:T(8,128)(2,1)S(1)}, bf16[2,96,384]{2,1,0:T(8,128)(2,1)S(1)}, u32[]{:S(2)}, u32[]{:S(2)}) collective-permute-start(bf16[2,96,384]{2,1,0:T(8,128)(2,1)S(1)} %slice.28), channel_id=1, source_target_pairs={{0,131},{1,0},{2,1},{3,2},{128,3},{129,128},{130,129},{131,130},{4... | collective-permute-start | bytes 442376 | tf_op jit(solution)/shard_map/ppermute | solution.py:155
  69.0 8.9 %collective-permute-start.9 = (bf16[2,96,384]{2,1,0:T(8,128)(2,1)S(1)}, bf16[2,96,384]{2,1,0:T(8,128)(2,1)}, u32[]{:S(2)}, u32[]{:S(2)}) collective-permute-start(bf16[2,96,384]{2,1,0:T(8,128)(2,1)S(1)} %slice.27), channel_id=1, source_target_pairs={{0,1},{1,2},{2,3},{3,128},{128,129},{129,130},{130,131},{131,0},{4... | collective-permute-start | bytes 442376 | tf_op jit(solution)/shard_map/ppermute | solution.py:155
  92.8 25.3 %all-to-all-start.2 = ((bf16[8,2,96,384]{3,2,1,0:T(8,128)(2,1)}), bf16[8,2,96,384]{3,2,1,0:T(8,128)(2,1)S(1)}, u32[]{:S(2)}, u32[]{:S(2)}) async-start(bf16[8,2,96,384]{3,2,1,0:T(8,128)(2,1)} %contract_a.1), calls=%async_computation.2 | async-start | bytes 2359296 | tf_op jit(solution)/shard_map/all_to_all | solution.py:198
  118.1 1.0 copy-start.1
  119.1 46.5 %all-to-all-start.1 = ((bf16[8,2,96,1152]{3,2,1,0:T(8,128)(2,1)}), bf16[8,2,96,1152]{3,2,1,0:T(8,128)(2,1)S(1)}, u32[]{:S(2)}, u32[]{:S(2)}) async-start(bf16[8,2,96,1152]{3,2,1,0:T(8,128)(2,1)} %contract_b.1), calls=%async_computation.1 | async-start | bytes 7077888 | tf_op jit(solution)/shard_map/all_to_all | solution.py:198
  123.8 1.3 copy-start.2
Sparse Core Ops, SparseCore 0:
  9.9 97.6 all-gather.2

commit v5 on v4

--- a/solution.py
+++ b/solution.py
@@ -70,14 +70,16 @@
             def _():
                 place(p_refs, w_ref, q, pos_ref[0], pos_ref[1])
 
-            w = w_ref[:, pl.ds(pl.multiple_of(n * nt, nt), nt)]
-
+            w = w_ref[...]
 
         x = x_ref[...].reshape(nb * ROWS, PAIRS)
-        acc = jnp.dot(x, w, preferred_element_type=jnp.float32)
-        for m in range(nb):
-            gap = r_ref[m] + c_ref[m]
-            o_ref[m] = (acc[ROWS * m : ROWS * m + ROWS] / gap).astype(jnp.bfloat16)
+        even = width // 256 * 256
+        for left, right in ((0, even), (even, width)):
+            acc = jnp.dot(x, w[:, left:right], preferred_element_type=jnp.float32)
+            for m in range(nb):
+                gap = r_ref[m] + c_ref[m, :, left:right]
+                val = acc[ROWS * m : ROWS * m + ROWS] / gap
+                o_ref[m, :, left:right] = val.astype(jnp.bfloat16)
 
     if place is None:
         piece = pl.BlockSpec((4, 4, NV, width), lambda q, n: (0, q, 0, 0))

time: 175 us -> 175 us (level)
  no operation moved by 1% of the time
where the time goes in v5:
time: 175 us; the launch traced here: 174 us
  waiting for transfers between devices  85.3 us (49%)
  starting transfers between devices  37.2 us (21%)
  Pallas kernels  30.5 us (17%)
  between operations  13.5 us (8%)
  local copies, waits for them, and re-layouts  6.44 us (4%)
    all_to_all x2, waiting for transfers between devices, per_device(): lax.all_to_all(res, ('x', 'c'), split_axis=0, concat_axis=0, tiled=True)  39.4 us
    ppermute x8, waiting for transfers between devices, z_permute(): return lax.ppermute(v, RING, [(i, (i + s) % 8) for i in range(8)])  27.2 us
    pallas_call x2, Pallas kernels, contract(): pl.pallas_call(kernel, grid=(2, width // nt), in_specs=[pl.BlockSpec(memo...  16.2 us
    ppermute x8, starting transfers between devices, z_permute(): return lax.ppermute(v, RING, [(i, (i + s) % 8) for i in range(8)])  16.2 us
    pallas_call x2, Pallas kernels, combine(): pl.pallas_call(kernel, grid=(nb // step,), in_specs=[pl.BlockSpec((None,...  11.2 us
    all_gather x1, waiting for transfers between devices, gather_w(): lax.all_gather(b, ('y',) + RING, axis=0).reshape(4, 8, NV, PAIRS - NA)  10.5 us
    all_to_all x2, starting transfers between devices, per_device(): lax.all_to_all(res, ('x', 'c'), split_axis=0, concat_axis=0, tiled=True)  9.03 us
    all_to_all x1, waiting for transfers between devices, per_device(): lax.all_to_all(comb, ('x', 'c'), split_axis=0, concat_axis=0, tiled=True)  8.13 us
  transfers between devices with their start and end apart: 15, of which 8 were waited for; matrix products, arithmetic and copies ran while one was open for 2% of the time, Pallas kernels for 16%

profile of v5, /device:TPU:1, one launch (start us, length us, event | category | flops | bytes accessed | tf_op | source)
XLA Modules:
  0.0 174.4 jit_solution(12381470020986814960)
XLA Ops:
  6.5 0.0 copy-start
  6.5 0.0 all-gather.3.cloned.1.call-start
  6.5 1.6 slice.30
  8.2 0.0 all-gather.3.cloned.1.call-update
  8.2 0.9 slice_bitcast_fusion
  9.1 2.2 %collective-permute-start.2 = (bf16[96,384]{1,0:T(8,128)(2,1)S(1)}, bf16[96,384]{1,0:T(8,128)(2,1)S(1)}, u32[]{:S(2)}, u32[]{:S(2)}) collective-permute-start(bf16[96,384]{1,0:T(8,128)(2,1)S(1)} %get-tuple-element.16), channel_id=1, source_target_pairs={{0,4},{4,8},{8,12},{12,0},{1,5},{5,9},{9,13},{13,1},{2,6},{6,10},{... | collective-permute-start | bytes 221192 | tf_op jit(solution)/shard_map/ppermute | solution.py:153
  11.3 2.6 %collective-permute-start.1 = (bf16[96,384]{1,0:T(8,128)(2,1)S(1)}, bf16[96,384]{1,0:T(8,128)(2,1)S(1)}, u32[]{:S(2)}, u32[]{:S(2)}) collective-permute-start(bf16[96,384]{1,0:T(8,128)(2,1)S(1)} %get-tuple-element.16), channel_id=1, source_target_pairs={{0,8},{4,12},{8,0},{12,4},{1,9},{5,13},{9,1},{13,5},{2,10},{6,14},... | collective-permute-start | bytes 221192 | tf_op jit(solution)/shard_map/ppermute | solution.py:153
  13.9 1.1 collective-permute-start
  15.0 5.6 %combine.2.refs_0_ = bf16[8,2,96,1536]{3,2,1,0:T(8,128)(2,1)} custom-call(bf16[2,8,96,1536]{3,2,1,0:T(8,128)(2,1)} %bitcast.32), custom_call_target="tpu_custom_call" | custom-call | flops 2400000000 | bytes 4718592 | tf_op jit(solution)/shard_map/combine/pallas_call | solution.py:38
  20.6 0.0 collective-permute-done.2
  20.6 0.0 collective-permute-done.1
  20.6 0.0 collective-permute-done
  20.6 0.1 pad_maximum_fusion.refs_0_
  20.7 5.6 %combine.3 = bf16[8,2,96,1536]{3,2,1,0:T(8,128)(2,1)} custom-call(bf16[2,8,96,1536]{3,2,1,0:T(8,128)(2,1)} %bitcast.33, bf16[8,2,96,1536]{3,2,1,0:T(8,128)(2,1)} %combine.2.refs_0_), custom_call_target="tpu_custom_call", output_to_operand_aliasing={{}: (1, {})} | custom-call | flops 2400000000 | bytes 4718592 | tf_op jit(solution)/shard_map/combine/pallas_call | solution.py:38
  26.3 0.0 copy-start.3
  26.3 6.1 %all-to-all-start = ((bf16[8,2,96,1536]{3,2,1,0:T(8,128)(2,1)}), bf16[8,2,96,1536]{3,2,1,0:T(8,128)(2,1)}, u32[]{:S(2)}, u32[]{:S(2)}) async-start(bf16[8,2,96,1536]{3,2,1,0:T(8,128)(2,1)} %combine.3), calls=%async_computation | async-start | bytes 9437184 | tf_op jit(solution)/shard_map/all_to_all | solution.py:186
  32.4 0.0 copy-done
  32.4 0.1 dynamic-slice_bitcast_fusion
  32.5 0.1 sub.62
  32.6 0.1 sub.63
  32.7 5.6 %collective-permute-start.3 = (bf16[4,96,384]{2,1,0:T(8,128)(2,1)S(1)}, bf16[4,96,384]{2,1,0:T(8,128)(2,1)S(1)}, u32[]{:S(2)}, u32[]{:S(2)}) collective-permute-start(bf16[4,96,384]{2,1,0:T(8,128)(2,1)S(1)} %pad_maximum_fusion.refs_0_), channel_id=1, source_target_pairs={{0,131},{1,0},{2,1},{3,2},{128,3},{129,128},{130,129},{131,130},{4... | collective-permute-start | bytes 884744 | tf_op jit(solution)/shard_map/ppermute | solution.py:157
  38.3 0.0 collective-permute-start.6
  38.3 0.0 copy-done.3
  38.3 0.1 sub.59
  38.4 0.0 copy-done.4
  38.4 0.1 reshape.44
  38.5 0.1 constant_dynamic-slice_fusion
  38.6 0.1 copy.14
  38.6 9.1 %collective-permute-done.3.refs_1_ = bf16[4,96,384]{2,1,0:T(8,128)(2,1)S(1)} collective-permute-done((bf16[4,96,384]{2,1,0:T(8,128)(2,1)S(1)}, bf16[4,96,384]{2,1,0:T(8,128)(2,1)S(1)}, u32[]{:S(2)}, u32[]{:S(2)}) %collective-permute-start.3) | collective-permute-done | bytes 294944 | tf_op jit(solution)/shard_map/ppermute | solution.py:157
  47.8 3.5 %collective-permute-start.4 = (bf16[4,96,384]{2,1,0:T(8,128)(2,1)S(1)}, bf16[4,96,384]{2,1,0:T(8,128)(2,1)S(1)}, u32[]{:S(2)}, u32[]{:S(2)}) collective-permute-start(bf16[4,96,384]{2,1,0:T(8,128)(2,1)S(1)} %collective-permute-done.3.refs_1_), channel_id=1, source_target_pairs={{0,131},{1,0},{2,1},{3,2},{128,3},{129,128},{130,129},{131,130},{4... | collective-permute-start | bytes 884744 | tf_op jit(solution)/shard_map/ppermute | solution.py:157
  51.3 0.0 collective-permute-done.6.refs_7_
  51.3 0.0 collective-permute-start.7
  51.3 0.1 reshape.49
  51.4 0.6 gather_fusion
  52.0 0.2 sub.71
  52.1 0.0 copy-done.5
  52.2 0.1 sub.67
  52.2 0.1 sub.68
  52.3 5.1 %collective-permute-done.4.refs_2_ = bf16[4,96,384]{2,1,0:T(8,128)(2,1)S(1)} collective-permute-done((bf16[4,96,384]{2,1,0:T(8,128)(2,1)S(1)}, bf16[4,96,384]{2,1,0:T(8,128)(2,1)S(1)}, u32[]{:S(2)}, u32[]{:S(2)}) %collective-permute-start.4) | collective-permute-done | bytes 294944 | tf_op jit(solution)/shard_map/ppermute | solution.py:157
  57.4 3.3 %collective-permute-start.5 = (bf16[4,96,384]{2,1,0:T(8,128)(2,1)S(1)}, bf16[4,96,384]{2,1,0:T(8,128)(2,1)S(1)}, u32[]{:S(2)}, u32[]{:S(2)}) collective-permute-start(bf16[4,96,384]{2,1,0:T(8,128)(2,1)S(1)} %collective-permute-done.4.refs_2_), channel_id=1, source_target_pairs={{0,131},{1,0},{2,1},{3,2},{128,3},{129,128},{130,129},{131,130},{4... | collective-permute-start | bytes 884744 | tf_op jit(solution)/shard_map/ppermute | solution.py:157
  60.7 0.0 collective-permute-done.7.refs_6_
  60.7 0.0 collective-permute-start.8
  60.8 0.1 broadcast_subtract_fusion.1
  60.8 4.6 %collective-permute-done.5.refs_3_ = bf16[4,96,384]{2,1,0:T(8,128)(2,1)S(1)} collective-permute-done((bf16[4,96,384]{2,1,0:T(8,128)(2,1)S(1)}, bf16[4,96,384]{2,1,0:T(8,128)(2,1)S(1)}, u32[]{:S(2)}, u32[]{:S(2)}) %collective-permute-start.5) | collective-permute-done | bytes 294944 | tf_op jit(solution)/shard_map/ppermute | solution.py:157
  65.4 3.6 %collective-permute-start.10 = (bf16[2,96,384]{2,1,0:T(8,128)(2,1)S(1)}, bf16[2,96,384]{2,1,0:T(8,128)(2,1)S(1)}, u32[]{:S(2)}, u32[]{:S(2)}) collective-permute-start(bf16[2,96,384]{2,1,0:T(8,128)(2,1)S(1)} %slice.28), channel_id=1, source_target_pairs={{0,131},{1,0},{2,1},{3,2},{128,3},{129,128},{130,129},{131,130},{4... | collective-permute-start | bytes 442376 | tf_op jit(solution)/shard_map/ppermute | solution.py:157
  69.0 0.0 collective-permute-done.8.refs_5_
  69.0 0.1 collective-permute-start.9
  69.1 0.2 broadcast_subtract_fusion.refs_8_.refs_1_
  69.4 0.1 pad_add_fusion.pos_ref
  69.5 5.2 %collective-permute-done.10 = bf16[2,96,384]{2,1,0:T(8,128)(2,1)S(1)} collective-permute-done((bf16[2,96,384]{2,1,0:T(8,128)(2,1)S(1)}, bf16[2,96,384]{2,1,0:T(8,128)(2,1)S(1)}, u32[]{:S(2)}, u32[]{:S(2)}) %collective-permute-start.10) | collective-permute-done | bytes 147488 | tf_op jit(solution)/shard_map/ppermute | solution.py:157
  74.6 3.3 %collective-permute-done.9 = bf16[2,96,384]{2,1,0:T(8,128)(2,1)} collective-permute-done((bf16[2,96,384]{2,1,0:T(8,128)(2,1)S(1)}, bf16[2,96,384]{2,1,0:T(8,128)(2,1)}, u32[]{:S(2)}, u32[]{:S(2)}) %collective-permute-start.9) | collective-permute-done | bytes 147488 | tf_op jit(solution)/shard_map/ppermute | solution.py:157
  77.9 0.9 pad_maximum_fusion.1.refs_4_
  78.9 8.1 %all-to-all-done.x_ref = bf16[8,2,96,1536]{3,2,1,0:T(8,128)(2,1)} async-done(((bf16[8,2,96,1536]{3,2,1,0:T(8,128)(2,1)}), bf16[8,2,96,1536]{3,2,1,0:T(8,128)(2,1)}, u32[]{:S(2)}, u32[]{:S(2)}) %all-to-all-start) | async-done | bytes 4718624 | tf_op jit(solution)/shard_map/all_to_all | solution.py:186
  87.0 5.8 %contract_a.1 = bf16[8,2,96,384]{3,2,1,0:T(8,128)(2,1)} custom-call(s32[2]{0:T(128)S(1)} %pad_add_fusion.pos_ref, bf16[8,2,96,1536]{3,2,1,0:T(8,128)(2,1)} %all-to-all-done.x_ref, bf16[4,96,384]{2,1,0:T(8,128)(2,1)S(1)} %pad_maximum_fusion.refs_0_, bf16[4,96,384]{2,1,0:T(8,128)(2,1)S(1)} %collective-permute-done.3.refs_1_, ...), custom_call_target="tpu_custom_call" | custom-call | flops 589824 | bytes 1536 | tf_op jit(solution)/shard_map/contract_a/pallas_call | solution.py:88
  92.8 4.3 %all-to-all-start.2 = ((bf16[8,2,96,384]{3,2,1,0:T(8,128)(2,1)}), bf16[8,2,96,384]{3,2,1,0:T(8,128)(2,1)S(1)}, u32[]{:S(2)}, u32[]{:S(2)}) async-start(bf16[8,2,96,384]{3,2,1,0:T(8,128)(2,1)} %contract_a.1), calls=%async_computation.2 | async-start | bytes 2359296 | tf_op jit(solution)/shard_map/all_to_all | solution.py:200
  97.1 10.5 %all-gather.3.cloned.1.call-done = bf16[3072,1152]{1,0:T(8,128)(2,1)} async-done(((bf16[96,1152]{1,0:T(8,128)(2,1)}), bf16[3072,1152]{1,0:T(8,128)(2,1)}) %all-gather.3.cloned.1.call-update) | async-done | bytes 7077904 | tf_op jit(solution)/shard_map/all_gather | solution.py:166
  107.7 10.4 %contract_b.1 = bf16[8,2,96,1152]{3,2,1,0:T(8,128)(2,1)} custom-call(s32[2]{0:T(128)S(1)} %pad_add_fusion.pos_ref, bf16[8,2,96,1536]{3,2,1,0:T(8,128)(2,1)} %all-to-all-done.x_ref, bf16[4,8,96,1152]{3,2,1,0:T(8,128)(2,1)} %bitcast.34, f32[2,8,96,1]{3,2,1,0:T(8,128)S(1)} %broadcast_subtract_fusion.refs_8_.refs_1_, f32[2,8,1,1152]{3,2,1,0:T(1,128)S(1)} %slice.31.refs_2_), custom_call_target="tpu_custom_call" | custom-call | flops 1769472 | bytes 1536 | tf_op jit(solution)/shard_map/contract_b/pallas_call | solution.py:88
  118.1 0.0 all-to-all-done.2.v_ref
  118.1 1.0 copy-done.1
  119.1 4.7 %all-to-all-start.1 = ((bf16[8,2,96,1152]{3,2,1,0:T(8,128)(2,1)}), bf16[8,2,96,1152]{3,2,1,0:T(8,128)(2,1)S(1)}, u32[]{:S(2)}, u32[]{:S(2)}) async-start(bf16[8,2,96,1152]{3,2,1,0:T(8,128)(2,1)} %contract_b.1), calls=%async_computation.1 | async-start | bytes 7077888 | tf_op jit(solution)/shard_map/all_to_all | solution.py:200
  123.8 1.3 copy-done.2
  125.1 1.1 merge_a.1.refs_0_
  126.2 39.4 %all-to-all-done.1.v_ref = bf16[8,2,96,1152]{3,2,1,0:T(8,128)(2,1)S(1)} async-done(((bf16[8,2,96,1152]{3,2,1,0:T(8,128)(2,1)}), bf16[8,2,96,1152]{3,2,1,0:T(8,128)(2,1)S(1)}, u32[]{:S(2)}, u32[]{:S(2)}) %all-to-all-start.1) | async-done | bytes 3538976 | tf_op jit(solution)/shard_map/all_to_all | solution.py:200
  165.6 1.9 %merge_b.1 = bf16[2,8,96,1536]{3,2,1,0:T(8,128)(2,1)} custom-call(bf16[8,2,96,1152]{3,2,1,0:T(8,128)(2,1)S(1)} %all-to-all-done.1.v_ref, bf16[2,8,96,1536]{3,2,1,0:T(8,128)(2,1)} %merge_a.1.refs_0_), custom_call_target="tpu_custom_call", output_to_operand_aliasing={{}: (1, {})} | custom-call | tf_op jit(solution)/shard_map/merge_b/pallas_call | solution.py:140
  (15 shorter events, 0.1 us)
Async XLA Ops:
  6.5 25.9 %copy-start = (f32[16,96]{1,0:T(8,128)S(1)}, f32[16,96]{1,0:T(8,128)}, u32[]{:S(2)}) copy-start(f32[16,96]{1,0:T(8,128)} %param.10) | copy-start | bytes 18436
  6.5 101.1 %all-gather.3.cloned.1.call-start = ((), (), s32[]{:S(2)}) async-start(), calls=%async_computation.3 | async-start | bytes 7299072 | tf_op jit(solution)/shard_map/all_gather | solution.py:166
  9.1 11.5 %collective-permute-start.2 = (bf16[96,384]{1,0:T(8,128)(2,1)S(1)}, bf16[96,384]{1,0:T(8,128)(2,1)S(1)}, u32[]{:S(2)}, u32[]{:S(2)}) collective-permute-start(bf16[96,384]{1,0:T(8,128)(2,1)S(1)} %get-tuple-element.16), channel_id=1, source_target_pairs={{0,4},{4,8},{8,12},{12,0},{1,5},{5,9},{9,13},{13,1},{2,6},{6,10},{... | collective-permute-start | bytes 221192 | tf_op jit(solution)/shard_map/ppermute | solution.py:153
  11.3 9.3 %collective-permute-start.1 = (bf16[96,384]{1,0:T(8,128)(2,1)S(1)}, bf16[96,384]{1,0:T(8,128)(2,1)S(1)}, u32[]{:S(2)}, u32[]{:S(2)}) collective-permute-start(bf16[96,384]{1,0:T(8,128)(2,1)S(1)} %get-tuple-element.16), channel_id=1, source_target_pairs={{0,8},{4,12},{8,0},{12,4},{1,9},{5,13},{9,1},{13,5},{2,10},{6,14},... | collective-permute-start | bytes 221192 | tf_op jit(solution)/shard_map/ppermute | solution.py:153
  13.9 6.7 %collective-permute-start = (bf16[96,384]{1,0:T(8,128)(2,1)S(1)}, bf16[96,384]{1,0:T(8,128)(2,1)S(1)}, u32[]{:S(2)}, u32[]{:S(2)}) collective-permute-start(bf16[96,384]{1,0:T(8,128)(2,1)S(1)} %get-tuple-element.16), channel_id=1, source_target_pairs={{0,12},{4,0},{8,4},{12,8},{1,13},{5,1},{9,5},{13,9},{2,14},{6,2},{... | collective-permute-start | bytes 221192 | tf_op jit(solution)/shard_map/ppermute | solution.py:153
  26.3 12.0 %copy-start.3 = (f32[16,16]{1,0:T(8,128)S(1)}, f32[16,16]{1,0:T(8,128)}, u32[]{:S(2)}) copy-start(f32[16,16]{1,0:T(8,128)} %param.8) | copy-start | bytes 3076
  26.3 12.1 %copy-start.4 = (s32[1,16,16]{2,1,0:T(8,128)S(1)}, s32[1,16,16]{2,1,0:T(8,128)}, u32[]{:S(2)}) copy-start(s32[1,16,16]{2,1,0:T(8,128)} %param.11) | copy-start | bytes 3076
  26.3 25.8 %copy-start.5 = (f32[1,16]{1,0:T(1,128)S(1)}, f32[1,16]{1,0:T(1,128)}, u32[]{:S(2)}) copy-start(f32[1,16]{1,0:T(1,128)} %param.9) | copy-start | bytes 196
  26.3 60.7 %all-to-all-start = ((bf16[8,2,96,1536]{3,2,1,0:T(8,128)(2,1)}), bf16[8,2,96,1536]{3,2,1,0:T(8,128)(2,1)}, u32[]{:S(2)}, u32[]{:S(2)}) async-start(bf16[8,2,96,1536]{3,2,1,0:T(8,128)(2,1)} %combine.3), calls=%async_computation | async-start | bytes 9437184 | tf_op jit(solution)/shard_map/all_to_all | solution.py:186
  32.7 15.1 %collective-permute-start.3 = (bf16[4,96,384]{2,1,0:T(8,128)(2,1)S(1)}, bf16[4,96,384]{2,1,0:T(8,128)(2,1)S(1)}, u32[]{:S(2)}, u32[]{:S(2)}) collective-permute-start(bf16[4,96,384]{2,1,0:T(8,128)(2,1)S(1)} %pad_maximum_fusion.refs_0_), channel_id=1, source_target_pairs={{0,131},{1,0},{2,1},{3,2},{128,3},{129,128},{130,129},{131,130},{4... | collective-permute-start | bytes 884744 | tf_op jit(solution)/shard_map/ppermute | solution.py:157
  38.3 13.0 %collective-permute-start.6 = (bf16[4,96,384]{2,1,0:T(8,128)(2,1)S(1)}, bf16[4,96,384]{2,1,0:T(8,128)(2,1)S(1)}, u32[]{:S(2)}, u32[]{:S(2)}) collective-permute-start(bf16[4,96,384]{2,1,0:T(8,128)(2,1)S(1)} %pad_maximum_fusion.refs_0_), channel_id=1, source_target_pairs={{0,1},{1,2},{2,3},{3,128},{128,129},{129,130},{130,131},{131,0},{4... | collective-permute-start | bytes 884744 | tf_op jit(solution)/shard_map/ppermute | solution.py:157
  47.8 9.6 %collective-permute-start.4 = (bf16[4,96,384]{2,1,0:T(8,128)(2,1)S(1)}, bf16[4,96,384]{2,1,0:T(8,128)(2,1)S(1)}, u32[]{:S(2)}, u32[]{:S(2)}) collective-permute-start(bf16[4,96,384]{2,1,0:T(8,128)(2,1)S(1)} %collective-permute-done.3.refs_1_), channel_id=1, source_target_pairs={{0,131},{1,0},{2,1},{3,2},{128,3},{129,128},{130,129},{131,130},{4... | collective-permute-start | bytes 884744 | tf_op jit(solution)/shard_map/ppermute | solution.py:157
  51.3 9.5 %collective-permute-start.7 = (bf16[4,96,384]{2,1,0:T(8,128)(2,1)S(1)}, bf16[4,96,384]{2,1,0:T(8,128)(2,1)S(1)}, u32[]{:S(2)}, u32[]{:S(2)}) collective-permute-start(bf16[4,96,384]{2,1,0:T(8,128)(2,1)S(1)} %collective-permute-done.6.refs_7_), channel_id=1, source_target_pairs={{0,1},{1,2},{2,3},{3,128},{128,129},{129,130},{130,131},{131,0},{4... | collective-permute-start | bytes 884744 | tf_op jit(solution)/shard_map/ppermute | solution.py:157
  57.4 8.0 %collective-permute-start.5 = (bf16[4,96,384]{2,1,0:T(8,128)(2,1)S(1)}, bf16[4,96,384]{2,1,0:T(8,128)(2,1)S(1)}, u32[]{:S(2)}, u32[]{:S(2)}) collective-permute-start(bf16[4,96,384]{2,1,0:T(8,128)(2,1)S(1)} %collective-permute-done.4.refs_2_), channel_id=1, source_target_pairs={{0,131},{1,0},{2,1},{3,2},{128,3},{129,128},{130,129},{131,130},{4... | collective-permute-start | bytes 884744 | tf_op jit(solution)/shard_map/ppermute | solution.py:157
  60.7 8.3 %collective-permute-start.8 = (bf16[4,96,384]{2,1,0:T(8,128)(2,1)S(1)}, bf16[4,96,384]{2,1,0:T(8,128)(2,1)S(1)}, u32[]{:S(2)}, u32[]{:S(2)}) collective-permute-start(bf16[4,96,384]{2,1,0:T(8,128)(2,1)S(1)} %collective-permute-done.7.refs_6_), channel_id=1, source_target_pairs={{0,1},{1,2},{2,3},{3,128},{128,129},{129,130},{130,131},{131,0},{4... | collective-permute-start | bytes 884744 | tf_op jit(solution)/shard_map/ppermute | solution.py:157
  65.4 9.2 %collective-permute-start.10 = (bf16[2,96,384]{2,1,0:T(8,128)(2,1)S(1)}, bf16[2,96,384]{2,1,0:T(8,128)(2,1)S(1)}, u32[]{:S(2)}, u32[]{:S(2)}) collective-permute-start(bf16[2,96,384]{2,1,0:T(8,128)(2,1)S(1)} %slice.28), channel_id=1, source_target_pairs={{0,131},{1,0},{2,1},{3,2},{128,3},{129,128},{130,129},{131,130},{4... | collective-permute-start | bytes 442376 | tf_op jit(solution)/shard_map/ppermute | solution.py:157
  69.0 8.9 %collective-permute-start.9 = (bf16[2,96,384]{2,1,0:T(8,128)(2,1)S(1)}, bf16[2,96,384]{2,1,0:T(8,128)(2,1)}, u32[]{:S(2)}, u32[]{:S(2)}) collective-permute-start(bf16[2,96,384]{2,1,0:T(8,128)(2,1)S(1)} %slice.27), channel_id=1, source_target_pairs={{0,1},{1,2},{2,3},{3,128},{128,129},{129,130},{130,131},{131,0},{4... | collective-permute-start | bytes 442376 | tf_op jit(solution)/shard_map/ppermute | solution.py:157
  92.8 25.3 %all-to-all-start.2 = ((bf16[8,2,96,384]{3,2,1,0:T(8,128)(2,1)}), bf16[8,2,96,384]{3,2,1,0:T(8,128)(2,1)S(1)}, u32[]{:S(2)}, u32[]{:S(2)}) async-start(bf16[8,2,96,384]{3,2,1,0:T(8,128)(2,1)} %contract_a.1), calls=%async_computation.2 | async-start | bytes 2359296 | tf_op jit(solution)/shard_map/all_to_all | solution.py:200
  118.1 1.0 copy-start.1
  119.1 46.5 %all-to-all-start.1 = ((bf16[8,2,96,1152]{3,2,1,0:T(8,128)(2,1)}), bf16[8,2,96,1152]{3,2,1,0:T(8,128)(2,1)S(1)}, u32[]{:S(2)}, u32[]{:S(2)}) async-start(bf16[8,2,96,1152]{3,2,1,0:T(8,128)(2,1)} %contract_b.1), calls=%async_computation.1 | async-start | bytes 7077888 | tf_op jit(solution)/shard_map/all_to_all | solution.py:200
  123.8 1.3 copy-start.2
Sparse Core Ops, SparseCore 0:
  9.9 97.6 all-gather.2

commit v6 on v5

--- a/solution.py
+++ b/solution.py
@@ -16,7 +16,7 @@
 
 
 def combine(x, q, out):
-    nb, sq, step = x.shape[1], NO * NO, 2
+    nb, sq, step = x.shape[1], NO * NO, 4
 
     def kernel(x_ref, *refs):
         o_ref, scr = refs[-2:]

time: 175 us -> 175 us (level)
  no operation moved by 1% of the time
where the time goes in v6:
time: 175 us; the launch traced here: 174 us
  waiting for transfers between devices  85.7 us (49%)
  starting transfers between devices  37 us (21%)
  Pallas kernels  30.2 us (17%)
  between operations  13.5 us (8%)
  local copies, waits for them, and re-layouts  6.43 us (4%)
    all_to_all x2, waiting for transfers between devices, per_device(): lax.all_to_all(res, ('x', 'c'), split_axis=0, concat_axis=0, tiled=True)  39.4 us
    ppermute x8, waiting for transfers between devices, z_permute(): return lax.ppermute(v, RING, [(i, (i + s) % 8) for i in range(8)])  28.1 us
    pallas_call x2, Pallas kernels, contract(): pl.pallas_call(kernel, grid=(2, width // nt), in_specs=[pl.BlockSpec(memo...  16.2 us
    ppermute x8, starting transfers between devices, z_permute(): return lax.ppermute(v, RING, [(i, (i + s) % 8) for i in range(8)])  16.2 us
    all_gather x1, waiting for transfers between devices, gather_w(): lax.all_gather(b, ('y',) + RING, axis=0).reshape(4, 8, NV, PAIRS - NA)  11 us
    pallas_call x2, Pallas kernels, combine(): pl.pallas_call(kernel, grid=(nb // step,), in_specs=[pl.BlockSpec((None,...  11 us
    all_to_all x2, starting transfers between devices, per_device(): lax.all_to_all(res, ('x', 'c'), split_axis=0, concat_axis=0, tiled=True)  8.79 us
    all_to_all x1, waiting for transfers between devices, per_device(): lax.all_to_all(comb, ('x', 'c'), split_axis=0, concat_axis=0, tiled=True)  7.26 us
  transfers between devices with their start and end apart: 15, of which 8 were waited for; matrix products, arithmetic and copies ran while one was open for 2% of the time, Pallas kernels for 16%

profile of v6, /device:TPU:1, one launch (start us, length us, event | category | flops | bytes accessed | tf_op | source)
XLA Modules:
  0.0 174.3 jit_solution(15016794592354125712)
XLA Ops:
  6.5 0.0 copy-start
  6.5 0.0 all-gather.3.cloned.1.call-start
  6.5 1.6 slice.30
  8.2 0.0 all-gather.3.cloned.1.call-update
  8.2 0.9 slice_bitcast_fusion
  9.1 2.2 %collective-permute-start.2 = (bf16[96,384]{1,0:T(8,128)(2,1)S(1)}, bf16[96,384]{1,0:T(8,128)(2,1)S(1)}, u32[]{:S(2)}, u32[]{:S(2)}) collective-permute-start(bf16[96,384]{1,0:T(8,128)(2,1)S(1)} %get-tuple-element.16), channel_id=1, source_target_pairs={{0,4},{4,8},{8,12},{12,0},{1,5},{5,9},{9,13},{13,1},{2,6},{6,10},{... | collective-permute-start | bytes 221192 | tf_op jit(solution)/shard_map/ppermute | solution.py:153
  11.3 2.6 %collective-permute-start.1 = (bf16[96,384]{1,0:T(8,128)(2,1)S(1)}, bf16[96,384]{1,0:T(8,128)(2,1)S(1)}, u32[]{:S(2)}, u32[]{:S(2)}) collective-permute-start(bf16[96,384]{1,0:T(8,128)(2,1)S(1)} %get-tuple-element.16), channel_id=1, source_target_pairs={{0,8},{4,12},{8,0},{12,4},{1,9},{5,13},{9,1},{13,5},{2,10},{6,14},... | collective-permute-start | bytes 221192 | tf_op jit(solution)/shard_map/ppermute | solution.py:153
  13.9 1.1 collective-permute-start
  15.0 5.5 %combine.2.refs_0_ = bf16[8,2,96,1536]{3,2,1,0:T(8,128)(2,1)} custom-call(bf16[2,8,96,1536]{3,2,1,0:T(8,128)(2,1)} %bitcast.32), custom_call_target="tpu_custom_call" | custom-call | flops 2400000000 | bytes 4718592 | tf_op jit(solution)/shard_map/combine/pallas_call | solution.py:38
  20.5 0.0 collective-permute-done.2
  20.5 0.0 collective-permute-done.1
  20.5 0.0 collective-permute-done
  20.5 0.1 pad_maximum_fusion.refs_0_
  20.5 5.5 %combine.3 = bf16[8,2,96,1536]{3,2,1,0:T(8,128)(2,1)} custom-call(bf16[2,8,96,1536]{3,2,1,0:T(8,128)(2,1)} %bitcast.33, bf16[8,2,96,1536]{3,2,1,0:T(8,128)(2,1)} %combine.2.refs_0_), custom_call_target="tpu_custom_call", output_to_operand_aliasing={{}: (1, {})} | custom-call | flops 2400000000 | bytes 4718592 | tf_op jit(solution)/shard_map/combine/pallas_call | solution.py:38
  26.0 0.0 copy-start.3
  26.0 6.1 %all-to-all-start = ((bf16[8,2,96,1536]{3,2,1,0:T(8,128)(2,1)}), bf16[8,2,96,1536]{3,2,1,0:T(8,128)(2,1)}, u32[]{:S(2)}, u32[]{:S(2)}) async-start(bf16[8,2,96,1536]{3,2,1,0:T(8,128)(2,1)} %combine.3), calls=%async_computation | async-start | bytes 9437184 | tf_op jit(solution)/shard_map/all_to_all | solution.py:186
  32.2 0.0 copy-done
  32.2 0.1 dynamic-slice_bitcast_fusion
  32.3 0.1 sub.62
  32.3 0.1 sub.63
  32.4 5.6 %collective-permute-start.3 = (bf16[4,96,384]{2,1,0:T(8,128)(2,1)S(1)}, bf16[4,96,384]{2,1,0:T(8,128)(2,1)S(1)}, u32[]{:S(2)}, u32[]{:S(2)}) collective-permute-start(bf16[4,96,384]{2,1,0:T(8,128)(2,1)S(1)} %pad_maximum_fusion.refs_0_), channel_id=1, source_target_pairs={{0,131},{1,0},{2,1},{3,2},{128,3},{129,128},{130,129},{131,130},{4... | collective-permute-start | bytes 884744 | tf_op jit(solution)/shard_map/ppermute | solution.py:157
  38.0 0.0 collective-permute-start.6
  38.0 0.0 copy-done.3
  38.0 0.1 sub.59
  38.1 0.0 copy-done.4
  38.1 0.1 reshape.44
  38.2 0.1 constant_dynamic-slice_fusion
  38.3 0.1 copy.14
  38.4 9.4 %collective-permute-done.3.refs_1_ = bf16[4,96,384]{2,1,0:T(8,128)(2,1)S(1)} collective-permute-done((bf16[4,96,384]{2,1,0:T(8,128)(2,1)S(1)}, bf16[4,96,384]{2,1,0:T(8,128)(2,1)S(1)}, u32[]{:S(2)}, u32[]{:S(2)}) %collective-permute-start.3) | collective-permute-done | bytes 294944 | tf_op jit(solution)/shard_map/ppermute | solution.py:157
  47.7 3.5 %collective-permute-start.4 = (bf16[4,96,384]{2,1,0:T(8,128)(2,1)S(1)}, bf16[4,96,384]{2,1,0:T(8,128)(2,1)S(1)}, u32[]{:S(2)}, u32[]{:S(2)}) collective-permute-start(bf16[4,96,384]{2,1,0:T(8,128)(2,1)S(1)} %collective-permute-done.3.refs_1_), channel_id=1, source_target_pairs={{0,131},{1,0},{2,1},{3,2},{128,3},{129,128},{130,129},{131,130},{4... | collective-permute-start | bytes 884744 | tf_op jit(solution)/shard_map/ppermute | solution.py:157
  51.2 0.0 collective-permute-done.6.refs_7_
  51.2 0.0 collective-permute-start.7
  51.2 0.1 reshape.49
  51.3 0.6 gather_fusion
  51.9 0.2 sub.71
  52.1 0.0 copy-done.5
  52.1 0.1 sub.67
  52.1 0.1 sub.68
  52.2 5.3 %collective-permute-done.4.refs_2_ = bf16[4,96,384]{2,1,0:T(8,128)(2,1)S(1)} collective-permute-done((bf16[4,96,384]{2,1,0:T(8,128)(2,1)S(1)}, bf16[4,96,384]{2,1,0:T(8,128)(2,1)S(1)}, u32[]{:S(2)}, u32[]{:S(2)}) %collective-permute-start.4) | collective-permute-done | bytes 294944 | tf_op jit(solution)/shard_map/ppermute | solution.py:157
  57.5 3.4 %collective-permute-start.5 = (bf16[4,96,384]{2,1,0:T(8,128)(2,1)S(1)}, bf16[4,96,384]{2,1,0:T(8,128)(2,1)S(1)}, u32[]{:S(2)}, u32[]{:S(2)}) collective-permute-start(bf16[4,96,384]{2,1,0:T(8,128)(2,1)S(1)} %collective-permute-done.4.refs_2_), channel_id=1, source_target_pairs={{0,131},{1,0},{2,1},{3,2},{128,3},{129,128},{130,129},{131,130},{4... | collective-permute-start | bytes 884744 | tf_op jit(solution)/shard_map/ppermute | solution.py:157
  60.9 0.0 collective-permute-done.7.refs_6_
  60.9 0.0 collective-permute-start.8
  60.9 0.1 broadcast_subtract_fusion.1
  60.9 4.8 %collective-permute-done.5.refs_3_ = bf16[4,96,384]{2,1,0:T(8,128)(2,1)S(1)} collective-permute-done((bf16[4,96,384]{2,1,0:T(8,128)(2,1)S(1)}, bf16[4,96,384]{2,1,0:T(8,128)(2,1)S(1)}, u32[]{:S(2)}, u32[]{:S(2)}) %collective-permute-start.5) | collective-permute-done | bytes 294944 | tf_op jit(solution)/shard_map/ppermute | solution.py:157
  65.7 3.7 %collective-permute-start.10 = (bf16[2,96,384]{2,1,0:T(8,128)(2,1)S(1)}, bf16[2,96,384]{2,1,0:T(8,128)(2,1)S(1)}, u32[]{:S(2)}, u32[]{:S(2)}) collective-permute-start(bf16[2,96,384]{2,1,0:T(8,128)(2,1)S(1)} %slice.28), channel_id=1, source_target_pairs={{0,131},{1,0},{2,1},{3,2},{128,3},{129,128},{130,129},{131,130},{4... | collective-permute-start | bytes 442376 | tf_op jit(solution)/shard_map/ppermute | solution.py:157
  69.4 0.0 collective-permute-done.8.refs_5_
  69.4 0.1 collective-permute-start.9
  69.5 0.2 broadcast_subtract_fusion.refs_8_.refs_1_
  69.8 0.1 pad_add_fusion.pos_ref
  69.8 5.3 %collective-permute-done.10 = bf16[2,96,384]{2,1,0:T(8,128)(2,1)S(1)} collective-permute-done((bf16[2,96,384]{2,1,0:T(8,128)(2,1)S(1)}, bf16[2,96,384]{2,1,0:T(8,128)(2,1)S(1)}, u32[]{:S(2)}, u32[]{:S(2)}) %collective-permute-start.10) | collective-permute-done | bytes 147488 | tf_op jit(solution)/shard_map/ppermute | solution.py:157
  75.1 3.4 %collective-permute-done.9 = bf16[2,96,384]{2,1,0:T(8,128)(2,1)} collective-permute-done((bf16[2,96,384]{2,1,0:T(8,128)(2,1)S(1)}, bf16[2,96,384]{2,1,0:T(8,128)(2,1)}, u32[]{:S(2)}, u32[]{:S(2)}) %collective-permute-start.9) | collective-permute-done | bytes 147488 | tf_op jit(solution)/shard_map/ppermute | solution.py:157
  78.5 0.9 pad_maximum_fusion.1.refs_4_
  79.5 7.3 %all-to-all-done.x_ref = bf16[8,2,96,1536]{3,2,1,0:T(8,128)(2,1)} async-done(((bf16[8,2,96,1536]{3,2,1,0:T(8,128)(2,1)}), bf16[8,2,96,1536]{3,2,1,0:T(8,128)(2,1)}, u32[]{:S(2)}, u32[]{:S(2)}) %all-to-all-start) | async-done | bytes 4718624 | tf_op jit(solution)/shard_map/all_to_all | solution.py:186
  86.7 5.8 %contract_a.1 = bf16[8,2,96,384]{3,2,1,0:T(8,128)(2,1)} custom-call(s32[2]{0:T(128)S(1)} %pad_add_fusion.pos_ref, bf16[8,2,96,1536]{3,2,1,0:T(8,128)(2,1)} %all-to-all-done.x_ref, bf16[4,96,384]{2,1,0:T(8,128)(2,1)S(1)} %pad_maximum_fusion.refs_0_, bf16[4,96,384]{2,1,0:T(8,128)(2,1)S(1)} %collective-permute-done.3.refs_1_, ...), custom_call_target="tpu_custom_call" | custom-call | flops 589824 | bytes 1536 | tf_op jit(solution)/shard_map/contract_a/pallas_call | solution.py:88
  92.5 4.3 %all-to-all-start.2 = ((bf16[8,2,96,384]{3,2,1,0:T(8,128)(2,1)}), bf16[8,2,96,384]{3,2,1,0:T(8,128)(2,1)S(1)}, u32[]{:S(2)}, u32[]{:S(2)}) async-start(bf16[8,2,96,384]{3,2,1,0:T(8,128)(2,1)} %contract_a.1), calls=%async_computation.2 | async-start | bytes 2359296 | tf_op jit(solution)/shard_map/all_to_all | solution.py:200
  96.9 11.0 %all-gather.3.cloned.1.call-done = bf16[3072,1152]{1,0:T(8,128)(2,1)} async-done(((bf16[96,1152]{1,0:T(8,128)(2,1)}), bf16[3072,1152]{1,0:T(8,128)(2,1)}) %all-gather.3.cloned.1.call-update) | async-done | bytes 7077904 | tf_op jit(solution)/shard_map/all_gather | solution.py:166
  107.8 10.4 %contract_b.1 = bf16[8,2,96,1152]{3,2,1,0:T(8,128)(2,1)} custom-call(s32[2]{0:T(128)S(1)} %pad_add_fusion.pos_ref, bf16[8,2,96,1536]{3,2,1,0:T(8,128)(2,1)} %all-to-all-done.x_ref, bf16[4,8,96,1152]{3,2,1,0:T(8,128)(2,1)} %bitcast.34, f32[2,8,96,1]{3,2,1,0:T(8,128)S(1)} %broadcast_subtract_fusion.refs_8_.refs_1_, f32[2,8,1,1152]{3,2,1,0:T(1,128)S(1)} %slice.31.refs_2_), custom_call_target="tpu_custom_call" | custom-call | flops 1769472 | bytes 1536 | tf_op jit(solution)/shard_map/contract_b/pallas_call | solution.py:88
  118.3 0.0 all-to-all-done.2.v_ref
  118.3 1.0 copy-done.1
  119.3 4.4 %all-to-all-start.1 = ((bf16[8,2,96,1152]{3,2,1,0:T(8,128)(2,1)}), bf16[8,2,96,1152]{3,2,1,0:T(8,128)(2,1)S(1)}, u32[]{:S(2)}, u32[]{:S(2)}) async-start(bf16[8,2,96,1152]{3,2,1,0:T(8,128)(2,1)} %contract_b.1), calls=%async_computation.1 | async-start | bytes 7077888 | tf_op jit(solution)/shard_map/all_to_all | solution.py:200
  123.7 1.3 copy-done.2
  125.0 1.1 merge_a.1.refs_0_
  126.1 39.4 %all-to-all-done.1.v_ref = bf16[8,2,96,1152]{3,2,1,0:T(8,128)(2,1)S(1)} async-done(((bf16[8,2,96,1152]{3,2,1,0:T(8,128)(2,1)}), bf16[8,2,96,1152]{3,2,1,0:T(8,128)(2,1)S(1)}, u32[]{:S(2)}, u32[]{:S(2)}) %all-to-all-start.1) | async-done | bytes 3538976 | tf_op jit(solution)/shard_map/all_to_all | solution.py:200
  165.5 1.9 %merge_b.1 = bf16[2,8,96,1536]{3,2,1,0:T(8,128)(2,1)} custom-call(bf16[8,2,96,1152]{3,2,1,0:T(8,128)(2,1)S(1)} %all-to-all-done.1.v_ref, bf16[2,8,96,1536]{3,2,1,0:T(8,128)(2,1)} %merge_a.1.refs_0_), custom_call_target="tpu_custom_call", output_to_operand_aliasing={{}: (1, {})} | custom-call | tf_op jit(solution)/shard_map/merge_b/pallas_call | solution.py:140
  (15 shorter events, 0.1 us)
Async XLA Ops:
  6.5 25.6 %copy-start = (f32[16,96]{1,0:T(8,128)S(1)}, f32[16,96]{1,0:T(8,128)}, u32[]{:S(2)}) copy-start(f32[16,96]{1,0:T(8,128)} %param.10) | copy-start | bytes 18436
  6.5 101.3 %all-gather.3.cloned.1.call-start = ((), (), s32[]{:S(2)}) async-start(), calls=%async_computation.3 | async-start | bytes 7299072 | tf_op jit(solution)/shard_map/all_gather | solution.py:166
  9.1 11.4 %collective-permute-start.2 = (bf16[96,384]{1,0:T(8,128)(2,1)S(1)}, bf16[96,384]{1,0:T(8,128)(2,1)S(1)}, u32[]{:S(2)}, u32[]{:S(2)}) collective-permute-start(bf16[96,384]{1,0:T(8,128)(2,1)S(1)} %get-tuple-element.16), channel_id=1, source_target_pairs={{0,4},{4,8},{8,12},{12,0},{1,5},{5,9},{9,13},{13,1},{2,6},{6,10},{... | collective-permute-start | bytes 221192 | tf_op jit(solution)/shard_map/ppermute | solution.py:153
  11.3 9.2 %collective-permute-start.1 = (bf16[96,384]{1,0:T(8,128)(2,1)S(1)}, bf16[96,384]{1,0:T(8,128)(2,1)S(1)}, u32[]{:S(2)}, u32[]{:S(2)}) collective-permute-start(bf16[96,384]{1,0:T(8,128)(2,1)S(1)} %get-tuple-element.16), channel_id=1, source_target_pairs={{0,8},{4,12},{8,0},{12,4},{1,9},{5,13},{9,1},{13,5},{2,10},{6,14},... | collective-permute-start | bytes 221192 | tf_op jit(solution)/shard_map/ppermute | solution.py:153
  13.9 6.6 %collective-permute-start = (bf16[96,384]{1,0:T(8,128)(2,1)S(1)}, bf16[96,384]{1,0:T(8,128)(2,1)S(1)}, u32[]{:S(2)}, u32[]{:S(2)}) collective-permute-start(bf16[96,384]{1,0:T(8,128)(2,1)S(1)} %get-tuple-element.16), channel_id=1, source_target_pairs={{0,12},{4,0},{8,4},{12,8},{1,13},{5,1},{9,5},{13,9},{2,14},{6,2},{... | collective-permute-start | bytes 221192 | tf_op jit(solution)/shard_map/ppermute | solution.py:153
  26.0 12.0 %copy-start.3 = (f32[16,16]{1,0:T(8,128)S(1)}, f32[16,16]{1,0:T(8,128)}, u32[]{:S(2)}) copy-start(f32[16,16]{1,0:T(8,128)} %param.8) | copy-start | bytes 3076
  26.0 12.1 %copy-start.4 = (s32[1,16,16]{2,1,0:T(8,128)S(1)}, s32[1,16,16]{2,1,0:T(8,128)}, u32[]{:S(2)}) copy-start(s32[1,16,16]{2,1,0:T(8,128)} %param.11) | copy-start | bytes 3076
  26.0 26.0 %copy-start.5 = (f32[1,16]{1,0:T(1,128)S(1)}, f32[1,16]{1,0:T(1,128)}, u32[]{:S(2)}) copy-start(f32[1,16]{1,0:T(1,128)} %param.9) | copy-start | bytes 196
  26.0 60.7 %all-to-all-start = ((bf16[8,2,96,1536]{3,2,1,0:T(8,128)(2,1)}), bf16[8,2,96,1536]{3,2,1,0:T(8,128)(2,1)}, u32[]{:S(2)}, u32[]{:S(2)}) async-start(bf16[8,2,96,1536]{3,2,1,0:T(8,128)(2,1)} %combine.3), calls=%async_computation | async-start | bytes 9437184 | tf_op jit(solution)/shard_map/all_to_all | solution.py:186
  32.4 15.3 %collective-permute-start.3 = (bf16[4,96,384]{2,1,0:T(8,128)(2,1)S(1)}, bf16[4,96,384]{2,1,0:T(8,128)(2,1)S(1)}, u32[]{:S(2)}, u32[]{:S(2)}) collective-permute-start(bf16[4,96,384]{2,1,0:T(8,128)(2,1)S(1)} %pad_maximum_fusion.refs_0_), channel_id=1, source_target_pairs={{0,131},{1,0},{2,1},{3,2},{128,3},{129,128},{130,129},{131,130},{4... | collective-permute-start | bytes 884744 | tf_op jit(solution)/shard_map/ppermute | solution.py:157
  38.0 13.2 %collective-permute-start.6 = (bf16[4,96,384]{2,1,0:T(8,128)(2,1)S(1)}, bf16[4,96,384]{2,1,0:T(8,128)(2,1)S(1)}, u32[]{:S(2)}, u32[]{:S(2)}) collective-permute-start(bf16[4,96,384]{2,1,0:T(8,128)(2,1)S(1)} %pad_maximum_fusion.refs_0_), channel_id=1, source_target_pairs={{0,1},{1,2},{2,3},{3,128},{128,129},{129,130},{130,131},{131,0},{4... | collective-permute-start | bytes 884744 | tf_op jit(solution)/shard_map/ppermute | solution.py:157
  47.7 9.7 %collective-permute-start.4 = (bf16[4,96,384]{2,1,0:T(8,128)(2,1)S(1)}, bf16[4,96,384]{2,1,0:T(8,128)(2,1)S(1)}, u32[]{:S(2)}, u32[]{:S(2)}) collective-permute-start(bf16[4,96,384]{2,1,0:T(8,128)(2,1)S(1)} %collective-permute-done.3.refs_1_), channel_id=1, source_target_pairs={{0,131},{1,0},{2,1},{3,2},{128,3},{129,128},{130,129},{131,130},{4... | collective-permute-start | bytes 884744 | tf_op jit(solution)/shard_map/ppermute | solution.py:157
  51.2 9.7 %collective-permute-start.7 = (bf16[4,96,384]{2,1,0:T(8,128)(2,1)S(1)}, bf16[4,96,384]{2,1,0:T(8,128)(2,1)S(1)}, u32[]{:S(2)}, u32[]{:S(2)}) collective-permute-start(bf16[4,96,384]{2,1,0:T(8,128)(2,1)S(1)} %collective-permute-done.6.refs_7_), channel_id=1, source_target_pairs={{0,1},{1,2},{2,3},{3,128},{128,129},{129,130},{130,131},{131,0},{4... | collective-permute-start | bytes 884744 | tf_op jit(solution)/shard_map/ppermute | solution.py:157
  57.5 8.2 %collective-permute-start.5 = (bf16[4,96,384]{2,1,0:T(8,128)(2,1)S(1)}, bf16[4,96,384]{2,1,0:T(8,128)(2,1)S(1)}, u32[]{:S(2)}, u32[]{:S(2)}) collective-permute-start(bf16[4,96,384]{2,1,0:T(8,128)(2,1)S(1)} %collective-permute-done.4.refs_2_), channel_id=1, source_target_pairs={{0,131},{1,0},{2,1},{3,2},{128,3},{129,128},{130,129},{131,130},{4... | collective-permute-start | bytes 884744 | tf_op jit(solution)/shard_map/ppermute | solution.py:157
  60.9 8.5 %collective-permute-start.8 = (bf16[4,96,384]{2,1,0:T(8,128)(2,1)S(1)}, bf16[4,96,384]{2,1,0:T(8,128)(2,1)S(1)}, u32[]{:S(2)}, u32[]{:S(2)}) collective-permute-start(bf16[4,96,384]{2,1,0:T(8,128)(2,1)S(1)} %collective-permute-done.7.refs_6_), channel_id=1, source_target_pairs={{0,1},{1,2},{2,3},{3,128},{128,129},{129,130},{130,131},{131,0},{4... | collective-permute-start | bytes 884744 | tf_op jit(solution)/shard_map/ppermute | solution.py:157
  65.7 9.4 %collective-permute-start.10 = (bf16[2,96,384]{2,1,0:T(8,128)(2,1)S(1)}, bf16[2,96,384]{2,1,0:T(8,128)(2,1)S(1)}, u32[]{:S(2)}, u32[]{:S(2)}) collective-permute-start(bf16[2,96,384]{2,1,0:T(8,128)(2,1)S(1)} %slice.28), channel_id=1, source_target_pairs={{0,131},{1,0},{2,1},{3,2},{128,3},{129,128},{130,129},{131,130},{4... | collective-permute-start | bytes 442376 | tf_op jit(solution)/shard_map/ppermute | solution.py:157
  69.4 9.1 %collective-permute-start.9 = (bf16[2,96,384]{2,1,0:T(8,128)(2,1)S(1)}, bf16[2,96,384]{2,1,0:T(8,128)(2,1)}, u32[]{:S(2)}, u32[]{:S(2)}) collective-permute-start(bf16[2,96,384]{2,1,0:T(8,128)(2,1)S(1)} %slice.27), channel_id=1, source_target_pairs={{0,1},{1,2},{2,3},{3,128},{128,129},{129,130},{130,131},{131,0},{4... | collective-permute-start | bytes 442376 | tf_op jit(solution)/shard_map/ppermute | solution.py:157
  92.5 25.8 %all-to-all-start.2 = ((bf16[8,2,96,384]{3,2,1,0:T(8,128)(2,1)}), bf16[8,2,96,384]{3,2,1,0:T(8,128)(2,1)S(1)}, u32[]{:S(2)}, u32[]{:S(2)}) async-start(bf16[8,2,96,384]{3,2,1,0:T(8,128)(2,1)} %contract_a.1), calls=%async_computation.2 | async-start | bytes 2359296 | tf_op jit(solution)/shard_map/all_to_all | solution.py:200
  118.3 1.0 copy-start.1
  119.3 46.2 %all-to-all-start.1 = ((bf16[8,2,96,1152]{3,2,1,0:T(8,128)(2,1)}), bf16[8,2,96,1152]{3,2,1,0:T(8,128)(2,1)S(1)}, u32[]{:S(2)}, u32[]{:S(2)}) async-start(bf16[8,2,96,1152]{3,2,1,0:T(8,128)(2,1)} %contract_b.1), calls=%async_computation.1 | async-start | bytes 7077888 | tf_op jit(solution)/shard_map/all_to_all | solution.py:200
  123.7 1.3 copy-start.2
Sparse Core Ops, SparseCore 0:
  9.9 97.8 all-gather.2
